TPU v7x, 32 devices: a whole 2x2x4 slice. The times are simulated.
32 devices in a mesh: section: 2 (over x), expert: 4 (over y, core), dp: 4 (over z).
Axes of the slice: x: 2, y: 2, z: 4, core: 2. Of those that a mesh axis runs over, the one named last changes fastest.
Arguments:
- layer_input: bfloat16 [2, 16, 128, 1536], P(None, ('expert', 'dp')), may hold values from -6 to 6
- cotangent: bfloat16 [2, 16, 128, 1536], P(None, ('expert', 'dp')), may hold values from -6 to 6
- segments: int32 [2, 16, 128], P(None, ('expert', 'dp')), may hold values from 0 to 3, never falling along the last dimension, each value on 1 to 64 neighbouring positions
- routes: int32 [2, 2, 16, 128, 4], P('section', None, ('expert', 'dp')), may hold values from 0 to 7, all different within a row; in each aligned block of 128 rows (0 to 127, 128 to 255, ..., all dimensions but the last counted through in order) at most 80 rows name the same one
- attn_gain: bfloat16 [2, 1536], P('section', ('expert', 'dp')), may hold values from 0.25 to 1.75
- w_qkv: bfloat16 [2, 1536, 2048], P('section', ('expert', 'dp')), may hold values from -0.15625 to 0.15625
- w_out: bfloat16 [2, 1536, 1536], P('section', ('expert', 'dp')), may hold values from -0.625 to 0.625
- moe_gain: bfloat16 [2, 1536], P('section', ('expert', 'dp')), may hold values from 0.25 to 1.75
- w_router: bfloat16 [2, 1536, 8], P('section', ('expert', 'dp')), may hold values from -0.078125 to 0.078125
- w_gate: bfloat16 [2, 8, 1536, 768], P('section', 'expert'), may hold values from -0.15625 to 0.15625
- w_up: bfloat16 [2, 8, 1536, 768], P('section', 'expert'), may hold values from -0.15625 to 0.15625
- w_down: bfloat16 [2, 8, 768, 1536], P('section', 'expert'), may hold values from -0.625 to 0.625
Outputs:
- section_out: bfloat16 [2, 2, 16, 128, 1536], P('section', None, ('expert', 'dp'))
- grad_in: bfloat16 [2, 2, 16, 128, 1536], P('section', None, ('expert', 'dp'))
- grad_attn_gain: float32 [2, 1536], P('section', ('expert', 'dp'))
- grad_qkv: float32 [2, 1536, 2048], P('section', ('expert', 'dp'))
- grad_out: float32 [2, 1536, 1536], P('section', ('expert', 'dp'))
- grad_moe_gain: float32 [2, 1536], P('section', ('expert', 'dp'))
- grad_router: float32 [2, 1536, 8], P('section', ('expert', 'dp'))
- grad_gate: float32 [2, 8, 1536, 768], P('section', 'expert', 'dp')
- grad_up: float32 [2, 8, 1536, 768], P('section', 'expert', 'dp')
- grad_down: float32 [2, 8, 768, 1536], P('section', 'expert', 'dp')
Inputs may be any that keep to these rules, and one draw needn't show every extreme that they name: `segments`: within each pack the numbers start at 0, never fall, reach 3, and each is held by at most half of 128 positions. `routes`: A row names 4 different experts. In each aligned block of 128 rows (one pack of one micro-batch of one section) no expert is named more than 80 times, a bound that some block reaches.
All inputs are finite; a program needn't handle non-finite values.
Results may differ from a plain program's by a relative error of at most 0.024.
Values may be sent and summed in bfloat16 or wider, within the bound.
A program may use at most 256 MiB of HBM per device.

v0:
```python
import jax
import jax.numpy as jnp
from jax import lax
from jax.sharding import PartitionSpec as P

D = 1536
QUERY_HEADS = 12
KEY_VALUE_HEADS = 2
HEAD_WIDTH = 128
TOP = 4
PACK_TOKENS = 128


EPS = 1e-06
THETA = 1000000.0
HIGHEST = lax.Precision.HIGHEST
NEGATIVE = -1e30


def shifted(value, axis, by):
    length = lax.axis_size(axis)
    pairs = [(i, i + by) for i in range(length) if 0 <= i + by < length]
    return lax.ppermute(value, axis, pairs)


def rms_scale(hidden, gain):
    return hidden * lax.rsqrt(jnp.mean(hidden * hidden, -1, keepdims=True) + EPS) * gain


def rope_tables():
    places = jnp.arange(PACK_TOKENS, dtype=jnp.float32)
    inverse = THETA ** (-2.0 * jnp.arange(HEAD_WIDTH // 2, dtype=jnp.float32) / HEAD_WIDTH)
    angles = places[:, None] * inverse[None, :]
    return (jnp.cos(angles), jnp.sin(angles))


def apply_rotary(vector, cosine_table, sine_table):
    half_size = vector.shape[-1] // 2
    first_half = vector[..., :half_size]
    second_half = vector[..., half_size:]
    return jnp.concatenate(
        [
            first_half * cosine_table - second_half * sine_table,
            second_half * cosine_table + first_half * sine_table,
        ],
        -1,
    )


def allowed_mask(segs):
    order = jnp.arange(PACK_TOKENS)
    return (segs[:, None] == segs[None, :]) & (order[:, None] >= order[None, :])


def score_block(query_matrix, key_matrix, allowed):
    raw = jnp.einsum(
        "tgih,sgh->gits", query_matrix, key_matrix, preferred_element_type=jnp.float32
    ) * HEAD_WIDTH ** (-0.5)
    return jnp.where(allowed, raw, NEGATIVE)


def activate(gate_proj, up_proj):
    return jax.nn.gelu(gate_proj, approximate=True) * up_proj


def attention_forward(normed_b, wqkv, wout, segs, tables):
    query_width = QUERY_HEADS * HEAD_WIDTH
    key_width = KEY_VALUE_HEADS * HEAD_WIDTH
    query_group = QUERY_HEADS // KEY_VALUE_HEADS
    cosine_table, sine_table = tables
    mixed_heads = jnp.dot(normed_b, wqkv, preferred_element_type=jnp.float32)
    query_matrix = apply_rotary(
        mixed_heads[:, :query_width].reshape(PACK_TOKENS, KEY_VALUE_HEADS, query_group, HEAD_WIDTH),
        cosine_table[:, None, None, :],
        sine_table[:, None, None, :],
    ).astype(jnp.bfloat16)
    key_matrix = apply_rotary(
        mixed_heads[:, query_width : query_width + key_width].reshape(
            PACK_TOKENS, KEY_VALUE_HEADS, HEAD_WIDTH
        ),
        cosine_table[:, None, :],
        sine_table[:, None, :],
    ).astype(jnp.bfloat16)
    value_matrix = (
        mixed_heads[:, query_width + key_width :]
        .reshape(PACK_TOKENS, KEY_VALUE_HEADS, HEAD_WIDTH)
        .astype(jnp.bfloat16)
    )
    scores = score_block(query_matrix, key_matrix, allowed_mask(segs))
    log_total = jax.nn.logsumexp(scores, -1)
    shares = jnp.exp(scores - log_total[..., None]).astype(jnp.bfloat16)
    context = (
        jnp.einsum("gits,sgh->tgih", shares, value_matrix, preferred_element_type=jnp.float32)
        .reshape(PACK_TOKENS, query_width)
        .astype(jnp.bfloat16)
    )
    branch = jnp.dot(context, wout, preferred_element_type=jnp.float32)
    return (branch, (query_matrix, key_matrix, value_matrix, log_total, context))


def attention_backward(grad_branch, normed_b, attn_kept, wqkv, wout, segs, tables):
    query_matrix, key_matrix, value_matrix, log_total, context = attn_kept
    query_width = QUERY_HEADS * HEAD_WIDTH
    key_width = KEY_VALUE_HEADS * HEAD_WIDTH
    query_group = QUERY_HEADS // KEY_VALUE_HEADS
    cosine_table, sine_table = tables
    grad_branch_b = grad_branch.astype(jnp.bfloat16)
    grad_wout = jnp.einsum("te,td->ed", context, grad_branch_b, preferred_element_type=jnp.float32)
    grad_context = (
        jnp.einsum("td,ed->te", grad_branch_b, wout, preferred_element_type=jnp.float32)
        .astype(jnp.bfloat16)
        .reshape(PACK_TOKENS, KEY_VALUE_HEADS, query_group, HEAD_WIDTH)
    )
    scores = score_block(query_matrix, key_matrix, allowed_mask(segs))
    shares = jnp.exp(scores - log_total[..., None])
    grad_shares = jnp.einsum(
        "tgih,sgh->gits", grad_context, value_matrix, preferred_element_type=jnp.float32
    )
    grad_vals = jnp.einsum(
        "gits,tgih->sgh",
        shares.astype(jnp.bfloat16),
        grad_context,
        preferred_element_type=jnp.float32,
    )
    grad_scores = (
        shares * (grad_shares - jnp.sum(shares * grad_shares, -1, keepdims=True))
    ).astype(jnp.bfloat16)
    grad_queries = jnp.einsum(
        "gits,sgh->tgih", grad_scores, key_matrix, preferred_element_type=jnp.float32
    ) * HEAD_WIDTH ** (-0.5)
    grad_keys = jnp.einsum(
        "gits,tgih->sgh", grad_scores, query_matrix, preferred_element_type=jnp.float32
    ) * HEAD_WIDTH ** (-0.5)
    grad_queries = apply_rotary(
        grad_queries, cosine_table[:, None, None, :], -sine_table[:, None, None, :]
    )
    grad_keys = apply_rotary(grad_keys, cosine_table[:, None, :], -sine_table[:, None, :])
    grad_mixed = jnp.concatenate(
        [
            grad_queries.reshape(PACK_TOKENS, query_width),
            grad_keys.reshape(PACK_TOKENS, key_width),
            grad_vals.reshape(PACK_TOKENS, key_width),
        ],
        1,
    ).astype(jnp.bfloat16)
    grad_wqkv = jnp.einsum("td,te->de", normed_b, grad_mixed, preferred_element_type=jnp.float32)
    grad_normed = jnp.einsum("te,de->td", grad_mixed, wqkv, preferred_element_type=jnp.float32)
    return (grad_normed, grad_wqkv, grad_wout)


def per_device(
    layer_input,
    cotangent,
    segments,
    routes,
    attn_gain,
    w_qkv,
    w_out,
    moe_gain,
    w_router,
    w_gate,
    w_up,
    w_down,
):
    gathered = (
        lax.all_gather(w_qkv, ("expert", "dp"), axis=1, tiled=True),
        lax.all_gather(w_out, ("expert", "dp"), axis=1, tiled=True),
        lax.all_gather(w_router, ("expert", "dp"), axis=1, tiled=True),
        lax.all_gather(attn_gain, ("expert", "dp"), axis=1, tiled=True),
        lax.all_gather(moe_gain, ("expert", "dp"), axis=1, tiled=True),
    )
    wqkv = gathered[0][0]
    wout = gathered[1][0]
    router = gathered[2][0]
    gain_attn = gathered[3][0].astype(jnp.float32)
    gain_moe = gathered[4][0].astype(jnp.float32)
    gate_w = w_gate[0]
    up_w = w_up[0]
    down_w = w_down[0]
    per_owner = gate_w.shape[0]
    owners = lax.axis_size("expert")
    total_experts = per_owner * owners
    capacity = 5 * PACK_TOKENS * TOP // (4 * total_experts)
    slot_count = total_experts * capacity
    section_no = lax.axis_index("section")
    is_first = section_no == 0
    tables = rope_tables()
    micro = layer_input.shape[0]
    seg_all = segments[:, 0]
    route_all = routes[0, :, 0]
    incoming = jnp.zeros((PACK_TOKENS, D), jnp.bfloat16)
    saved = []
    produced = []
    for tick_no in range(micro + 1):
        micro_no = jnp.clip(tick_no - section_no, 0, micro - 1)
        hidden_b = jnp.where(is_first, layer_input[min(tick_no, micro - 1), 0], incoming)
        segs = lax.dynamic_index_in_dim(seg_all, micro_no, 0, keepdims=False)
        route = lax.dynamic_index_in_dim(route_all, micro_no, 0, keepdims=False)
        forward_hidden = hidden_b.astype(jnp.float32)
        forward_normed_b = rms_scale(forward_hidden, gain_attn).astype(jnp.bfloat16)
        branch, forward_attn_kept = attention_forward(forward_normed_b, wqkv, wout, segs, tables)
        forward_after_attn = forward_hidden + branch
        forward_moe_in = rms_scale(forward_after_attn, gain_moe).astype(jnp.bfloat16)
        logits = jnp.dot(forward_moe_in, router, preferred_element_type=jnp.float32)
        forward_gates = jax.nn.softmax(jnp.take_along_axis(logits, route, 1), -1)
        flat_route = route.reshape(-1)
        onehot = (flat_route[:, None] == jnp.arange(total_experts)[None, :]).astype(jnp.int32)
        rank = jnp.sum((jnp.cumsum(onehot, 0) - onehot) * onehot, 1)
        forward_slot = flat_route * capacity + rank
        match = forward_slot[:, None] == jnp.arange(slot_count)[None, :]
        forward_filled = jnp.any(match, 0)
        forward_source = jnp.sum(jnp.where(match, jnp.arange(PACK_TOKENS * TOP)[:, None], 0), 0)
        send = jnp.where(
            forward_filled[:, None],
            jnp.take(forward_moe_in, forward_source // TOP, 0),
            jnp.zeros((), jnp.bfloat16),
        )
        expert_received = lax.all_to_all(
            send.reshape(owners, per_owner, capacity, D),
            "expert",
            split_axis=0,
            concat_axis=0,
            tiled=True,
        )
        expert_gate_proj = jnp.einsum(
            "sjcd,jdh->sjch", expert_received, gate_w, preferred_element_type=jnp.float32
        )
        expert_up_proj = jnp.einsum(
            "sjcd,jdh->sjch", expert_received, up_w, preferred_element_type=jnp.float32
        )
        expert_inner = activate(expert_gate_proj, expert_up_proj).astype(jnp.bfloat16)
        result = jnp.einsum(
            "sjch,jhd->sjcd", expert_inner, down_w, preferred_element_type=jnp.float32
        ).astype(jnp.bfloat16)
        returned = lax.all_to_all(result, "expert", split_axis=0, concat_axis=0, tiled=True)
        outputs = (returned, expert_received, expert_gate_proj, expert_up_proj)
        forward_rows = jnp.take(outputs[0].reshape(slot_count, D), forward_slot, 0).reshape(
            PACK_TOKENS, TOP, D
        )
        output = forward_after_attn + jnp.sum(
            forward_gates[:, :, None] * forward_rows.astype(jnp.float32), 1
        )
        forward_kept = (
            forward_hidden,
            forward_after_attn,
            forward_normed_b,
            forward_attn_kept,
            forward_moe_in,
            forward_gates,
            forward_rows,
            forward_slot,
            forward_source,
            forward_filled,
            route,
            segs,
            outputs[1:],
        )
        output, kept = (output, forward_kept)
        output_b = output.astype(jnp.bfloat16)
        saved.append(kept)
        produced.append(output_b)
        if tick_no < micro:
            incoming = shifted(output_b, "section", 1)
    incoming_grad = jnp.zeros((PACK_TOKENS, D), jnp.bfloat16)
    sent = []
    mixer_total = None
    expert_total = None
    for tick_no in range(micro + 1):
        if tick_no < micro:
            top_grad = cotangent[tick_no, 0].astype(jnp.float32)
        else:
            top_grad = jnp.zeros((PACK_TOKENS, D), jnp.float32)
        grad_output = jnp.where(is_first, incoming_grad.astype(jnp.float32), top_grad)
        kept = jax.tree.map(
            lambda early_part, late_part: jnp.where(is_first, early_part, late_part),
            saved[max(tick_no - 1, 0)],
            saved[min(tick_no + 1, micro)],
        )
        (
            hidden,
            after_attn,
            normed_b,
            attn_kept,
            moe_in,
            gates,
            rows,
            slot,
            source,
            filled,
            backward_route,
            backward_segs,
            stored,
        ) = kept
        received = stored[0]
        grad_rows = (
            (gates[:, :, None] * grad_output[:, None, :])
            .astype(jnp.bfloat16)
            .reshape(PACK_TOKENS * TOP, D)
        )
        grad_gates = jnp.sum(grad_output[:, None, :] * rows.astype(jnp.float32), -1)
        grad_chosen = gates * (grad_gates - jnp.sum(gates * grad_gates, 1, keepdims=True))
        picks = (backward_route[:, :, None] == jnp.arange(total_experts)[None, None, :]).astype(
            jnp.float32
        )
        grad_logits = jnp.einsum("tk,tke->te", grad_chosen, picks, precision=HIGHEST)
        grad_send = jnp.where(
            filled[:, None], jnp.take(grad_rows, source, 0), jnp.zeros((), jnp.bfloat16)
        )
        grad_received = lax.all_to_all(
            grad_send.reshape(owners, per_owner, capacity, D),
            "expert",
            split_axis=0,
            concat_axis=0,
            tiled=True,
        )
        gate_proj = stored[1]
        up_proj = stored[2]
        inner, pull_act = jax.vjp(activate, gate_proj, up_proj)
        grad_inner = jnp.einsum(
            "sjcd,jhd->sjch", grad_received, down_w, preferred_element_type=jnp.float32
        )
        grad_gate_proj, grad_up_proj = pull_act(grad_inner)
        grad_gate_b = grad_gate_proj.astype(jnp.bfloat16)
        grad_up_b = grad_up_proj.astype(jnp.bfloat16)
        grad_down_w = jnp.einsum(
            "sjch,sjcd->jhd",
            inner.astype(jnp.bfloat16),
            grad_received,
            preferred_element_type=jnp.float32,
        )
        grad_gate_w = jnp.einsum(
            "sjcd,sjch->jdh", received, grad_gate_b, preferred_element_type=jnp.float32
        )
        grad_up_w = jnp.einsum(
            "sjcd,sjch->jdh", received, grad_up_b, preferred_element_type=jnp.float32
        )
        expert_part = (grad_gate_w, grad_up_w, grad_down_w)
        grad_input = jnp.einsum(
            "sjch,jdh->sjcd", grad_gate_b, gate_w, preferred_element_type=jnp.float32
        )
        grad_input = (
            grad_input
            + jnp.einsum("sjch,jdh->sjcd", grad_up_b, up_w, preferred_element_type=jnp.float32)
        ).astype(jnp.bfloat16)
        grad_slots = lax.all_to_all(
            grad_input, "expert", split_axis=0, concat_axis=0, tiled=True
        ).reshape(slot_count, D)
        grad_moe_in = jnp.sum(
            jnp.take(grad_slots, slot, 0).reshape(PACK_TOKENS, TOP, D).astype(jnp.float32), 1
        )
        grad_moe_in = grad_moe_in + jnp.dot(
            grad_logits, router.astype(jnp.float32).T, precision=HIGHEST
        )
        grad_router = jnp.dot(moe_in.astype(jnp.float32).T, grad_logits, precision=HIGHEST)
        unused_moe, pull_moe = jax.vjp(rms_scale, after_attn, gain_moe)
        grad_after, grad_gain_moe = pull_moe(grad_moe_in)
        grad_after = grad_after + grad_output
        grad_normed, grad_wqkv, grad_wout = attention_backward(
            grad_after, normed_b, attn_kept, wqkv, wout, backward_segs, tables
        )
        unused_attn, pull_attn = jax.vjp(rms_scale, hidden, gain_attn)
        grad_hidden, grad_gain_attn = pull_attn(grad_normed)
        grad_hidden, mixer_part, expert_part = (
            grad_hidden + grad_after,
            (grad_wqkv, grad_wout, grad_router, grad_gain_attn, grad_gain_moe),
            expert_part,
        )
        grad_hidden_b = grad_hidden.astype(jnp.bfloat16)
        sent.append(grad_hidden_b)
        if tick_no < micro:
            incoming_grad = shifted(grad_hidden_b, "section", -1)
        mixer_total = (
            mixer_part if mixer_total is None else jax.tree.map(jnp.add, mixer_total, mixer_part)
        )
        expert_total = (
            expert_part
            if expert_total is None
            else jax.tree.map(jnp.add, expert_total, expert_part)
        )
    mixer_total = (
        lax.psum_scatter(mixer_total[0], ("expert", "dp"), scatter_dimension=0, tiled=True),
        lax.psum_scatter(mixer_total[1], ("expert", "dp"), scatter_dimension=0, tiled=True),
        lax.psum_scatter(mixer_total[2], ("expert", "dp"), scatter_dimension=0, tiled=True),
        lax.psum_scatter(mixer_total[3], ("expert", "dp"), scatter_dimension=0, tiled=True),
        lax.psum_scatter(mixer_total[4], ("expert", "dp"), scatter_dimension=0, tiled=True),
    )
    expert_total = (
        lax.psum_scatter(
            expert_total[0].astype(jnp.bfloat16), "dp", scatter_dimension=1, tiled=True
        ).astype(jnp.float32),
        lax.psum_scatter(
            expert_total[1].astype(jnp.bfloat16), "dp", scatter_dimension=1, tiled=True
        ).astype(jnp.float32),
        lax.psum_scatter(
            expert_total[2].astype(jnp.bfloat16), "dp", scatter_dimension=1, tiled=True
        ).astype(jnp.float32),
    )
    section_out = jnp.stack(
        [
            jnp.where(is_first, produced[micro_idx], produced[micro_idx + 1])
            for micro_idx in range(micro)
        ]
    ).reshape(1, micro, 1, PACK_TOKENS, D)
    grad_in = jnp.stack(
        [jnp.where(is_first, sent[micro_idx + 1], sent[micro_idx]) for micro_idx in range(micro)]
    ).reshape(1, micro, 1, PACK_TOKENS, D)
    return (
        section_out,
        grad_in,
        mixer_total[3][None],
        mixer_total[0][None],
        mixer_total[1][None],
        mixer_total[4][None],
        mixer_total[2][None],
        expert_total[0][None],
        expert_total[1][None],
        expert_total[2][None],
    )


def solution(mesh):
    return jax.shard_map(
        per_device,
        mesh=mesh,
        in_specs=(
            P(None, ("expert", "dp"), None, None),
            P(None, ("expert", "dp"), None, None),
            P(None, ("expert", "dp"), None),
            P("section", None, ("expert", "dp"), None, None),
            P("section", ("expert", "dp")),
            P("section", ("expert", "dp"), None),
            P("section", ("expert", "dp"), None),
            P("section", ("expert", "dp")),
            P("section", ("expert", "dp"), None),
            P("section", "expert", None, None),
            P("section", "expert", None, None),
            P("section", "expert", None, None),
        ),
        out_specs=(
            P("section", None, ("expert", "dp"), None, None),
            P("section", None, ("expert", "dp"), None, None),
            P("section", ("expert", "dp")),
            P("section", ("expert", "dp"), None),
            P("section", ("expert", "dp"), None),
            P("section", ("expert", "dp")),
            P("section", ("expert", "dp"), None),
            P("section", "expert", "dp", None),
            P("section", "expert", "dp", None),
            P("section", "expert", "dp", None),
        ),
        check_vma=False,
    )
```

profile of v0, /device:TPU:0, one launch (start us, length us, event | category | flops | bytes accessed | tf_op | source)
XLA Modules:
  0.0 1312.5 jit_solution(17821819590812520252)
XLA Ops:
  16.0 37.7 %all-reduce.5 = (bf16[1536]{0:T(1024)(128)(2,1)S(1)}, bf16[1536]{0:T(1024)(128)(2,1)S(1)}) all-reduce(bf16[1536]{0:T(1024)(128)(2,1)S(1)} %dynamic-update-slice, bf16[1536]{0:T(1024)(128)(2,1)S(1)} %dynamic-update-slice.1), channel_id=1, replica_groups=mesh['section'=2,'expert'=4,'dp'=4] {'expert','dp'}, use_global_device_ids=true, to_apply=%add | all-reduce | flops 3072 | bytes 12288
  65.7 10.4 all-gather.3.cloned.1.call-done
  85.6 44.9 %all-gather.5.cloned.1.call-done = bf16[1,1536,1536]{2,1,0:T(8,128)(2,1)} async-done(((bf16[1,96,1536]{2,1,0:T(8,128)(2,1)}), bf16[1,1536,1536]{2,1,0:T(8,128)(2,1)}) %all-gather.5.cloned.1.call-update) | async-done | bytes 4718608 | tf_op jit(solution)/shard_map/all_gather | solution.py:167
  138.3 27.2 %all_to_all.60 = bf16[4,2,80,1536]{3,2,1,0:T(8,128)(2,1)S(1)} all-to-all(bf16[4,2,80,1536]{3,2,1,0:T(8,128)(2,1)S(1)} %bitcast.770), channel_id=1, replica_groups=mesh['section'=2,'expert'=4,'dp'=4] {'expert'}, dimensions={0} | all-to-all | bytes 3932160 | tf_op jit(solution)/shard_map/all_to_all | solution.py:218
  179.5 39.9 %all_gather.19 = bf16[1,1536,8]{2,0,1:T(2,128)(2,1)S(1)} all-gather(bf16[1,96,8]{2,0,1:T(2,128)(2,1)S(1)} %copy.431), channel_id=1, replica_groups=mesh['section'=2,'expert'=4,'dp'=4] {'expert','dp'}, dimensions={1}, use_global_device_ids=true | all-gather | bytes 26112 | tf_op jit(solution)/shard_map/all_gather | solution.py:168
  271.5 23.2 %all-to-all-done.2 = bf16[4,2,80,1536]{3,2,1,0:T(8,128)(2,1)S(1)} async-done(((bf16[4,2,80,1536]{3,2,1,0:T(8,128)(2,1)}), bf16[4,2,80,1536]{3,2,1,0:T(8,128)(2,1)S(1)}, u32[]{:S(2)}, u32[]{:S(2)}) %all-to-all-start.2) | async-done | bytes 1966112 | tf_op jit(solution)/shard_map/all_to_all | solution.py:218
  324.4 11.4 all-to-all-done.3
  363.6 17.7 %all-to-all-done.6 = bf16[4,2,80,1536]{3,2,1,0:T(8,128)(2,1)} async-done(((bf16[4,2,80,1536]{3,2,1,0:T(8,128)(2,1)}), bf16[4,2,80,1536]{3,2,1,0:T(8,128)(2,1)}, u32[]{:S(2)}, u32[]{:S(2)}) %all-to-all-start.6) | async-done | bytes 1966112 | tf_op jit(solution)/shard_map/all_to_all | solution.py:309
  381.3 7.4 fusion.120
  454.7 6.9 multiply_reduce_fusion.11
  488.6 19.5 %all-to-all-done.4 = bf16[4,2,80,1536]{3,2,1,0:T(8,128)(2,1)S(1)} async-done(((bf16[4,2,80,1536]{3,2,1,0:T(8,128)(2,1)}), bf16[4,2,80,1536]{3,2,1,0:T(8,128)(2,1)S(1)}, u32[]{:S(2)}, u32[]{:S(2)}) %all-to-all-start.4) | async-done | bytes 1966112 | tf_op jit(solution)/shard_map/all_to_all | solution.py:218
  531.5 9.5 collective-permute-done.2
  572.7 23.5 %all-to-all-done.8 = bf16[4,2,80,1536]{3,2,1,0:T(8,128)(2,1)} async-done(((bf16[4,2,80,1536]{3,2,1,0:T(8,128)(2,1)}), bf16[4,2,80,1536]{3,2,1,0:T(8,128)(2,1)}, u32[]{:S(2)}, u32[]{:S(2)}) %all-to-all-start.8) | async-done | bytes 1966112 | tf_op jit(solution)/shard_map/all_to_all | solution.py:309
  596.2 7.4 fusion.127
  620.4 21.2 %all-to-all-done.9 = bf16[4,2,80,1536]{3,2,1,0:T(8,128)(2,1)S(1)} async-done(((bf16[4,2,80,1536]{3,2,1,0:T(8,128)(2,1)}), bf16[4,2,80,1536]{3,2,1,0:T(8,128)(2,1)S(1)}, u32[]{:S(2)}, u32[]{:S(2)}) %all-to-all-start.9) | async-done | bytes 1966112 | tf_op jit(solution)/shard_map/all_to_all | solution.py:345
  720.4 7.5 fusion.221
  730.3 12.6 all-to-all-done.10
  742.9 10.0 fusion.134
  754.0 10.2 fusion.2
  778.3 9.9 fusion.1
  789.8 10.1 fusion.170
  799.9 7.4 fusion.167
  807.3 13.7 %fusion = bf16[2,768,1536]{2,1,0:T(8,128)(2,1)} fusion(f32[2,768,1536,1]{2,1,3,0:T(8,128)} %fusion.167, f32[2,768,1536,1]{2,1,3,0:T(8,128)} %fusion.170, bf16[4,2,80,1536]{3,2,1,0:T(8,128)(2,1)} %all-to-all-done.10, f32[4,2,80,768]{3,2,0,1:T(8,128)} %get-tuple-element.104, f32[2,4,80,768]{3,2,1,0:T(8,128)} %copy-done.65, ...), kind=kOutput, calls=%fused_computation.19 | convolution fusion | flops 1522434048 | bytes 31457280 | tf_op jit(solution)/shard_map/sjch,sjcd->jhd/dot_general | solution.py:325
  843.3 15.4 %all-to-all-done.11 = bf16[4,2,80,1536]{3,2,1,0:T(8,128)(2,1)S(1)} async-done(((bf16[4,2,80,1536]{3,2,1,0:T(8,128)(2,1)}), bf16[4,2,80,1536]{3,2,1,0:T(8,128)(2,1)S(1)}, u32[]{:S(2)}, u32[]{:S(2)}) %all-to-all-start.11) | async-done | bytes 1966112 | tf_op jit(solution)/shard_map/all_to_all | solution.py:345
  871.8 9.0 convolution_add_fusion
  882.2 6.4 fusion.273
  888.7 6.5 fusion.271
  903.7 14.9 %add_add_fusion = f32[1536,2048]{1,0:T(8,128)} fusion(f32[1536,2048]{1,0:T(8,128)} %fusion.273, f32[1536,2048]{1,0:T(8,128)} %fusion.271, pred[]{:T(512)S(6)} %eq.234, bf16[128,256]{0,1:T(8,128)(2,1)S(1)} %bitcast.802, bf16[128,256]{0,1:T(8,128)(2,1)S(1)} %bitcast.808, bf16[128,1536]{0,1:T(8,128)(2,1)S(1)} %bitcast.783, ...), kind=kOutput, calls=%fused_computation.15 | convolution fusion | flops 814940160 | bytes 39066624 | tf_op jit(solution)/shard_map/td,te->de/dot_general | solution.py:146
  941.0 62.2 %all-reduce.4 = (f32[1536]{0:T(1024)S(1)}, f32[1536]{0:T(1024)S(1)}) all-reduce(f32[1536]{0:T(1024)S(1)} %add_add_fusion.8, f32[1536]{0:T(1024)S(1)} %add_add_fusion.7), channel_id=2, replica_groups=mesh['section'=2,'expert'=4,'dp'=4] {'expert','dp'}, use_global_device_ids=true, to_apply=%region_63.68.clone | all-reduce | flops 3072 | bytes 24576
  1012.0 37.4 %reduce-scatter.17.cloned.1.call-done = bf16[2,192,1536]{2,1,0:T(8,128)(2,1)} async-done(((bf16[2,768,1536]{2,1,0:T(8,128)(2,1)}), bf16[2,192,1536]{2,1,0:T(8,128)(2,1)}) %reduce-scatter.17.cloned.1.call-update) | async-done | bytes 1179664 | tf_op jit(solution)/shard_map/reduce_scatter | solution.py:394
  1052.4 113.9 %reduce-scatter.11.cloned.1.call-done = f32[96,1536]{1,0:T(8,128)} async-done(((f32[1536,1536]{1,0:T(8,128)}), f32[96,1536]{1,0:T(8,128)}) %reduce-scatter.11.cloned.1.call-update) | async-done | bytes 589840 | tf_op jit(solution)/shard_map/reduce_scatter | solution.py:382
  1166.3 139.1 %reduce-scatter.9.cloned.1.call-done = f32[96,2048]{1,0:T(8,128)} async-done(((f32[1536,2048]{1,0:T(8,128)}), f32[96,2048]{1,0:T(8,128)}) %reduce-scatter.9.cloned.1.call-update) | async-done | bytes 786448 | tf_op jit(solution)/shard_map/reduce_scatter | solution.py:381
  (1056 shorter events, 498.1 us)
Async XLA Ops:
  7.2 56.4 %copy-start.271 = (s32[2,1,128]{2,1,0:T(1,128)S(1)}, s32[2,1,128]{2,1,0:T(1,128)}, u32[]{:S(2)}) copy-start(s32[2,1,128]{2,1,0:T(1,128)} %param.22) | copy-start | bytes 3076
  7.2 56.2 %copy-start.24 = (bf16[2,1,128,1536]{3,2,1,0:T(8,128)(2,1)S(1)}, bf16[2,1,128,1536]{3,2,1,0:T(8,128)(2,1)}, u32[]{:S(2)}) copy-start(bf16[2,1,128,1536]{3,2,1,0:T(8,128)(2,1)} %param.20) | copy-start | bytes 2359300
  7.2 68.9 %all-gather.3.cloned.1.call-start = ((), (), s32[]{:S(2)}) async-start(), calls=%async_computation.18 | async-start | bytes 6684672 | tf_op jit(solution)/shard_map/all_gather | solution.py:166
  7.9 122.6 %all-gather.5.cloned.1.call-start = ((), (), s32[]{:S(2)}) async-start(), calls=%async_computation.19 | async-start | bytes 5013504 | tf_op jit(solution)/shard_map/all_gather | solution.py:167
  53.7 385.4 %copy-start.129 = (f32[1536]{0:T(1024)}, f32[1536]{0:T(1024)S(1)}, u32[]{:S(2)}) copy-start(f32[1536]{0:T(1024)S(1)} %mul.1809) | copy-start | bytes 18436
  134.8 86.2 %copy-start = (bf16[128,1536]{1,0:T(8,128)(2,1)}, bf16[128,1536]{1,0:T(8,128)(2,1)S(1)}, u32[]{:S(2)}) copy-start(bf16[128,1536]{1,0:T(8,128)(2,1)S(1)} %multiply_convert_fusion.14) | copy-start | bytes 1179652
  175.4 49.4 %all-to-all-start.1 = ((bf16[4,2,80,1536]{3,2,1,0:T(8,128)(2,1)}), bf16[4,2,80,1536]{3,2,1,0:T(8,128)(2,1)S(1)}, u32[]{:S(2)}, u32[]{:S(2)}) async-start(bf16[4,2,80,1536]{3,2,1,0:T(8,128)(2,1)} %copy.440), calls=%async_computation.1 | async-start | bytes 3932160 | tf_op jit(solution)/shard_map/all_to_all | solution.py:235
  240.4 8.8 collective-permute-start
  262.1 59.3 %copy-start.2 = (bf16[128,1536]{1,0:T(8,128)(2,1)}, bf16[128,1536]{1,0:T(8,128)(2,1)S(1)}, u32[]{:S(2)}) copy-start(bf16[128,1536]{1,0:T(8,128)(2,1)S(1)} %get-tuple-element.169) | copy-start | bytes 1179652
  266.9 27.9 %all-to-all-start.2 = ((bf16[4,2,80,1536]{3,2,1,0:T(8,128)(2,1)}), bf16[4,2,80,1536]{3,2,1,0:T(8,128)(2,1)S(1)}, u32[]{:S(2)}, u32[]{:S(2)}) async-start(bf16[4,2,80,1536]{3,2,1,0:T(8,128)(2,1)} %bitcast.769), calls=%async_computation.2 | async-start | bytes 3932160 | tf_op jit(solution)/shard_map/all_to_all | solution.py:218
  307.7 28.2 %all-to-all-start.3 = ((bf16[4,2,80,1536]{3,2,1,0:T(8,128)(2,1)}), bf16[4,2,80,1536]{3,2,1,0:T(8,128)(2,1)S(1)}, u32[]{:S(2)}, u32[]{:S(2)}) async-start(bf16[4,2,80,1536]{3,2,1,0:T(8,128)(2,1)} %copy.456), calls=%async_computation.3 | async-start | bytes 3932160 | tf_op jit(solution)/shard_map/all_to_all | solution.py:235
  352.3 28.9 %all-to-all-start.6 = ((bf16[4,2,80,1536]{3,2,1,0:T(8,128)(2,1)}), bf16[4,2,80,1536]{3,2,1,0:T(8,128)(2,1)}, u32[]{:S(2)}, u32[]{:S(2)}) async-start(bf16[4,2,80,1536]{3,2,1,0:T(8,128)(2,1)} %bitcast.95), calls=%async_computation.6 | async-start | bytes 3932160 | tf_op jit(solution)/shard_map/all_to_all | solution.py:309
  398.8 28.0 %all-to-all-start.7 = ((bf16[4,2,80,1536]{3,2,1,0:T(8,128)(2,1)}), bf16[4,2,80,1536]{3,2,1,0:T(8,128)(2,1)S(1)}, u32[]{:S(2)}, u32[]{:S(2)}) async-start(bf16[4,2,80,1536]{3,2,1,0:T(8,128)(2,1)} %copy.480), calls=%async_computation.7 | async-start | bytes 3932160 | tf_op jit(solution)/shard_map/all_to_all | solution.py:345
  415.4 39.3 %collective-permute-start.1 = (bf16[128,1536]{1,0:T(8,128)(2,1)}, bf16[128,1536]{1,0:T(8,128)(2,1)}, u32[]{:S(2)}, u32[]{:S(2)}) collective-permute-start(bf16[128,1536]{1,0:T(8,128)(2,1)} %get-tuple-element.124), channel_id=1, source_target_pairs={{0,16},{1,17},{2,18},{3,19},{4,20},{5,21},{6,22},{7,23},{8,24},{9,... | collective-permute-start | bytes 1179656 | tf_op jit(solution)/shard_map/ppermute | solution.py:23
  480.1 28.0 %all-to-all-start.4 = ((bf16[4,2,80,1536]{3,2,1,0:T(8,128)(2,1)}), bf16[4,2,80,1536]{3,2,1,0:T(8,128)(2,1)S(1)}, u32[]{:S(2)}, u32[]{:S(2)}) async-start(bf16[4,2,80,1536]{3,2,1,0:T(8,128)(2,1)} %bitcast.768), calls=%async_computation.4 | async-start | bytes 3932160 | tf_op jit(solution)/shard_map/all_to_all | solution.py:218
  521.0 29.1 %all-to-all-start.5 = ((bf16[4,2,80,1536]{3,2,1,0:T(8,128)(2,1)}), bf16[4,2,80,1536]{3,2,1,0:T(8,128)(2,1)S(1)}, u32[]{:S(2)}, u32[]{:S(2)}) async-start(bf16[4,2,80,1536]{3,2,1,0:T(8,128)(2,1)} %copy.472), calls=%async_computation.5 | async-start | bytes 3932160 | tf_op jit(solution)/shard_map/all_to_all | solution.py:235
  527.2 13.8 %collective-permute-start.2 = (bf16[128,1536]{1,0:T(8,128)(2,1)}, bf16[128,1536]{1,0:T(8,128)(2,1)}, u32[]{:S(2)}, u32[]{:S(2)}) collective-permute-start(bf16[128,1536]{1,0:T(8,128)(2,1)} %fusion.246), channel_id=1, source_target_pairs={{16,0},{17,1},{18,2},{19,3},{20,4},{21,5},{22,6},{23,7},{24,8},{25... | collective-permute-start | bytes 1179656 | tf_op jit(solution)/shard_map/ppermute | solution.py:23
  566.9 29.3 %all-to-all-start.8 = ((bf16[4,2,80,1536]{3,2,1,0:T(8,128)(2,1)}), bf16[4,2,80,1536]{3,2,1,0:T(8,128)(2,1)}, u32[]{:S(2)}, u32[]{:S(2)}) async-start(bf16[4,2,80,1536]{3,2,1,0:T(8,128)(2,1)} %bitcast.114), calls=%async_computation.8 | async-start | bytes 3932160 | tf_op jit(solution)/shard_map/all_to_all | solution.py:309
  613.6 28.0 %all-to-all-start.9 = ((bf16[4,2,80,1536]{3,2,1,0:T(8,128)(2,1)}), bf16[4,2,80,1536]{3,2,1,0:T(8,128)(2,1)S(1)}, u32[]{:S(2)}, u32[]{:S(2)}) async-start(bf16[4,2,80,1536]{3,2,1,0:T(8,128)(2,1)} %copy.496), calls=%async_computation.9 | async-start | bytes 3932160 | tf_op jit(solution)/shard_map/all_to_all | solution.py:345
  679.7 12.7 collective-permute-start.3
  714.0 28.9 %all-to-all-start.10 = ((bf16[4,2,80,1536]{3,2,1,0:T(8,128)(2,1)}), bf16[4,2,80,1536]{3,2,1,0:T(8,128)(2,1)}, u32[]{:S(2)}, u32[]{:S(2)}) async-start(bf16[4,2,80,1536]{3,2,1,0:T(8,128)(2,1)} %bitcast.767), calls=%async_computation.10 | async-start | bytes 3932160 | tf_op jit(solution)/shard_map/all_to_all | solution.py:309
  718.6 215.7 %reduce-scatter.19.cloned.1.call-start = ((), (), s32[]{:S(2)}) async-start(), calls=%async_computation.25 | async-start | bytes 835584
  730.2 276.1 %reduce-scatter.13.cloned.1.call-start = ((), (), s32[]{:S(2)}) async-start(), calls=%async_computation.22 | async-start | bytes 5898240 | tf_op jit(solution)/shard_map/reduce_scatter | solution.py:388
  764.2 244.9 %reduce-scatter.15.cloned.1.call-start = ((), (), s32[]{:S(2)}) async-start(), calls=%async_computation.23 | async-start | bytes 5898240 | tf_op jit(solution)/shard_map/reduce_scatter | solution.py:391
  788.2 261.1 %reduce-scatter.17.cloned.1.call-start = ((), (), s32[]{:S(2)}) async-start(), calls=%async_computation.24 | async-start | bytes 5898240 | tf_op jit(solution)/shard_map/reduce_scatter | solution.py:394
  830.7 28.0 %all-to-all-start.11 = ((bf16[4,2,80,1536]{3,2,1,0:T(8,128)(2,1)}), bf16[4,2,80,1536]{3,2,1,0:T(8,128)(2,1)S(1)}, u32[]{:S(2)}, u32[]{:S(2)}) async-start(bf16[4,2,80,1536]{3,2,1,0:T(8,128)(2,1)} %copy.515), calls=%async_computation.11 | async-start | bytes 3932160 | tf_op jit(solution)/shard_map/all_to_all | solution.py:345
  834.4 331.8 %reduce-scatter.11.cloned.1.call-start = ((), (), s32[]{:S(2)}) async-start(), calls=%async_computation.21 | async-start | bytes 10027008 | tf_op jit(solution)/shard_map/reduce_scatter | solution.py:382
  880.9 424.5 %reduce-scatter.9.cloned.1.call-start = ((), (), s32[]{:S(2)}) async-start(), calls=%async_computation.20 | async-start | bytes 13369344 | tf_op jit(solution)/shard_map/reduce_scatter | solution.py:381
  935.7 68.6 %copy-start.291 = (f32[128]{0:T(128)S(1)}, f32[128]{0:T(128)}, u32[]{:S(2)}) copy-start(f32[128]{0:T(128)} %get-tuple-element.77) | copy-start | bytes 1540
  935.8 68.6 %copy-start.44 = (f32[128,1536]{1,0:T(8,128)S(1)}, f32[128,1536]{1,0:T(8,128)}, u32[]{:S(2)}) copy-start(f32[128,1536]{1,0:T(8,128)} %copy-done.43) | copy-start | bytes 2359300
  935.8 68.6 %copy-start.112 = (bf16[128,1536]{1,0:T(8,128)(2,1)S(1)}, bf16[128,1536]{1,0:T(8,128)(2,1)}, u32[]{:S(2)}) copy-start(bf16[128,1536]{1,0:T(8,128)(2,1)} %copy-done.111) | copy-start | bytes 1179652
  941.0 64.4 %copy-start.113 = (bf16[1,128,1536]{2,1,0:T(8,128)(2,1)S(1)}, bf16[1,128,1536]{2,1,0:T(8,128)(2,1)}, u32[]{:S(2)}) copy-start(bf16[1,128,1536]{2,1,0:T(8,128)(2,1)} %get-tuple-element.85) | copy-start | bytes 1179652
  (308 other events, 1811.4 us)
Sparse Core Ops, SparseCore 0:
  10.3 65.7 all-gather.2
  78.4 52.0 all-gather.4
  730.3 54.1 reduce-scatter.18
  786.8 84.3 reduce-scatter.12
  873.4 86.4 reduce-scatter.14
  962.2 87.1 reduce-scatter.16
  1054.6 111.5 reduce-scatter.10
  1170.9 134.4 reduce-scatter.8
where the time goes:
time: 1320 us; the launch traced here: 1310 us
  waiting for transfers between devices  515 us (39%)
  matrix products  262 us (20%)
  blocking collectives  167 us (13%)
  local copies, waits for them, and re-layouts  153 us (12%)
  other arithmetic  139 us (11%)
  starting transfers between devices  56.2 us (4%)
  between operations  20.2 us (2%)
    reduce_scatter x1, waiting for transfers between devices, per_device(): lax.psum_scatter(mixer_total[0], ('expert', 'dp'), scatter_dimension=0, t...  139 us
    reduce_scatter x1, waiting for transfers between devices, per_device(): lax.psum_scatter(mixer_total[1], ('expert', 'dp'), scatter_dimension=0, t...  114 us
    unnamed x2, blocking collectives  99.9 us
    all_to_all x3, waiting for transfers between devices, per_device(): lax.all_to_all(grad_send.reshape(owners, per_owner, capacity, D), 'expert...  53.8 us
    all_gather x1, waiting for transfers between devices, per_device(): lax.all_gather(w_out, ('expert', 'dp'), axis=1, tiled=True)  44.9 us
    all_to_all x2, waiting for transfers between devices, per_device(): lax.all_to_all(send.reshape(owners, per_owner, capacity, D), 'expert', sp...  42.6 us
    all_to_all x3, waiting for transfers between devices, per_device(): lax.all_to_all(grad_input, 'expert', split_axis=0, concat_axis=0, tiled=T...  42.2 us
    all_gather x1, blocking collectives, per_device(): lax.all_gather(w_router, ('expert', 'dp'), axis=1, tiled=True)  39.9 us
  transfers between devices with their start and end apart: 23, of which 17 were waited for; matrix products, arithmetic and copies ran while one was open for 24% of the time, Pallas kernels for 0%

commit v1 on v0

v1 whole, which is shorter than its diff:
```python
import functools

import jax
import jax.numpy as jnp
import numpy as np
from jax import lax
from jax.experimental import pallas as pl
from jax.experimental.pallas import tpu as pltpu
from jax.sharding import PartitionSpec as P

HEAD = 128
QUERY_HEADS = 12
KEY_VALUE_HEADS = 2
GROUP = QUERY_HEADS // KEY_VALUE_HEADS
EPS = 1e-06
THETA = 1000000.0
NEGATIVE = -1e30
SCALE = HEAD ** (-0.5)
ROUTER_ROWS = 16
SMALL_ROWS = 32
CHUNKS = 2
MESH = pl.DeviceIdType.MESH
F32 = jnp.float32
BF16 = jnp.bfloat16
GELU_C = float(np.sqrt(2.0 / np.pi))
GELU_A = 0.044715


def dot(a, b):
    return jnp.dot(a, b, preferred_element_type=F32)


def dot_nt(a, b):
    return lax.dot_general(a, b, (((1,), (1,)), ((), ())), preferred_element_type=F32)


def dot_tn(a, b):
    return lax.dot_general(a, b, (((0,), (0,)), ((), ())), preferred_element_type=F32)


def rotary_tables(tokens):
    places = np.arange(tokens, dtype=np.float64)
    inverse = THETA ** (-2.0 * np.arange(HEAD // 2, dtype=np.float64) / HEAD)
    angles = places[:, None] * inverse[None, :]
    cosine, sine = np.cos(angles), np.sin(angles)
    return (
        jnp.asarray(np.concatenate([cosine, cosine], 1), F32),
        jnp.asarray(np.concatenate([-sine, sine], 1), F32),
    )


def mask_bias(col, row):
    tokens = row.shape[1]
    ti = lax.broadcasted_iota(jnp.int32, (tokens, tokens), 0)
    ui = lax.broadcasted_iota(jnp.int32, (tokens, tokens), 1)
    return jnp.where((col == row) & (ui <= ti), 0.0, NEGATIVE).astype(F32)


def heads_of(value, first, count):
    return jnp.concatenate(
        [value[:, (first + i) * HEAD : (first + i + 1) * HEAD] for i in range(count)], 0
    )


def attention_shares(q6, k, bias6):
    scores = dot_nt(q6, k) * SCALE + bias6
    top = jnp.max(scores, -1, keepdims=True)
    raised = jnp.exp(scores - top)
    return raised / jnp.sum(raised, -1, keepdims=True)


class Place:
    def __init__(self, ny):
        self.ny = ny
        self.s = lax.axis_index("section")
        self.e = lax.axis_index("expert")
        self.d = lax.axis_index("dp")
        self.y = lax.div(self.e, 2)
        self.c = lax.rem(self.e, 2)
        self.core = (self.s, self.y * 2 + 1 - self.c, self.d)
        self.x = (1 - self.s, self.e, self.d)

    def ahead(self, r):
        return (self.s, lax.rem(self.y + r, self.ny) * 2 + self.c, self.d)

    def behind(self, r):
        return (self.s, lax.rem(self.y + self.ny - r, self.ny) * 2 + self.c, self.d)

    def pack(self, r, other):
        core = 1 - self.c if other else self.c
        return lax.rem(self.y + r, self.ny) * 2 + core

    def greet(self):
        barrier = pltpu.get_barrier_semaphore()
        partners = [self.core, self.x] + [self.ahead(r) for r in range(1, self.ny)]
        for partner in partners:
            pl.semaphore_signal(barrier, inc=1, device_id=partner, device_id_type=MESH)
        pl.semaphore_wait(barrier, len(partners))


def remote(src, dst, send, recv, device):
    return pltpu.make_async_remote_copy(
        src_ref=src, dst_ref=dst, send_sem=send, recv_sem=recv, device_id=device, device_id_type=MESH
    )


class Exchange:
    def __init__(self, place, rows_ref, retl, retc, rety, sendl, sendc, sendy, sems):
        self.place = place
        self.rows_ref = rows_ref
        self.retl, self.retc, self.rety = retl, retc, rety
        self.sendl, self.sendc, self.sendy = sendl, sendc, sendy
        self.sems = sems
        self.tokens = rows_ref.shape[2]
        self.span = self.tokens // CHUNKS

    def rows(self, q):
        return pl.ds(q * self.span, self.span)

    def core_own(self):
        g = self.place
        return remote(
            self.rows_ref.at[0, 0], self.rows_ref.at[0, 1], self.sems.cs.at[0, 0], self.sems.cr.at[0, 0], g.core
        )

    def y_own(self, r, q):
        g = self.place
        return remote(
            self.rows_ref.at[0, 0, self.rows(q)],
            self.rows_ref.at[r, 0, self.rows(q)],
            self.sems.ys.at[r, q],
            self.sems.yr.at[r, q],
            g.behind(r),
        )

    def forward(self, r, q):
        g = self.place
        return remote(
            self.rows_ref.at[r, 0, self.rows(q)],
            self.rows_ref.at[r, 1, self.rows(q)],
            self.sems.cs.at[r, q],
            self.sems.cr.at[r, q],
            g.core,
        )

    def back_local(self):
        return remote(self.sendl, self.retl, self.sems.bs.at[0, 0], self.sems.br.at[0, 0], self.place.core)

    def back_core(self, r, q):
        return remote(
            self.sendc.at[r, self.rows(q)],
            self.retc.at[r, self.rows(q)],
            self.sems.bs.at[r, q],
            self.sems.br.at[r, q],
            self.place.core,
        )

    def back_y(self, r, q):
        g = self.place
        return remote(
            self.sendy.at[r, self.rows(q)],
            self.rety.at[g.ny - r, self.rows(q)],
            self.sems.zs.at[r, q],
            self.sems.zr.at[g.ny - r, q],
            g.ahead(r),
        )

    def back_y_arrival(self, r, q):
        g = self.place
        return remote(
            self.sendy.at[r, self.rows(q)],
            self.rety.at[r, self.rows(q)],
            self.sems.zs.at[r, q],
            self.sems.zr.at[r, q],
            g.ahead(r),
        )

    def send_own(self):
        for q in range(CHUNKS):
            for r in range(1, self.place.ny):
                self.y_own(r, q).start()
        self.core_own().start()

    def run(self, local_block, remote_block):
        ny = self.place.ny
        items = [(r, q) for q in range(CHUNKS) for r in range(1, ny)]
        self.core_own().wait_recv()
        local_block()
        self.back_local().start()
        if items:
            self.y_own(*items[0]).wait_recv()
            self.forward(*items[0]).start()
        for i, (r, q) in enumerate(items):
            self.forward(r, q).wait_recv()
            own = remote_block(r, q)
            self.back_core(r, q).start()
            if i + 1 < len(items):
                self.y_own(*items[i + 1]).wait_recv()
                self.forward(*items[i + 1]).start()
            self.back_core(r, q).wait_recv()
            here = self.rows(q)
            self.sendy[r, here, :] = (own() + self.retc[r, here, :].astype(F32)).astype(BF16)
            self.back_y(r, q).start()
        self.back_local().wait_recv()

    def arrived(self, q):
        for r in range(1, self.place.ny):
            self.back_y_arrival(r, q).wait_recv()

    def finish(self):
        ny = self.place.ny
        self.core_own().wait_send()
        self.back_local().wait_send()
        for q in range(CHUNKS):
            for r in range(1, ny):
                self.y_own(r, q).wait_send()
                self.forward(r, q).wait_send()
                self.back_core(r, q).wait_send()
                self.back_y(r, q).wait_send()


class Sems:
    def __init__(self, refs, m):
        self.cs, self.cr, self.ys, self.yr, self.bs, self.br, self.zs, self.zr = [ref.at[m] for ref in refs]


def sem_shapes(micro, ny):
    return [pltpu.SemaphoreType.DMA((micro, ny, CHUNKS)) for _ in range(8)]


def chosen_gates(logits_t, route):
    experts = lax.broadcasted_iota(jnp.int32, logits_t.shape, 0)
    chosen = route[0:1, :] == experts
    for k in range(1, route.shape[0]):
        chosen = chosen | (route[k : k + 1, :] == experts)
    masked = jnp.where(chosen, logits_t, NEGATIVE)
    raised = jnp.where(chosen, jnp.exp(masked - jnp.max(masked, 0, keepdims=True)), 0.0)
    return raised / jnp.sum(raised, 0, keepdims=True)


def gate_lanes(gates_t, expert):
    rows = lax.broadcasted_iota(jnp.int32, gates_t.shape, 0)
    one = jnp.sum(jnp.where(rows == expert, gates_t, 0.0), 0, keepdims=True)
    return jnp.transpose(jnp.broadcast_to(one, (128, one.shape[1])))


def widen(lanes, width):
    return jnp.concatenate([lanes] * (width // 128), 1)


def forward_kernel(
    ny, sections,
    x_ref, segc_ref, segr_ref, route_ref, small_ref, cos_ref, sin_ref,
    wqkv_h, wout_h, wg_h, wu_h, wd_h,
    out_ref, hin_ref, h1_ref, qkv_ref, ob_ref, xm_ref, gates_ref,
    wqkv, wout, wg, wu, wd, hid, accl, accr, gl, retl, retc, rety, sendl, sendc, sendy,
    wsem, xs, xr, *sem_refs,
):
    micro, tokens, width = x_ref.shape
    hidden = wg.shape[2]
    span = tokens // CHUNKS
    loads = [
        pltpu.make_async_copy(src, dst, wsem.at[i])
        for i, (src, dst) in enumerate([(wqkv_h, wqkv), (wout_h, wout), (wg_h, wg), (wu_h, wu), (wd_h, wd)])
    ]
    for load in loads:
        load.start()
    g = Place(ny)
    g.greet()
    gain_a = small_ref[ROUTER_ROWS : ROUTER_ROWS + 1, :].astype(F32)
    gain_m = small_ref[ROUTER_ROWS + 1 : ROUTER_ROWS + 2, :].astype(F32)
    cos, sin = cos_ref[...], sin_ref[...]

    def hop(m, q):
        here = pl.ds(q * span, span)
        return remote(out_ref.at[m, here], hin_ref.at[m, here], xs.at[m, q], xr.at[m, q], g.x)

    def experts(rows, lanes, keep):
        count = rows.shape[0]
        for j in range(2):
            for n in range(hidden // 256):
                cols = slice(n * 256, (n + 1) * 256)
                a = dot(rows, wg[j, :, cols])
                b = dot(rows, wu[j, :, cols])
                act = 0.5 * a * (1.0 + jnp.tanh(GELU_C * (a + GELU_A * a * a * a)))
                hid[j, 0:count, cols] = (act * b).astype(BF16)
        for n in range(width // 512):
            cols = slice(n * 512, (n + 1) * 512)
            total = None
            for j in range(2):
                eo = dot(hid[j, 0:count, :], wd[j, :, cols]).astype(BF16).astype(F32)
                term = widen(lanes[j], 512) * eo
                total = term if total is None else total + term
            keep(cols, total)

    def body(m, carry):
        @pl.when(g.s == 0)
        def _():
            hin_ref[m] = x_ref[m]

        @pl.when(g.s > 0)
        def _():
            for q in range(CHUNKS):
                hop(m, q).wait_recv()

        h = hin_ref[m].astype(F32)
        xa = (h * lax.rsqrt(jnp.mean(h * h, -1, keepdims=True) + EPS) * gain_a).astype(BF16)

        @pl.when(m == 0)
        def _():
            loads[0].wait()

        turned = QUERY_HEADS + KEY_VALUE_HEADS
        for i in range(wqkv.shape[1] // 256):
            mixed = dot(xa, wqkv[:, i * 256 : (i + 1) * 256])
            for half in range(2):
                head = 2 * i + half
                part = mixed[:, half * HEAD : (half + 1) * HEAD]
                if head < turned:
                    part = part * cos + pltpu.roll(part, HEAD // 2, 1) * sin
                qkv_ref[m, :, head * HEAD : (head + 1) * HEAD] = part.astype(BF16)
        bias = mask_bias(segc_ref[m], segr_ref[m])
        bias6 = jnp.concatenate([bias] * GROUP, 0)
        qkv = qkv_ref.at[m]
        for kv in range(KEY_VALUE_HEADS):
            q6 = heads_of(qkv, kv * GROUP, GROUP)
            k = heads_of(qkv, QUERY_HEADS + kv, 1)
            v = heads_of(qkv, turned + kv, 1)
            shares = attention_shares(q6, k, bias6).astype(BF16)
            o6 = dot(shares, v).astype(BF16)
            for i in range(GROUP):
                head = kv * GROUP + i
                ob_ref[m, :, head * HEAD : (head + 1) * HEAD] = o6[i * tokens : (i + 1) * tokens]

        @pl.when(m == 0)
        def _():
            loads[1].wait()

        ob = ob_ref[m]
        for n in range(width // 512):
            cols = slice(n * 512, (n + 1) * 512)
            h1_ref[m, :, cols] = hin_ref[m, :, cols].astype(F32) + dot(ob, wout[:, cols])
        h1 = h1_ref[m]
        xm_ref[m, 0, 0] = (h1 * lax.rsqrt(jnp.mean(h1 * h1, -1, keepdims=True) + EPS) * gain_m).astype(BF16)

        ex = Exchange(g, xm_ref.at[m], retl, retc, rety, sendl, sendc, sendy, Sems(sem_refs, m))
        ex.send_own()

        @pl.when(m == 0)
        def _():
            for load in loads[2:]:
                load.wait()

        def gates_for(r, other, here):
            rows = xm_ref[m, r, other, here, :]
            logits_t = dot_nt(small_ref[0:ROUTER_ROWS, :], rows)
            gates_t = chosen_gates(logits_t, route_ref[g.pack(r, other), m][:, here])
            return gates_t

        def lanes_of(blocks):
            return [
                jnp.concatenate([gate_lanes(gates_t, 2 * g.e + j) for gates_t in blocks], 0) for j in range(2)
            ]

        full = slice(0, tokens)

        def local_block():
            blocks = []
            for other in range(2):
                gates_t = gates_for(0, other, full)
                gates_ref[m, 0, other] = gates_t
                blocks.append(gates_t)

            def keep(cols, total):
                accl[:, cols] = total[0:tokens]
                sendl[:, cols] = total[tokens:].astype(BF16)

            experts(xm_ref[m, 0].reshape(2 * tokens, width), lanes_of(blocks), keep)

        def remote_block(r, q):
            here = slice(q * span, (q + 1) * span)
            blocks = []
            for other in range(2):
                gates_t = gates_for(r, other, here)
                gates_ref[m, r, other, :, here] = gates_t
                blocks.append(jnp.concatenate([gates_t] * (128 // span), 1))
            lanes = [
                jnp.concatenate([gate_lanes(gates_t, 2 * g.e + j)[0:span] for gates_t in blocks], 0)
                for j in range(2)
            ]

            def keep(cols, total):
                accr[:, cols] = total[0:span]
                sendc[r, here, cols] = total[span:].astype(BF16)

            experts(xm_ref[m, r, :, here, :].reshape(2 * span, width), lanes, keep)
            return lambda: accr[...]

        ex.run(local_block, remote_block)
        for q in range(CHUNKS):
            here = slice(q * span, (q + 1) * span)
            ex.arrived(q)
            total = h1_ref[m, here, :] + accl[here, :] + retl[here, :].astype(F32)
            for r in range(1, ny):
                total = total + rety[r, here, :].astype(F32)
            out_ref[m, here, :] = total.astype(BF16)

            @pl.when(g.s < sections - 1)
            def _():
                hop(m, q).start()

        ex.finish()
        return carry

    lax.fori_loop(0, micro, body, 0)

    @pl.when(g.s < sections - 1)
    def _():
        for m in range(micro):
            for q in range(CHUNKS):
                hop(m, q).wait_send()


def backward_kernel(
    ny, sections,
    cot_ref, segc_ref, segr_ref, small_ref, cos_ref, sin_ref,
    hin_ref, h1_ref, qkv_ref, gates_ref,
    xm_h, wqkv_h, wout_h, wg_h, wu_h, wd_h,
    gin_ref, grows_ref, xa_ref, dqkv_ref, dattn_ref, gsmall_ref,
    wqkv, wout, wg, wu, wd, xm_s, hid, act_s, slope_s, da_s, db_s, accl, accr, dh1_s, n_s,
    retl, retc, rety, sendl, sendc, sendy,
    wsem, xmsem, xs, xr, *sem_refs,
):
    micro, tokens, width = cot_ref.shape
    hidden = wg.shape[2]
    span = tokens // CHUNKS
    loads = [
        pltpu.make_async_copy(src, dst, wsem.at[i])
        for i, (src, dst) in enumerate([(wg_h, wg), (wu_h, wu), (wd_h, wd), (wout_h, wout), (wqkv_h, wqkv)])
    ]
    for load in loads:
        load.start()
    g = Place(ny)
    g.greet()
    gain_a = small_ref[ROUTER_ROWS : ROUTER_ROWS + 1, :].astype(F32)
    gain_m = small_ref[ROUTER_ROWS + 1 : ROUTER_ROWS + 2, :].astype(F32)
    cos, sin = cos_ref[...], sin_ref[...]
    gsmall_ref[...] = jnp.zeros_like(gsmall_ref)

    def hop(m, q):
        here = pl.ds(q * span, span)
        return remote(gin_ref.at[m, here], grows_ref.at[m, 0, 0, here], xs.at[m, q], xr.at[m, q], g.x)

    def body(m, carry):
        load_xm = pltpu.make_async_copy(xm_h.at[m], xm_s, xmsem)
        load_xm.start()

        @pl.when(g.s == sections - 1)
        def _():
            grows_ref[m, 0, 0] = cot_ref[m]

        @pl.when(g.s < sections - 1)
        def _():
            for q in range(CHUNKS):
                hop(m, q).wait_recv()

        ex = Exchange(g, grows_ref.at[m], retl, retc, rety, sendl, sendc, sendy, Sems(sem_refs, m))
        ex.send_own()

        @pl.when(m == 0)
        def _():
            for load in loads[:3]:
                load.wait()

        load_xm.wait()

        def again(r, _):
            rows = xm_s[r].reshape(2 * tokens, width)
            for j in range(2):
                for n in range(hidden // 256):
                    cols = slice(n * 256, (n + 1) * 256)
                    a = dot(rows, wg[j, :, cols])
                    b = dot(rows, wu[j, :, cols])
                    square = a * a
                    th = jnp.tanh(GELU_C * (a + GELU_A * square * a))
                    half = 0.5 * (1.0 + th)
                    act = a * half
                    slope = half + (0.5 * GELU_C) * a * (1.0 - th * th) * (1.0 + (3.0 * GELU_A) * square)
                    shape = (2, tokens, 256)
                    hid[j, r, :, :, cols] = (act * b).astype(BF16).reshape(shape)
                    act_s[j, r, :, :, cols] = act.astype(BF16).reshape(shape)
                    slope_s[j, r, :, :, cols] = (slope * b).astype(BF16).reshape(shape)
            return 0

        lax.fori_loop(0, ny, again, 0)

        def experts(rows, r, here, keep):
            count = 2 * (here.stop - here.start)
            part = slice(0, count)
            lane = lax.broadcasted_iota(jnp.int32, (count, 128), 1)
            gate_grads = jnp.zeros((count, 128), F32)
            for j in range(2):
                expert = 2 * g.e + j
                lanes = []
                for other in range(2):
                    gates_t = gates_ref[m, r, other]
                    lanes.append(gate_lanes(gates_t, expert)[here])
                lanes = widen(jnp.concatenate(lanes, 0), 256)
                summed = jnp.zeros((count, 1), F32)
                for n in range(hidden // 256):
                    cols = slice(n * 256, (n + 1) * 256)
                    u = dot_nt(rows, wd[j, cols, :])
                    inner = hid[j, r, :, here, cols].reshape(count, 256).astype(F32)
                    summed = summed + jnp.sum(u * inner, -1, keepdims=True)
                    u = u * lanes
                    slope = slope_s[j, r, :, here, cols].reshape(count, 256).astype(F32)
                    act = act_s[j, r, :, here, cols].reshape(count, 256).astype(F32)
                    da_s[j, part, cols] = (u * slope).astype(BF16)
                    db_s[j, part, cols] = (u * act).astype(BF16)
                high = summed.astype(BF16).astype(F32)
                gate_grads = jnp.where(lane == expert, high, gate_grads)
                gate_grads = jnp.where(lane == expert + 64, summed - high, gate_grads)
            for n in range(width // 512):
                cols = slice(n * 512, (n + 1) * 512)
                total = None
                for j in range(2):
                    term = dot_nt(da_s[j, part, :], wg[j, cols, :]) + dot_nt(db_s[j, part, :], wu[j, cols, :])
                    total = term if total is None else total + term
                keep(cols, total)
            keep(slice(width, width + 128), gate_grads)

        full = slice(0, tokens)

        def local_block():
            def keep(cols, total):
                accl[:, cols] = total[0:tokens]
                sendl[:, cols] = total[tokens:].astype(BF16)

            experts(grows_ref[m, 0].reshape(2 * tokens, width), 0, full, keep)

        def remote_block(r, q):
            here = slice(q * span, (q + 1) * span)

            def keep(cols, total):
                accr[:, cols] = total[0:span]
                sendc[r, here, cols] = total[span:].astype(BF16)

            experts(grows_ref[m, r, :, here, :].reshape(2 * span, width), r, here, keep)
            return lambda: accr[...]

        ex.run(local_block, remote_block)
        for q in range(CHUNKS):
            ex.arrived(q)
        total = accl[...] + retl[...].astype(F32)
        for r in range(1, ny):
            total = total + rety[r].astype(F32)
        dgates = total[:, width:]
        dgates = dgates + pltpu.roll(dgates, 64, 1)
        gates_t = gates_ref[m, 0, 0]
        gates = jnp.transpose(
            jnp.concatenate([gates_t, jnp.zeros((128 - ROUTER_ROWS, tokens), F32)], 0)
        )
        dlog = gates * (dgates - jnp.sum(gates * dgates, -1, keepdims=True))
        dlog = dlog[:, 0:SMALL_ROWS]
        high = dlog.astype(BF16)
        low = (dlog - high.astype(F32)).astype(BF16)
        router = small_ref[...]
        dxm = total[:, 0:width] + dot(high, router) + dot(low, router)
        xm = xm_s[0, 0]
        gsmall_ref[0:ROUTER_ROWS, :] += (dot_tn(high, xm) + dot_tn(low, xm))[0:ROUTER_ROWS]
        h1 = h1_ref[m]
        rinv = lax.rsqrt(jnp.mean(h1 * h1, -1, keepdims=True) + EPS)
        n2 = h1 * rinv
        gsmall_ref[ROUTER_ROWS + 1 : ROUTER_ROWS + 2, :] += jnp.sum(dxm * n2, 0, keepdims=True)
        scaled = dxm * gain_m
        dh1 = grows_ref[m, 0, 0].astype(F32) + rinv * (scaled - n2 * jnp.mean(scaled * n2, -1, keepdims=True))
        dh1_s[...] = dh1
        dattn = dh1.astype(BF16)
        dattn_ref[m] = dattn

        @pl.when(m == 0)
        def _():
            for load in loads[3:]:
                load.wait()

        bias = mask_bias(segc_ref[m], segr_ref[m])
        bias6 = jnp.concatenate([bias] * GROUP, 0)
        qkv = qkv_ref.at[m]
        turned = QUERY_HEADS + KEY_VALUE_HEADS

        def unturn(part):
            return part * cos - pltpu.roll(part, HEAD // 2, 1) * sin

        for kv in range(KEY_VALUE_HEADS):
            wide = GROUP * HEAD
            dob = dot_nt(dattn, wout[kv * wide : (kv + 1) * wide, :]).astype(BF16)
            dob6 = heads_of(dob, 0, GROUP)
            q6 = heads_of(qkv, kv * GROUP, GROUP)
            k = heads_of(qkv, QUERY_HEADS + kv, 1)
            v = heads_of(qkv, turned + kv, 1)
            shares = attention_shares(q6, k, bias6)
            dshares = dot_nt(dob6, v)
            dv = dot_tn(shares.astype(BF16), dob6)
            ds = (shares * (dshares - jnp.sum(shares * dshares, -1, keepdims=True))).astype(BF16)
            dq6 = dot(ds, k) * SCALE
            dk = dot_tn(ds, q6) * SCALE
            for i in range(GROUP):
                head = kv * GROUP + i
                dqkv_ref[m, :, head * HEAD : (head + 1) * HEAD] = unturn(
                    dq6[i * tokens : (i + 1) * tokens]
                ).astype(BF16)
            head = QUERY_HEADS + kv
            dqkv_ref[m, :, head * HEAD : (head + 1) * HEAD] = unturn(dk).astype(BF16)
            head = turned + kv
            dqkv_ref[m, :, head * HEAD : (head + 1) * HEAD] = dv.astype(BF16)

        h = hin_ref[m].astype(F32)
        rinv = lax.rsqrt(jnp.mean(h * h, -1, keepdims=True) + EPS)
        n1 = h * rinv
        xa_ref[m] = (n1 * gain_a).astype(BF16)
        n_s[...] = n1
        dqkv = dqkv_ref[m]
        for n in range(width // 512):
            cols = slice(n * 512, (n + 1) * 512)
            accl[:, cols] = dot_nt(dqkv, wqkv[cols, :])
        dxa = accl[:, 0:width]
        n1 = n_s[...]
        gsmall_ref[ROUTER_ROWS : ROUTER_ROWS + 1, :] += jnp.sum(dxa * n1, 0, keepdims=True)
        scaled = dxa * gain_a
        grad = dh1_s[...] + rinv * (scaled - n1 * jnp.mean(scaled * n1, -1, keepdims=True))
        gin_ref[m] = grad.astype(BF16)

        @pl.when(g.s > 0)
        def _():
            for q in range(CHUNKS):
                hop(m, q).start()

        ex.finish()
        return carry

    lax.fori_loop(0, micro, body, 0)

    @pl.when(g.s > 0)
    def _():
        for m in range(micro):
            for q in range(CHUNKS):
                hop(m, q).wait_send()


VMEM = pl.BlockSpec(memory_space=pltpu.VMEM)
ANY = pl.BlockSpec(memory_space=pl.ANY)


def per_device(
    ne, sections,
    layer_input, cotangent, segments, routes, attn_gain, w_qkv, w_out, moe_gain, w_router, w_gate, w_up, w_down,
):
    ny = ne // 2
    micro, _, tokens, width = layer_input.shape
    total_experts = w_router.shape[2]
    hidden = w_gate.shape[3]
    owners = ("expert", "dp")
    shard = w_qkv.shape[1]
    small = jnp.concatenate(
        [
            jnp.pad(w_router[0], ((0, 0), (0, ROUTER_ROWS - total_experts))),
            attn_gain[0][:, None],
            moe_gain[0][:, None],
            jnp.zeros((shard, SMALL_ROWS - ROUTER_ROWS - 2), BF16),
        ],
        1,
    )
    small = lax.all_gather(small, owners, axis=0, tiled=True).T
    wqkv = lax.all_gather(w_qkv[0], owners, axis=0, tiled=True)
    wout = lax.all_gather(w_out[0], owners, axis=0, tiled=True)
    route = lax.all_gather(jnp.transpose(routes[0, :, 0], (0, 2, 1)), "expert", axis=0)
    cos, sin = rotary_tables(tokens)
    segs = segments[:, 0]
    segc, segr = segs[:, :, None], segs[:, None, :]
    x = layer_input[:, 0]
    cot = cotangent[:, 0]
    wg, wu, wd = w_gate[0], w_up[0], w_down[0]
    span = tokens // CHUNKS
    qkv_width = wqkv.shape[1]

    def shape(*dims, dtype=BF16):
        return jax.ShapeDtypeStruct(dims, dtype)

    weight_scratch = {
        "wqkv": pltpu.VMEM(wqkv.shape, BF16),
        "wout": pltpu.VMEM(wout.shape, BF16),
        "wg": pltpu.VMEM(wg.shape, BF16),
        "wu": pltpu.VMEM(wu.shape, BF16),
        "wd": pltpu.VMEM(wd.shape, BF16),
    }
    order = ("wqkv", "wout", "wg", "wu", "wd")
    hop_sems = [pltpu.SemaphoreType.DMA((micro, CHUNKS)) for _ in range(2)]

    def returns(wide):
        return [
            pltpu.VMEM((tokens, wide), BF16),
            pltpu.VMEM((ny, tokens, wide), BF16),
            pltpu.VMEM((ny, tokens, wide), BF16),
            pltpu.VMEM((tokens, wide), BF16),
            pltpu.VMEM((ny, tokens, wide), BF16),
            pltpu.VMEM((ny, tokens, wide), BF16),
        ]

    out, hin, h1, qkv, ob, xm, gates = pl.pallas_call(
        functools.partial(forward_kernel, ny, sections),
        out_shape=(
            shape(micro, tokens, width),
            shape(micro, tokens, width),
            shape(micro, tokens, width, dtype=F32),
            shape(micro, tokens, qkv_width),
            shape(micro, tokens, width),
            shape(micro, ny, 2, tokens, width),
            shape(micro, ny, 2, ROUTER_ROWS, tokens, dtype=F32),
        ),
        in_specs=[VMEM] * 7 + [ANY] * 5,
        out_specs=tuple([VMEM] * 7),
        scratch_shapes=[weight_scratch[name] for name in order]
        + [
            pltpu.VMEM((2, 2 * tokens, hidden), BF16),
            pltpu.VMEM((tokens, width), F32),
            pltpu.VMEM((span, width), F32),
            pltpu.VMEM((8, 128), F32),
        ]
        + returns(width)
        + [pltpu.SemaphoreType.DMA((5,))]
        + hop_sems
        + sem_shapes(micro, ny),
        compiler_params=pltpu.CompilerParams(
            collective_id=0, has_side_effects=True, vmem_limit_bytes=60 * 2**20
        ),
        name="layers_forward",
    )(x, segc, segr, route, small, cos, sin, wqkv, wout, wg, wu, wd)

    wide = width + 128
    every = (2, ny, 2, tokens, hidden)
    gin, grows, xa, dqkv, dattn, gsmall = pl.pallas_call(
        functools.partial(backward_kernel, ny, sections),
        out_shape=(
            shape(micro, tokens, width),
            shape(micro, ny, 2, tokens, width),
            shape(micro, tokens, width),
            shape(micro, tokens, qkv_width),
            shape(micro, tokens, width),
            shape(SMALL_ROWS, width, dtype=F32),
        ),
        in_specs=[VMEM] * 10 + [ANY] * 6,
        out_specs=tuple([VMEM] * 6),
        scratch_shapes=[weight_scratch[name] for name in order]
        + [
            pltpu.VMEM((ny, 2, tokens, width), BF16),
            pltpu.VMEM(every, BF16),
            pltpu.VMEM(every, BF16),
            pltpu.VMEM(every, BF16),
            pltpu.VMEM((2, 2 * tokens, hidden), BF16),
            pltpu.VMEM((2, 2 * tokens, hidden), BF16),
            pltpu.VMEM((tokens, wide), F32),
            pltpu.VMEM((span, wide), F32),
            pltpu.VMEM((tokens, width), F32),
            pltpu.VMEM((tokens, width), F32),
        ]
        + returns(wide)
        + [pltpu.SemaphoreType.DMA((5,)), pltpu.SemaphoreType.DMA]
        + hop_sems
        + sem_shapes(micro, ny),
        compiler_params=pltpu.CompilerParams(
            collective_id=1, has_side_effects=True, vmem_limit_bytes=62 * 2**20
        ),
        name="layers_backward",
    )(cot, segc, segr, small, cos, sin, hin, h1, qkv, gates, xm, wqkv, wout, wg, wu, wd)

    e = lax.axis_index("expert")
    packs = micro * ny * 2
    rows = xm.reshape(packs * tokens, width)
    grads = grows.reshape(packs * tokens, width)
    own = lax.dynamic_slice_in_dim(gates, 2 * e, 2, 3)
    own = jnp.transpose(own, (3, 0, 1, 2, 4)).reshape(2, packs * tokens, 1)
    a = jnp.einsum("td,jdh->jth", rows, wg, preferred_element_type=F32)
    b = jnp.einsum("td,jdh->jth", rows, wu, preferred_element_type=F32)
    u = own * jnp.einsum("td,jhd->jth", grads, wd, preferred_element_type=F32)
    th = jnp.tanh(GELU_C * (a + GELU_A * a * a * a))
    half = 0.5 * (1.0 + th)
    act = a * half
    slope = half + (0.5 * GELU_C) * a * (1.0 - th * th) * (1.0 + (3.0 * GELU_A) * a * a)
    da = (u * b * slope).astype(BF16)
    db = (u * act).astype(BF16)
    gh = (own * act * b).astype(BF16)
    grad_gate = jnp.einsum("td,jth->jdh", rows, da, preferred_element_type=F32)
    grad_up = jnp.einsum("td,jth->jdh", rows, db, preferred_element_type=F32)
    grad_down = jnp.einsum("jth,td->jhd", gh, grads, preferred_element_type=F32)

    def over_dp(value):
        return lax.psum_scatter(value.astype(BF16), "dp", scatter_dimension=1, tiled=True).astype(F32)

    grad_qkv = jnp.einsum("mtd,mte->de", xa, dqkv, preferred_element_type=F32).astype(BF16)
    grad_out = jnp.einsum("mtd,mte->de", ob, dattn, preferred_element_type=F32).astype(BF16)
    grad_qkv = lax.psum_scatter(grad_qkv, owners, scatter_dimension=0, tiled=True).astype(F32)
    grad_out = lax.psum_scatter(grad_out, owners, scatter_dimension=0, tiled=True).astype(F32)
    grad_small = lax.psum_scatter(gsmall.T, owners, scatter_dimension=0, tiled=True)
    return (
        out[None, :, None],
        gin[None, :, None],
        grad_small[:, ROUTER_ROWS][None],
        grad_qkv[None],
        grad_out[None],
        grad_small[:, ROUTER_ROWS + 1][None],
        grad_small[:, 0:total_experts][None],
        over_dp(grad_gate)[None],
        over_dp(grad_up)[None],
        over_dp(grad_down)[None],
    )


def solution(mesh):
    owners = ("expert", "dp")
    return jax.shard_map(
        functools.partial(per_device, mesh.shape["expert"], mesh.shape["section"]),
        mesh=mesh,
        in_specs=(
            P(None, owners, None, None),
            P(None, owners, None, None),
            P(None, owners, None),
            P("section", None, owners, None, None),
            P("section", owners),
            P("section", owners, None),
            P("section", owners, None),
            P("section", owners),
            P("section", owners, None),
            P("section", "expert", None, None),
            P("section", "expert", None, None),
            P("section", "expert", None, None),
        ),
        out_specs=(
            P("section", None, owners, None, None),
            P("section", None, owners, None, None),
            P("section", owners),
            P("section", owners, None),
            P("section", owners, None),
            P("section", owners),
            P("section", owners, None),
            P("section", "expert", "dp", None),
            P("section", "expert", "dp", None),
            P("section", "expert", "dp", None),
        ),
        check_vma=False,
    )
```

time: 1320 us -> 862 us (0.65)
  Pallas kernels: 0 us -> 223 us
  matrix products: 262 us -> 61.8 us
  other arithmetic: 139 us -> 7.82 us
  blocking collectives: 167 us -> 41.5 us
  local copies, waits for them, and re-layouts: 153 us -> 66.2 us
  waiting for transfers between devices: 515 us -> 437 us
  starting transfers between devices: 56.2 us -> 0.32 us
    pallas_call x0 -> x2, Pallas kernels: none -> 223 us  [the longest x1 161 us: per_device(): pl.pallas_call(functools.partial(backward_kernel, ny, sections), out_shap...]
    dot_general x78 -> x8, matrix products: 262 us -> 61.8 us  [the longest x1 12.4 us: per_device(): grad_gate = jnp.einsum('td,jth->jdh', rows, da, preferred_element_type=F32)]
    unnamed x9 -> x11, waiting for transfers between devices: 1.48 us -> 167 us
    all_to_all x11 -> x0, waiting for transfers between devices: 150 us -> none  [the longest x3 53.8 us: per_device(): lax.all_to_all(grad_send.reshape(owners, per_owner, capacity, D), 'expert...]
    unnamed x2 -> x0, blocking collectives: 99.9 us -> none
    reduce_scatter x5 -> x3, waiting for transfers between devices: 290 us -> 194 us  [the longest x1 86.7 us: per_device(): lax.psum_scatter(grad_qkv, owners, scatter_dimension=0, tiled=True)]
    gather x27 -> x0, local copies, waits for them, and re-layouts: 47.2 us -> none  [the longest x3 10.6 us: per_device(): jnp.take(grad_rows, source, 0)]
    all_to_all x11 -> x0, starting transfers between devices: 44 us -> none  [the longest x3 14.1 us: per_device(): lax.all_to_all(grad_send.reshape(owners, per_owner, capacity, D), 'expert...]
  transfers between devices with their start and end apart: 23 -> 8, of which waited for: 17 -> 7; matrix products, arithmetic and copies ran while one was open for 24% -> 15% of each run, Pallas kernels for 0% -> 0%
where the time goes in v1:
time: 862 us; the launch traced here: 853 us
  waiting for transfers between devices  437 us (51%)
  Pallas kernels  223 us (26%)
  local copies, waits for them, and re-layouts  66.2 us (8%)
  matrix products  61.8 us (7%)
  blocking collectives  41.5 us (5%)
  between operations  14.9 us (2%)
    unnamed x11, waiting for transfers between devices  167 us
    pallas_call x1, Pallas kernels, per_device(): pl.pallas_call(functools.partial(backward_kernel, ny, sections), out_shap...  161 us
    reduce_scatter x1, waiting for transfers between devices, per_device(): lax.psum_scatter(grad_qkv, owners, scatter_dimension=0, tiled=True)  86.7 us
    reduce_scatter x1, waiting for transfers between devices, over_dp(): lax.psum_scatter(value.astype(BF16), 'dp', scatter_dimension=1, tiled=True)  81.1 us
    unnamed x43, local copies, waits for them, and re-layouts  62.8 us
    all_gather x1, waiting for transfers between devices, per_device(): wqkv = lax.all_gather(w_qkv[0], owners, axis=0, tiled=True)  62.7 us
    pallas_call x1, Pallas kernels, per_device(): pl.pallas_call(functools.partial(forward_kernel, ny, sections), out_shape...  62.2 us
    all_gather x1, blocking collectives, per_device(): small = lax.all_gather(small, owners, axis=0, tiled=True).T  35.7 us
  transfers between devices with their start and end apart: 8, of which 7 were waited for; matrix products, arithmetic and copies ran while one was open for 15% of the time, Pallas kernels for 0%

profile of v1, /device:TPU:0, one launch (start us, length us, event | category | flops | bytes accessed | tf_op | source)
XLA Modules:
  0.0 853.0 jit_solution(1689579118023943966)
XLA Ops:
  9.6 35.7 %all-gather.3 = bf16[16,96,32]{1,2,0:T(8,128)(2,1)S(1)} all-gather(bf16[1,96,32]{1,2,0:T(8,128)(2,1)S(1)} %fusion.17), channel_id=1, replica_groups=mesh['section'=2,'expert'=4,'dp'=4] {'expert','dp'}, dimensions={0}, use_global_device_ids=true | all-gather | bytes 104448 | tf_op jit(solution)/shard_map/all_gather | solution.py:673
  47.6 5.9 all-gather
  53.4 13.8 %all-gather.9.cloned.1.call-done = bf16[1,1536,1536]{2,1,0:T(8,128)(2,1)} async-done(((bf16[1,96,1536]{2,1,0:T(8,128)(2,1)}), bf16[1,1536,1536]{2,1,0:T(8,128)(2,1)}) %all-gather.9.cloned.1.call-update) | async-done | bytes 4718608 | tf_op jit(solution)/shard_map/all_gather | solution.py:675
  67.2 62.7 %all-gather.7.cloned.1.call-done = bf16[1,1536,2048]{2,1,0:T(8,128)(2,1)} async-done(((bf16[1,96,2048]{2,1,0:T(8,128)(2,1)}), bf16[1,1536,2048]{2,1,0:T(8,128)(2,1)}) %all-gather.7.cloned.1.call-update) | async-done | bytes 6291472 | tf_op jit(solution)/shard_map/all_gather | solution.py:674
  129.9 62.2 %layers_forward.1 = (bf16[2,128,1536]{2,1,0:T(8,128)(2,1)}, bf16[2,128,1536]{2,1,0:T(8,128)(2,1)}, f32[2,128,1536]{2,1,0:T(8,128)}, bf16[2,128,2048]{2,1,0:T(8,1...) custom-call(bf16[2,128,1536]{2,1,0:T(8,128)(2,1)} %bitcast.151, ...), custom_call_target="tpu_custom_call" | custom-call | tf_op jit(solution)/shard_map/layers_forward/pallas_call | solution.py:709
  192.2 161.1 %layers_backward.1 = (bf16[2,128,1536]{2,1,0:T(8,128)(2,1)}, bf16[2,2,2,128,1536]{4,3,2,1,0:T(8,128)(2,1)}, bf16[2,128,1536]{2,1,0:T(8,128)(2,1)}, bf16[2,128,20...) custom-call(bf16[2,128,1536]{2,1,0:T(8,128)(2,1)} %bitcast.154, s32[2,128,1]{2,1,0:T(8,128)} %copy.47.segc_ref, ...), custom_call_target="tpu_custom_call" | custom-call | tf_op jit(solution)/shard_map/layers_backward/pallas_call | solution.py:741
  353.3 2.1 copy.63
  355.5 4.8 bitcast_convert_fusion.1
  361.2 8.2 fusion.22
  369.5 5.1 fusion.18
  374.5 2.6 copy-done.10
  377.1 8.2 convert_bitcast_fusion
  385.3 12.6 %copy.67 = bf16[2,1536,768]{2,0,1:T(2,128)(2,1)} copy(bf16[2,1536,768]{1,2,0:T(8,128)(2,1)} %convert_bitcast_fusion) | data formatting | bytes 9437184
  397.9 5.7 copy.73
  403.7 7.3 fusion.20
  411.0 2.6 copy-done.9
  413.6 12.4 %convert_bitcast_fusion.1 = bf16[2,1536,768]{1,2,0:T(8,128)(2,1)} fusion(bf16[1024,1536,1]{1,0,2:T(8,128)(2,1)S(1)} %bitcast.148, f32[1024,2,768]{2,0,1:T(8,128)} %copy-done.8, f32[1024,2,768]{2,0,1:T(8,128)S(1)} %fusion.20, f32[1024,2,768]{2,0,1:T(8,128)} %copy-done.10, f32[2,1024]{1,0:T(2,128)S(1)} %bitcast.160), kind=kOutput, calls=%fused_computation.21 | convolution fusion | flops 4865654784 | bytes 26746880 | tf_op jit(solution)/shard_map/td,jth->jdh/dot_general | solution.py:792
  426.0 12.7 %copy.65 = bf16[2,1536,768]{2,0,1:T(2,128)(2,1)} copy(bf16[2,1536,768]{1,2,0:T(8,128)(2,1)} %convert_bitcast_fusion.1) | data formatting | bytes 9437184
  438.7 5.4 copy.72
  444.3 11.3 %convolution_convert_fusion = bf16[2,768,1536]{2,1,0:T(8,128)(2,1)} fusion(bf16[1024,1536,1]{1,0,2:T(8,128)(2,1)} %bitcast.169, f32[1024,2,768]{2,0,1:T(8,128)} %copy-done.9, f32[2,1024]{1,0:T(2,128)S(1)} %bitcast.161, f32[1024,2,768]{2,0,1:T(8,128)} %copy-done.8), kind=kOutput, calls=%fused_computation.22 | convolution fusion | flops 4851499008 | bytes 20455424 | tf_op jit(solution)/shard_map/jth,td->jhd/dot_general | solution.py:794
  455.7 4.5 bitcast_convert_fusion
  463.8 25.9 %reduce-scatter.15.cloned.1.call-done = bf16[96,1536]{1,0:T(8,128)(2,1)} async-done(((bf16[1536,1536]{1,0:T(8,128)(2,1)}), bf16[96,1536]{1,0:T(8,128)(2,1)}) %reduce-scatter.15.cloned.1.call-update) | async-done | bytes 294928 | tf_op jit(solution)/shard_map/reduce_scatter | solution.py:802
  491.6 84.7 %reduce-scatter.23.cloned.1.call-done = bf16[384,1536]{1,0:T(8,128)(2,1)} async-done(((bf16[1536,1536]{1,0:T(8,128)(2,1)}), bf16[384,1536]{1,0:T(8,128)(2,1)}) %reduce-scatter.23.cloned.1.call-update) | async-done | bytes 1179664
  576.2 3.2 reshape.49
  579.4 2.0 copy.68
  581.5 2.0 copy.57
  583.5 80.7 %reduce-scatter.21.cloned.1.call-done = bf16[384,1536]{1,0:T(8,128)(2,1)} async-done(((bf16[1536,1536]{1,0:T(8,128)(2,1)}), bf16[384,1536]{1,0:T(8,128)(2,1)}) %reduce-scatter.21.cloned.1.call-update) | async-done | bytes 1179664
  664.2 2.9 reshape.47
  667.1 2.0 copy.66
  671.2 81.1 %reduce-scatter.17.cloned.1.call-done = bf16[2,192,1536]{2,1,0:T(8,128)(2,1)} async-done(((bf16[2,768,1536]{2,1,0:T(8,128)(2,1)}), bf16[2,192,1536]{2,1,0:T(8,128)(2,1)}) %reduce-scatter.17.cloned.1.call-update) | async-done | bytes 1179664 | tf_op jit(solution)/shard_map/reduce_scatter | solution.py:797
  752.3 3.0 bitcast_convert_fusion.2
  755.3 86.7 %reduce-scatter.13.cloned.1.call-done = bf16[96,2048]{1,0:T(8,128)(2,1)} async-done(((bf16[1536,2048]{1,0:T(8,128)(2,1)}), bf16[96,2048]{1,0:T(8,128)(2,1)}) %reduce-scatter.13.cloned.1.call-update) | async-done | bytes 393232 | tf_op jit(solution)/shard_map/reduce_scatter | solution.py:801
  (60 shorter events, 17.3 us)
Async XLA Ops:
  7.2 60.0 %all-gather.9.cloned.1.call-start = ((), (), s32[]{:S(2)}) async-start(), calls=%async_computation.10 | async-start | bytes 5013504 | tf_op jit(solution)/shard_map/all_gather | solution.py:675
  7.9 122.0 %all-gather.7.cloned.1.call-start = ((), (), s32[]{:S(2)}) async-start(), calls=%async_computation.9 | async-start | bytes 6684672 | tf_op jit(solution)/shard_map/all_gather | solution.py:674
  8.7 451.6 %reduce-scatter.19.cloned.1.call-start = ((), (), s32[]{:S(2)}) async-start(), calls=%async_computation.11 | async-start | bytes 835584
  192.2 163.3 %copy-start.2 = (bf16[2,128,1536]{2,1,0:T(8,128)(2,1)S(1)}, bf16[2,128,1536]{2,1,0:T(8,128)(2,1)}, u32[]{:S(2)}) copy-start(bf16[2,128,1536]{2,1,0:T(8,128)(2,1)} %get-tuple-element.33) | copy-start | bytes 2359300
  355.4 134.3 %reduce-scatter.15.cloned.1.call-start = ((), (), s32[]{:S(2)}) async-start(), calls=%async_computation.7 | async-start | bytes 5013504 | tf_op jit(solution)/shard_map/reduce_scatter | solution.py:802
  360.3 9.2 %slice-start = ((s8[4718592]{0:T(1024)(128)(4,1)}), s8[524288]{0:T(1024)(128)(4,1)S(1)}, s32[]{:S(2)}) async-start(s8[4718592]{0:T(1024)(128)(4,1)} %bitcast.137), calls=%async_computation.14 | async-start | bytes 1048576
  360.3 216.0 %reduce-scatter.23.cloned.1.call-start = ((), (), s32[]{:S(2)}) async-start(), calls=%async_computation.13 | async-start | bytes 5898240
  361.2 8.3 slice-start.1
  361.2 8.3 copy-start.7
  369.4 5.1 copy-start.8
  369.5 7.7 copy-start
  374.5 2.6 copy-start.10
  397.9 5.7 copy-start.1
  403.6 260.6 %reduce-scatter.21.cloned.1.call-start = ((), (), s32[]{:S(2)}) async-start(), calls=%async_computation.12 | async-start | bytes 5898240
  411.0 2.6 copy-start.9
  444.2 11.5 %copy-start.3 = (bf16[2,128,1536]{2,1,0:T(8,128)(2,1)S(1)}, bf16[2,128,1536]{2,1,0:T(8,128)(2,1)}, u32[]{:S(2)}) copy-start(bf16[2,128,1536]{2,1,0:T(8,128)(2,1)} %get-tuple-element.31) | copy-start | bytes 2359300
  444.2 11.5 %copy-start.4 = (bf16[2,128,2048]{2,1,0:T(8,128)(2,1)S(1)}, bf16[2,128,2048]{2,1,0:T(8,128)(2,1)}, u32[]{:S(2)}) copy-start(bf16[2,128,2048]{2,1,0:T(8,128)(2,1)} %get-tuple-element.32) | copy-start | bytes 3145732
  444.2 308.1 %reduce-scatter.17.cloned.1.call-start = ((), (), s32[]{:S(2)}) async-start(), calls=%async_computation.8 | async-start | bytes 5898240 | tf_op jit(solution)/shard_map/reduce_scatter | solution.py:797
  455.6 386.4 %reduce-scatter.13.cloned.1.call-start = ((), (), s32[]{:S(2)}) async-start(), calls=%async_computation.6 | async-start | bytes 6684672 | tf_op jit(solution)/shard_map/reduce_scatter | solution.py:801
  669.3 174.7 %copy-start.5 = (bf16[2,128,1536]{2,1,0:T(8,128)(2,1)S(1)}, bf16[2,128,1536]{2,1,0:T(8,128)(2,1)}, u32[]{:S(2)}) copy-start(bf16[2,128,1536]{2,1,0:T(8,128)(2,1)} %get-tuple-element.23) | copy-start | bytes 2359300
  671.2 173.6 %copy-start.6 = (bf16[2,128,1536]{2,1,0:T(8,128)(2,1)S(1)}, bf16[2,128,1536]{2,1,0:T(8,128)(2,1)}, u32[]{:S(2)}) copy-start(bf16[2,128,1536]{2,1,0:T(8,128)(2,1)} %get-tuple-element.29) | copy-start | bytes 2359300
Sparse Core Ops, SparseCore 0:
  10.3 56.8 all-gather.8
  69.5 60.3 all-gather.6
  355.5 55.3 reduce-scatter.18
  415.1 74.6 reduce-scatter.14
  491.9 84.2 reduce-scatter.22
  578.4 85.7 reduce-scatter.20
  666.5 85.7 reduce-scatter.16
  756.3 85.7 reduce-scatter.12

commit v2 on v1

--- a/solution.py
+++ b/solution.py
@@ -70,8 +70,9 @@
 
 
 class Place:
-    def __init__(self, ny):
+    def __init__(self, ny, nz):
         self.ny = ny
+        self.nz = nz
         self.s = lax.axis_index("section")
         self.e = lax.axis_index("expert")
         self.d = lax.axis_index("dp")
@@ -90,9 +91,20 @@
         core = 1 - self.c if other else self.c
         return lax.rem(self.y + r, self.ny) * 2 + core
 
-    def greet(self):
+    def z_of(self, k):
+        return lax.rem(self.d + k, self.nz)
+
+    def z_ahead(self, k):
+        return (self.s, self.e, self.z_of(k))
+
+    def z_behind(self, k):
+        return (self.s, self.e, self.z_of(self.nz - k))
+
+    def greet(self, with_x=True):
         barrier = pltpu.get_barrier_semaphore()
-        partners = [self.core, self.x] + [self.ahead(r) for r in range(1, self.ny)]
+        partners = [self.core] + ([self.x] if with_x else [])
+        partners += [self.ahead(r) for r in range(1, self.ny)]
+        partners += [self.z_ahead(k) for k in range(1, self.nz)]
         for partner in partners:
             pl.semaphore_signal(barrier, inc=1, device_id=partner, device_id_type=MESH)
         pl.semaphore_wait(barrier, len(partners))
@@ -102,6 +114,58 @@
     return pltpu.make_async_remote_copy(
         src_ref=src, dst_ref=dst, send_sem=send, recv_sem=recv, device_id=device, device_id_type=MESH
     )
+
+
+class Gather:
+    def __init__(self, place, buf, send, recv, local):
+        self.place, self.buf, self.send, self.recv, self.local = place, buf, send, recv, local
+
+    def one(self, i, k, r, src):
+        return remote(
+            src, self.buf.at[i, k, r], self.send.at[i, k, r], self.recv.at[i, k, r], self.place.z_behind(k)
+        )
+
+    def away(self, i, r, src):
+        return [self.one(i, k, r, src) for k in range(1, self.place.nz)]
+
+    def near(self, i, r, src):
+        return pltpu.make_async_copy(src, self.buf.at[i, 0, r], self.local.at[i, r])
+
+    def push(self, i, r, src, keep=True):
+        if keep:
+            self.near(i, r, src).start()
+        for copy in self.away(i, r, src):
+            copy.start()
+
+    def across(self, i, k, r):
+        g = self.place
+        return remote(
+            self.buf.at[i, k, 0], self.buf.at[i, k, r], self.send.at[i, k, r], self.recv.at[i, k, r], g.behind(r)
+        )
+
+    def pass_on(self, i):
+        for k in range(1, self.place.nz):
+            self.one(i, k, 0, self.buf.at[i, 0, 0]).wait_recv()
+            for r in range(1, self.place.ny):
+                self.across(i, k, r).start()
+
+    def drain(self, i, keep=True):
+        for r in range(self.place.ny):
+            src = self.buf.at[i, 0, r]
+            if keep or r == 0:
+                self.near(i, r, src).wait()
+            for copy in self.away(i, r, src):
+                copy.wait()
+
+    def drain_passed(self, i):
+        g = self.place
+        for r in range(g.ny):
+            self.near(i, r, self.buf.at[i, 0, r]).wait()
+        for copy in self.away(i, 0, self.buf.at[i, 0, 0]):
+            copy.wait_send()
+        for k in range(1, g.nz):
+            for r in range(1, g.ny):
+                self.across(i, k, r).wait()
 
 
 class Exchange:
@@ -148,8 +212,8 @@
 
     def back_core(self, r, q):
         return remote(
-            self.sendc.at[r, self.rows(q)],
-            self.retc.at[r, self.rows(q)],
+            self.sendc.at[r - 1, self.rows(q)],
+            self.retc.at[r - 1, self.rows(q)],
             self.sems.bs.at[r, q],
             self.sems.br.at[r, q],
             self.place.core,
@@ -158,8 +222,8 @@
     def back_y(self, r, q):
         g = self.place
         return remote(
-            self.sendy.at[r, self.rows(q)],
-            self.rety.at[g.ny - r, self.rows(q)],
+            self.sendy.at[r - 1, self.rows(q)],
+            self.rety.at[g.ny - r - 1, self.rows(q)],
             self.sems.zs.at[r, q],
             self.sems.zr.at[g.ny - r, q],
             g.ahead(r),
@@ -168,8 +232,8 @@
     def back_y_arrival(self, r, q):
         g = self.place
         return remote(
-            self.sendy.at[r, self.rows(q)],
-            self.rety.at[r, self.rows(q)],
+            self.sendy.at[r - 1, self.rows(q)],
+            self.rety.at[r - 1, self.rows(q)],
             self.sems.zs.at[r, q],
             self.sems.zr.at[r, q],
             g.ahead(r),
@@ -181,25 +245,30 @@
                 self.y_own(r, q).start()
         self.core_own().start()
 
-    def run(self, local_block, remote_block):
+    def run(self, local_block, remote_block, complete):
         ny = self.place.ny
         items = [(r, q) for q in range(CHUNKS) for r in range(1, ny)]
         self.core_own().wait_recv()
         local_block()
         self.back_local().start()
+
+        def arrive(r, q):
+            self.y_own(r, q).wait_recv()
+            self.forward(r, q).start()
+            if q == CHUNKS - 1:
+                complete(r)
+
         if items:
-            self.y_own(*items[0]).wait_recv()
-            self.forward(*items[0]).start()
+            arrive(*items[0])
         for i, (r, q) in enumerate(items):
             self.forward(r, q).wait_recv()
             own = remote_block(r, q)
             self.back_core(r, q).start()
             if i + 1 < len(items):
-                self.y_own(*items[i + 1]).wait_recv()
-                self.forward(*items[i + 1]).start()
+                arrive(*items[i + 1])
             self.back_core(r, q).wait_recv()
             here = self.rows(q)
-            self.sendy[r, here, :] = (own() + self.retc[r, here, :].astype(F32)).astype(BF16)
+            self.sendy[r - 1, here, :] = (own() + self.retc[r - 1, here, :].astype(F32)).astype(BF16)
             self.back_y(r, q).start()
         self.back_local().wait_recv()
 
@@ -249,12 +318,12 @@
 
 
 def forward_kernel(
-    ny, sections,
+    ny, nz, sections,
     x_ref, segc_ref, segr_ref, route_ref, small_ref, cos_ref, sin_ref,
-    wqkv_h, wout_h, wg_h, wu_h, wd_h,
-    out_ref, hin_ref, h1_ref, qkv_ref, ob_ref, xm_ref, gates_ref,
-    wqkv, wout, wg, wu, wd, hid, accl, accr, gl, retl, retc, rety, sendl, sendc, sendy,
-    wsem, xs, xr, *sem_refs,
+    cot_h, slices_h, wqkv_h, wout_h, wg_h, wu_h, wd_h,
+    out_ref, hin_ref, h1_ref, qkv_ref, obb_ref, xm_ref, gates_ref, zf_h, partner_h,
+    wqkv, wout, wg, wu, wd, ob_s, hid, accl, accr, retl, retc, rety, sendl, sendc, sendy,
+    wsem, zs, zr, zl, ps, pr, gs, gr, xs, xr, *sem_refs,
 ):
     micro, tokens, width = x_ref.shape
     hidden = wg.shape[2]
@@ -265,11 +334,28 @@
     ]
     for load in loads:
         load.start()
-    g = Place(ny)
+    g = Place(ny, nz)
     g.greet()
     gain_a = small_ref[ROUTER_ROWS : ROUTER_ROWS + 1, :].astype(F32)
     gain_m = small_ref[ROUTER_ROWS + 1 : ROUTER_ROWS + 2, :].astype(F32)
     cos, sin = cos_ref[...], sin_ref[...]
+    gather = Gather(g, zf_h, zs, zr, zl)
+    first, last = g.s == 0, g.s == sections - 1
+
+    partner_copy = remote(slices_h, partner_h, ps, pr, g.core)
+    partner_copy.start()
+
+    def cot_copy(r):
+        return remote(cot_h.at[0], zf_h.at[0, 0, r], gs.at[r], gr.at[r], g.behind(r))
+
+    @pl.when(last)
+    def _():
+        for r in range(1, ny):
+            cot_copy(r).start()
+        gather.push(0, 0, cot_h.at[0])
+        for r in range(1, ny):
+            cot_copy(r).wait_recv()
+            gather.push(0, r, zf_h.at[0, 0, r], keep=False)
 
     def hop(m, q):
         here = pl.ds(q * span, span)
@@ -330,13 +416,16 @@
             o6 = dot(shares, v).astype(BF16)
             for i in range(GROUP):
                 head = kv * GROUP + i
-                ob_ref[m, :, head * HEAD : (head + 1) * HEAD] = o6[i * tokens : (i + 1) * tokens]
+                ob_s[:, head * HEAD : (head + 1) * HEAD] = o6[i * tokens : (i + 1) * tokens]
 
         @pl.when(m == 0)
         def _():
             loads[1].wait()
 
-        ob = ob_ref[m]
+        ob = ob_s[...]
+        block = obb_ref.shape[3]
+        for i in range(2 * ny):
+            obb_ref[m, i] = ob[:, i * block : (i + 1) * block]
         for n in range(width // 512):
             cols = slice(n * 512, (n + 1) * 512)
             h1_ref[m, :, cols] = hin_ref[m, :, cols].astype(F32) + dot(ob, wout[:, cols])
@@ -345,6 +434,13 @@
 
         ex = Exchange(g, xm_ref.at[m], retl, retc, rety, sendl, sendc, sendy, Sems(sem_refs, m))
         ex.send_own()
+
+        def complete(r):
+            @pl.when(first & (m == 0))
+            def _():
+                gather.push(0, r, xm_ref.at[0, r, 0])
+
+        complete(0)
 
         @pl.when(m == 0)
         def _():
@@ -391,18 +487,18 @@
 
             def keep(cols, total):
                 accr[:, cols] = total[0:span]
-                sendc[r, here, cols] = total[span:].astype(BF16)
+                sendc[r - 1, here, cols] = total[span:].astype(BF16)
 
             experts(xm_ref[m, r, :, here, :].reshape(2 * span, width), lanes, keep)
             return lambda: accr[...]
 
-        ex.run(local_block, remote_block)
+        ex.run(local_block, remote_block, complete)
         for q in range(CHUNKS):
             here = slice(q * span, (q + 1) * span)
             ex.arrived(q)
             total = h1_ref[m, here, :] + accl[here, :] + retl[here, :].astype(F32)
             for r in range(1, ny):
-                total = total + rety[r, here, :].astype(F32)
+                total = total + rety[r - 1, here, :].astype(F32)
             out_ref[m, here, :] = total.astype(BF16)
 
             @pl.when(g.s < sections - 1)
@@ -413,6 +509,7 @@
         return carry
 
     lax.fori_loop(0, micro, body, 0)
+    partner_copy.wait()
 
     @pl.when(g.s < sections - 1)
     def _():
@@ -420,16 +517,26 @@
             for q in range(CHUNKS):
                 hop(m, q).wait_send()
 
+    @pl.when(first)
+    def _():
+        gather.drain(0)
+
+    @pl.when(last)
+    def _():
+        for r in range(1, ny):
+            cot_copy(r).wait_send()
+        gather.drain(0, keep=False)
+
 
 def backward_kernel(
-    ny, sections,
+    ny, nz, sections,
     cot_ref, segc_ref, segr_ref, small_ref, cos_ref, sin_ref,
     hin_ref, h1_ref, qkv_ref, gates_ref,
     xm_h, wqkv_h, wout_h, wg_h, wu_h, wd_h,
-    gin_ref, grows_ref, xa_ref, dqkv_ref, dattn_ref, gsmall_ref,
+    gin_ref, grows_ref, xab_ref, dqkv_ref, dattn_ref, gsmall_ref, zb_h,
     wqkv, wout, wg, wu, wd, xm_s, hid, act_s, slope_s, da_s, db_s, accl, accr, dh1_s, n_s,
     retl, retc, rety, sendl, sendc, sendy,
-    wsem, xmsem, xs, xr, *sem_refs,
+    wsem, xmsem, zs, zr, zl, xs, xr, *sem_refs,
 ):
     micro, tokens, width = cot_ref.shape
     hidden = wg.shape[2]
@@ -440,12 +547,27 @@
     ]
     for load in loads:
         load.start()
-    g = Place(ny)
+    g = Place(ny, nz)
     g.greet()
     gain_a = small_ref[ROUTER_ROWS : ROUTER_ROWS + 1, :].astype(F32)
     gain_m = small_ref[ROUTER_ROWS + 1 : ROUTER_ROWS + 2, :].astype(F32)
     cos, sin = cos_ref[...], sin_ref[...]
     gsmall_ref[...] = jnp.zeros_like(gsmall_ref)
+    gather = Gather(g, zb_h, zs, zr, zl)
+    first, last = g.s == 0, g.s == sections - 1
+
+    @pl.when(first)
+    def _():
+        for m in range(1, micro):
+            for r in range(ny):
+                gather.push(micro + m, r, xm_h.at[m, r, 0])
+
+    @pl.when(last)
+    def _():
+        for m in range(micro):
+            gather.push(m, 0, xm_h.at[m, 0, 0])
+            for r in range(1, ny):
+                gather.near(m, r, xm_h.at[m, r, 0]).start()
 
     def hop(m, q):
         here = pl.ds(q * span, span)
@@ -466,6 +588,22 @@
 
         ex = Exchange(g, grows_ref.at[m], retl, retc, rety, sendl, sendc, sendy, Sems(sem_refs, m))
         ex.send_own()
+
+        def complete(r):
+            src = grows_ref.at[m, r, 0]
+
+            @pl.when(first)
+            def _():
+                if r == 0:
+                    gather.push(m, 0, src)
+                else:
+                    gather.near(m, r, src).start()
+
+            @pl.when(last & (m > 0))
+            def _():
+                gather.push(micro + m, r, src)
+
+        complete(0)
 
         @pl.when(m == 0)
         def _():
@@ -543,17 +681,17 @@
 
             def keep(cols, total):
                 accr[:, cols] = total[0:span]
-                sendc[r, here, cols] = total[span:].astype(BF16)
+                sendc[r - 1, here, cols] = total[span:].astype(BF16)
 
             experts(grows_ref[m, r, :, here, :].reshape(2 * span, width), r, here, keep)
             return lambda: accr[...]
 
-        ex.run(local_block, remote_block)
+        ex.run(local_block, remote_block, complete)
         for q in range(CHUNKS):
             ex.arrived(q)
         total = accl[...] + retl[...].astype(F32)
         for r in range(1, ny):
-            total = total + rety[r].astype(F32)
+            total = total + rety[r - 1].astype(F32)
         dgates = total[:, width:]
         dgates = dgates + pltpu.roll(dgates, 64, 1)
         gates_t = gates_ref[m, 0, 0]
@@ -583,6 +721,7 @@
             for load in loads[3:]:
                 load.wait()
 
+        gather.pass_on(m)
         bias = mask_bias(segc_ref[m], segr_ref[m])
         bias6 = jnp.concatenate([bias] * GROUP, 0)
         qkv = qkv_ref.at[m]
@@ -617,7 +756,10 @@
         h = hin_ref[m].astype(F32)
         rinv = lax.rsqrt(jnp.mean(h * h, -1, keepdims=True) + EPS)
         n1 = h * rinv
-        xa_ref[m] = (n1 * gain_a).astype(BF16)
+        xa = (n1 * gain_a).astype(BF16)
+        block = xab_ref.shape[3]
+        for i in range(2 * ny):
+            xab_ref[m, i] = xa[:, i * block : (i + 1) * block]
         n_s[...] = n1
         dqkv = dqkv_ref[m]
         for n in range(width // 512):
@@ -646,13 +788,295 @@
             for q in range(CHUNKS):
                 hop(m, q).wait_send()
 
+    for m in range(micro):
+        gather.drain_passed(m)
+    for m in range(1, micro):
+        gather.drain(micro + m)
+
+
+def tail_kernel(
+    ny, nz, sections, span,
+    route_ref, small_ref, gsmall_ref,
+    zf_h, zb_h, slices_h, partner_h, xab_h, obb_h, dqkv_h, dattn_h,
+    gate_ref, up_ref, down_ref, attn_ref, small_out,
+    w4, x_s, g_s, da_s, db_s, gh_s, acc_g, acc_u, acc_d, csend, cland, dsend, dland,
+    xa_s, ob_s, dq_s, dt_s, own_s, ysend, yland, zland, sm_s, smy, smz,
+    wsem, xsem, asem, as_, ar, ss, sr, cs, cr, ts, tr, ys, yr, zs, zr,
+):
+    micro, tokens, width = dqkv_h.shape[0], zf_h.shape[3], zf_h.shape[4]
+    half = slices_h.shape[1]
+    slice_h = half // 2
+    both = 2 * half
+    tile = 256 if both % 256 == 0 else 128
+    qkv_width = dqkv_h.shape[2]
+    shard = width // (2 * ny * nz)
+    part = width // nz
+    rows = span * ny * tokens
+    groups = nz // span
+    g = Place(ny, nz)
+    first = g.s == 0
+    mine = [pltpu.make_async_copy(src, w4.at[:, i * half : (i + 1) * half], wsem.at[i])
+            for i, src in enumerate((slices_h, partner_h))]
+
+    def load(i):
+        m, k = lax.div(i, groups), pl.ds(lax.rem(i, groups) * span, span)
+        early = [(first, x_s, 0), (jnp.logical_not(first), g_s, 1)]
+        late = [(first, g_s, 1), (jnp.logical_not(first), x_s, 0)]
+        copies = [(when, pltpu.make_async_copy(zb_h.at[m, k], dst, xsem.at[n])) for when, dst, n in late]
+        for when, dst, n in early:
+            copies.append((when & (m == 0), pltpu.make_async_copy(zf_h.at[0, k], dst, xsem.at[n])))
+            copies.append((when & (m > 0), pltpu.make_async_copy(zb_h.at[micro + m, k], dst, xsem.at[n])))
+        return copies
+
+    def start_load(i):
+        for when, copy in load(i):
+            @pl.when(when)
+            def _():
+                copy.start()
+
+    def wait_load():
+        pltpu.make_async_copy(zf_h.at[0, pl.ds(0, span)], x_s, xsem.at[0]).wait()
+        pltpu.make_async_copy(zf_h.at[0, pl.ds(0, span)], g_s, xsem.at[1]).wait()
+
+    for copy in mine:
+        copy.start()
+    start_load(0)
+    g.greet(with_x=False)
+
+    away, here = [], []
+    for m in range(micro):
+        for yy in range(ny):
+            other = yy * 2 + 1 - g.c
+            own = yy * 2 + g.c
+            for n, (src, dst) in enumerate(((xab_h, xa_s), (obb_h, ob_s))):
+                i = (m * ny + yy) * 2 + n
+                away.append(remote(src.at[m, other], dst.at[yy, 1, m], as_.at[i], ar.at[i], g.core))
+                here.append(pltpu.make_async_copy(src.at[m, own], dst.at[yy, 0, m], asem.at[i]))
+    base = 2 * ny * micro
+    for n, (src, dst) in enumerate(((dqkv_h, dq_s), (dattn_h, dt_s))):
+        i = base + n
+        away.append(remote(src, dst.at[1], as_.at[i], ar.at[i], g.core))
+        here.append(pltpu.make_async_copy(src, dst.at[0], asem.at[i]))
+    for copy in away + here:
+        copy.start()
+    sm_core = remote(gsmall_ref, sm_s.at[1], ss.at[0], sr.at[0], g.core)
+    sm_core.start()
+
+    def sm_y(r):
+        return remote(sm_s.at[0], smy.at[ny - r], ss.at[r], sr.at[ny - r], g.ahead(r))
+
+    def sm_y_arrival(r):
+        return remote(sm_s.at[0], smy.at[r], ss.at[r], sr.at[r], g.ahead(r))
+
+    def sm_z(k):
+        return remote(sm_s.at[1], smz.at[k], ss.at[ny + k], sr.at[ny + k], g.z_behind(k))
+
+    for copy in away:
+        copy.wait_recv()
+    for copy in here:
+        copy.wait()
+
+    count = 2 * micro * tokens
+
+    def attn_rows(yy, dst):
+        for src, grad, at in ((xa_s, dq_s, 0), (ob_s, dt_s, qkv_width)):
+            left = src[yy].reshape(count, shard * nz)
+            wide = grad.shape[3]
+            for n in range(wide // 512):
+                cols = slice(n * 512, (n + 1) * 512)
+                got = dot_tn(left, grad[:, :, :, cols].reshape(count, 512)).astype(BF16)
+                for zi in range(nz):
+                    dst[zi, 0:shard, at + n * 512 : at + (n + 1) * 512] = got[zi * shard : (zi + 1) * shard]
+
+    def y_copy(r, k):
+        zi = g.z_of(k)
+        return remote(ysend.at[r - 1, zi], yland.at[ny - r - 1, zi], ys.at[r, k], yr.at[ny - r, k], g.ahead(r))
+
+    def y_arrival(r, k):
+        zi = g.z_of(k)
+        return remote(ysend.at[r - 1, zi], yland.at[r - 1, zi], ys.at[r, k], yr.at[r, k], g.ahead(r))
+
+    order = list(range(1, nz)) + [0]
+    for r in range(1, ny):
+        attn_rows(lax.rem(g.y + r, ny), ysend.at[r - 1])
+    for k in order:
+        for r in range(1, ny):
+            y_copy(r, k).start()
+    sm_core.wait_recv()
+    sm_s[0] = gsmall_ref[...] + sm_s[1]
+    sm_core.wait_send()
+    for r in range(1, ny):
+        sm_y(r).start()
+    attn_rows(g.y, own_s)
+
+    def z_copy(k):
+        return remote(own_s.at[g.z_of(k)], zland.at[nz - k - 1], zs.at[0, k], zr.at[0, nz - k], g.z_ahead(k))
+
+    def z_arrival(k):
+        return remote(own_s.at[g.d], zland.at[k - 1], zs.at[0, k], zr.at[0, k], g.z_ahead(k))
+
+    def attn_sum(k):
+        for r in range(1, ny):
+            y_arrival(r, k).wait_recv()
+        zi = g.z_of(k)
+        total = own_s[zi].astype(F32)
+        for r in range(1, ny):
+            total = total + yland[r - 1, zi].astype(F32)
+        own_s[zi] = total.astype(BF16)
+        if k:
+            z_copy(k).start()
+
+    for copy in mine:
+        copy.wait()
+    acc_g[...] = jnp.zeros_like(acc_g)
+    acc_u[...] = jnp.zeros_like(acc_u)
+    acc_d[...] = jnp.zeros_like(acc_d)
+    column = lax.broadcasted_iota(jnp.int32, (ROUTER_ROWS, both), 1)
+    expert = lax.broadcasted_iota(jnp.int32, (ROUTER_ROWS, both), 0)
+    owner = jnp.where(column < half, g.e, 2 * g.y + 1 - g.c)
+    local = jnp.where(column < half, column, column - half)
+    chosen = 2 * owner + jnp.where(local < slice_h, 0, 1)
+    spread = jnp.where(expert == chosen, 1.0, 0.0).astype(BF16)
+
+    def group(i, carry):
+        m = lax.div(i, groups)
+        wait_load()
+
+        def block(b, carry):
+            k = lax.rem(i, groups) * span + lax.div(b, ny)
+            r = lax.rem(b, ny)
+            place = (lax.rem(g.y + r, ny) * 2 + g.c) * nz + g.z_of(k)
+            x = x_s[lax.div(b, ny), r]
+            gr = g_s[lax.div(b, ny), r]
+            gates_t = chosen_gates(dot_nt(small_ref[0:ROUTER_ROWS, :], x), route_ref[place, m])
+            high = gates_t.astype(BF16)
+            low = (gates_t - high.astype(F32)).astype(BF16)
+            here = pl.ds(pl.multiple_of(b * tokens, tokens), tokens)
+            for n in range(both // tile):
+                cols = slice(n * tile, (n + 1) * tile)
+                a = dot_nt(x, w4[0, cols])
+                bb = dot_nt(x, w4[1, cols])
+                gate = dot_tn(high, spread[:, cols]) + dot_tn(low, spread[:, cols])
+                u = dot_nt(gr, w4[2, cols]) * gate
+                square = a * a
+                th = jnp.tanh(GELU_C * (a + GELU_A * square * a))
+                hf = 0.5 * (1.0 + th)
+                act = a * hf
+                slope = hf + (0.5 * GELU_C) * a * (1.0 - th * th) * (1.0 + (3.0 * GELU_A) * square)
+                da_s[here, cols] = (u * slope * bb).astype(BF16)
+                db_s[here, cols] = (u * act).astype(BF16)
+                gh_s[here, cols] = ((act * bb).astype(BF16).astype(F32) * gate).astype(BF16)
+            return carry
+
+        lax.fori_loop(0, span * ny, block, 0)
+
+        def columns(n, carry):
+            cols = pl.ds(pl.multiple_of(n * 256, 256), 256)
+            x = x_s[:, :, :, cols].reshape(rows, 256)
+            acc_g[cols, :] += dot_tn(x, da_s[...])
+            acc_u[cols, :] += dot_tn(x, db_s[...])
+            acc_d[:, cols] += dot_tn(gh_s[...], g_s[:, :, :, cols].reshape(rows, 256))
+            return carry
+
+        lax.fori_loop(0, width // 256, columns, 0)
+
+        @pl.when(i + 1 < micro * groups)
+        def _():
+            start_load(i + 1)
+
+        return carry
+
+    lax.fori_loop(0, micro * groups, group, 0)
+
+    def core_copy(n, k):
+        return remote(csend.at[n, k], cland.at[n, k], cs.at[n, k], cr.at[n, k], g.core)
+
+    def turn_copy(n, k):
+        dst = (gate_ref, up_ref)[n]
+        return remote(cland.at[n, k], dst.at[g.d], ts.at[n, k], tr.at[n, k], g.z_ahead(k))
+
+    def turn_near(n):
+        return pltpu.make_async_copy(cland.at[n, 0], (gate_ref, up_ref)[n].at[g.d], ts.at[n, 0])
+
+    def turn_arrival(n, k):
+        dst = (gate_ref, up_ref)[n]
+        return remote(cland.at[n, k], dst.at[g.z_of(nz - k)], ts.at[n, k], tr.at[n, k], g.z_behind(k))
+
+    def width_rows(k):
+        return pl.ds(pl.multiple_of(g.z_of(k) * part, part), part)
+
+    down_copy = remote(dsend, dland, cs.at[2, 0], cr.at[2, 0], g.core)
+    accs = (acc_g, acc_u)
+    for n in range(2):
+        for k in order:
+            csend[n, k] = accs[n][width_rows(k), half:both].astype(BF16)
+            core_copy(n, k).start()
+    dsend[...] = acc_d[half:both, :].astype(BF16)
+    down_copy.start()
+    for k in order[:-1]:
+        attn_sum(k)
+        for n in range(2):
+            core_copy(n, k).wait_recv()
+            total = accs[n][width_rows(k), 0:half] + cland[n, k].astype(F32)
+            cland[n, k] = total.astype(BF16)
+            turn_copy(n, k).start()
+    for n in range(2):
+        core_copy(n, 0).wait_recv()
+        cland[n, 0] = (accs[n][width_rows(0), 0:half] + cland[n, 0].astype(F32)).astype(BF16)
+        turn_near(n).start()
+    down_copy.wait_recv()
+    down_ref[...] = (acc_d[0:half, :] + dland[...].astype(F32)).astype(BF16)
+    attn_sum(0)
+
+    for r in range(1, ny):
+        sm_y_arrival(r).wait_recv()
+    total = sm_s[0]
+    for r in range(1, ny):
+        total = total + smy[r]
+    sm_s[1] = total
+    for k in range(1, nz):
+        sm_z(k).start()
+    for k in range(1, nz):
+        sm_z(k).wait_recv()
+        total = total + smz[k]
+    small_out[...] = total
+
+    for k in range(1, nz):
+        z_arrival(k).wait_recv()
+    total = own_s[g.d].astype(F32)
+    for k in range(1, nz):
+        total = total + zland[k - 1].astype(F32)
+    attn_ref[...] = total
+    for k in range(1, nz):
+        for n in range(2):
+            turn_arrival(n, k).wait_recv()
+
+    for copy in away:
+        copy.wait_send()
+    for r in range(1, ny):
+        sm_y(r).wait_send()
+        for k in range(nz):
+            y_copy(r, k).wait_send()
+    for k in range(1, nz):
+        sm_z(k).wait_send()
+        z_copy(k).wait_send()
+        for n in range(2):
+            turn_copy(n, k).wait_send()
+    for n in range(2):
+        for k in range(nz):
+            core_copy(n, k).wait_send()
+    down_copy.wait_send()
+    for n in range(2):
+        turn_near(n).wait()
+
 
 VMEM = pl.BlockSpec(memory_space=pltpu.VMEM)
 ANY = pl.BlockSpec(memory_space=pl.ANY)
+DMA = pltpu.SemaphoreType.DMA
 
 
 def per_device(
-    ne, sections,
+    ne, nz, sections,
     layer_input, cotangent, segments, routes, attn_gain, w_qkv, w_out, moe_gain, w_router, w_gate, w_up, w_down,
 ):
     ny = ne // 2
@@ -661,6 +1085,7 @@
     hidden = w_gate.shape[3]
     owners = ("expert", "dp")
     shard = w_qkv.shape[1]
+    place_e, place_d = lax.axis_index("expert"), lax.axis_index("dp")
     small = jnp.concatenate(
         [
             jnp.pad(w_router[0], ((0, 0), (0, ROUTER_ROWS - total_experts))),
@@ -673,7 +1098,10 @@
     small = lax.all_gather(small, owners, axis=0, tiled=True).T
     wqkv = lax.all_gather(w_qkv[0], owners, axis=0, tiled=True)
     wout = lax.all_gather(w_out[0], owners, axis=0, tiled=True)
-    route = lax.all_gather(jnp.transpose(routes[0, :, 0], (0, 2, 1)), "expert", axis=0)
+    routes_all = lax.all_gather(jnp.transpose(routes[0, :, 0], (0, 2, 1)), owners, axis=0)
+    route = lax.dynamic_index_in_dim(
+        routes_all.reshape((ne, nz) + routes_all.shape[1:]), place_d, 1, keepdims=False
+    )
     cos, sin = rotary_tables(tokens)
     segs = segments[:, 0]
     segc, segr = segs[:, :, None], segs[:, None, :]
@@ -682,75 +1110,87 @@
     wg, wu, wd = w_gate[0], w_up[0], w_down[0]
     span = tokens // CHUNKS
     qkv_width = wqkv.shape[1]
+    slice_h = hidden // nz
+    half = 2 * slice_h
+    at = place_d * slice_h
+    slices = jnp.stack(
+        [
+            jnp.swapaxes(lax.dynamic_slice_in_dim(wg, at, slice_h, 2), 1, 2).reshape(half, width),
+            jnp.swapaxes(lax.dynamic_slice_in_dim(wu, at, slice_h, 2), 1, 2).reshape(half, width),
+            lax.dynamic_slice_in_dim(wd, at, slice_h, 1).reshape(half, width),
+        ]
+    )
 
     def shape(*dims, dtype=BF16):
         return jax.ShapeDtypeStruct(dims, dtype)
 
-    weight_scratch = {
-        "wqkv": pltpu.VMEM(wqkv.shape, BF16),
-        "wout": pltpu.VMEM(wout.shape, BF16),
-        "wg": pltpu.VMEM(wg.shape, BF16),
-        "wu": pltpu.VMEM(wu.shape, BF16),
-        "wd": pltpu.VMEM(wd.shape, BF16),
-    }
-    order = ("wqkv", "wout", "wg", "wu", "wd")
-    hop_sems = [pltpu.SemaphoreType.DMA((micro, CHUNKS)) for _ in range(2)]
+    weights = [pltpu.VMEM(w.shape, BF16) for w in (wqkv, wout, wg, wu, wd)]
+    hop_sems = [DMA((micro, CHUNKS)) for _ in range(2)]
+    block = width // ne
+
+    def gather_sems(count):
+        return [DMA((count, nz, ny)), DMA((count, nz, ny)), DMA((count, ny))]
 
     def returns(wide):
         return [
             pltpu.VMEM((tokens, wide), BF16),
-            pltpu.VMEM((ny, tokens, wide), BF16),
-            pltpu.VMEM((ny, tokens, wide), BF16),
+            pltpu.VMEM((max(1, ny - 1), tokens, wide), BF16),
+            pltpu.VMEM((max(1, ny - 1), tokens, wide), BF16),
             pltpu.VMEM((tokens, wide), BF16),
-            pltpu.VMEM((ny, tokens, wide), BF16),
-            pltpu.VMEM((ny, tokens, wide), BF16),
+            pltpu.VMEM((max(1, ny - 1), tokens, wide), BF16),
+            pltpu.VMEM((max(1, ny - 1), tokens, wide), BF16),
         ]
 
-    out, hin, h1, qkv, ob, xm, gates = pl.pallas_call(
-        functools.partial(forward_kernel, ny, sections),
+    out, hin, h1, qkv, obb, xm, gates, zf, partner = pl.pallas_call(
+        functools.partial(forward_kernel, ny, nz, sections),
         out_shape=(
             shape(micro, tokens, width),
             shape(micro, tokens, width),
             shape(micro, tokens, width, dtype=F32),
             shape(micro, tokens, qkv_width),
-            shape(micro, tokens, width),
+            shape(micro, ne, tokens, block),
             shape(micro, ny, 2, tokens, width),
             shape(micro, ny, 2, ROUTER_ROWS, tokens, dtype=F32),
+            shape(1, nz, ny, tokens, width),
+            shape(3, half, width),
         ),
-        in_specs=[VMEM] * 7 + [ANY] * 5,
-        out_specs=tuple([VMEM] * 7),
-        scratch_shapes=[weight_scratch[name] for name in order]
+        in_specs=[VMEM] * 7 + [ANY] * 7,
+        out_specs=tuple([VMEM] * 7 + [ANY] * 2),
+        scratch_shapes=weights
         + [
+            pltpu.VMEM((tokens, width), BF16),
             pltpu.VMEM((2, 2 * tokens, hidden), BF16),
             pltpu.VMEM((tokens, width), F32),
             pltpu.VMEM((span, width), F32),
-            pltpu.VMEM((8, 128), F32),
         ]
         + returns(width)
-        + [pltpu.SemaphoreType.DMA((5,))]
+        + [DMA((5,))]
+        + gather_sems(1)
+        + [DMA, DMA, DMA((ny,)), DMA((ny,))]
         + hop_sems
         + sem_shapes(micro, ny),
         compiler_params=pltpu.CompilerParams(
             collective_id=0, has_side_effects=True, vmem_limit_bytes=60 * 2**20
         ),
         name="layers_forward",
-    )(x, segc, segr, route, small, cos, sin, wqkv, wout, wg, wu, wd)
+    )(x, segc, segr, route, small, cos, sin, cot, slices, wqkv, wout, wg, wu, wd)
 
     wide = width + 128
     every = (2, ny, 2, tokens, hidden)
-    gin, grows, xa, dqkv, dattn, gsmall = pl.pallas_call(
-        functools.partial(backward_kernel, ny, sections),
+    gin, grows, xab, dqkv, dattn, gsmall, zb = pl.pallas_call(
+        functools.partial(backward_kernel, ny, nz, sections),
         out_shape=(
             shape(micro, tokens, width),
             shape(micro, ny, 2, tokens, width),
-            shape(micro, tokens, width),
+            shape(micro, ne, tokens, block),
             shape(micro, tokens, qkv_width),
             shape(micro, tokens, width),
             shape(SMALL_ROWS, width, dtype=F32),
+            shape(2 * micro, nz, ny, tokens, width),
         ),
         in_specs=[VMEM] * 10 + [ANY] * 6,
-        out_specs=tuple([VMEM] * 6),
-        scratch_shapes=[weight_scratch[name] for name in order]
+        out_specs=tuple([VMEM] * 6 + [ANY]),
+        scratch_shapes=weights
         + [
             pltpu.VMEM((ny, 2, tokens, width), BF16),
             pltpu.VMEM(every, BF16),
@@ -764,7 +1204,8 @@
             pltpu.VMEM((tokens, width), F32),
         ]
         + returns(wide)
-        + [pltpu.SemaphoreType.DMA((5,)), pltpu.SemaphoreType.DMA]
+        + [DMA((5,)), DMA]
+        + gather_sems(2 * micro)
         + hop_sems
         + sem_shapes(micro, ny),
         compiler_params=pltpu.CompilerParams(
@@ -773,52 +1214,85 @@
         name="layers_backward",
     )(cot, segc, segr, small, cos, sin, hin, h1, qkv, gates, xm, wqkv, wout, wg, wu, wd)
 
-    e = lax.axis_index("expert")
-    packs = micro * ny * 2
-    rows = xm.reshape(packs * tokens, width)
-    grads = grows.reshape(packs * tokens, width)
-    own = lax.dynamic_slice_in_dim(gates, 2 * e, 2, 3)
-    own = jnp.transpose(own, (3, 0, 1, 2, 4)).reshape(2, packs * tokens, 1)
-    a = jnp.einsum("td,jdh->jth", rows, wg, preferred_element_type=F32)
-    b = jnp.einsum("td,jdh->jth", rows, wu, preferred_element_type=F32)
-    u = own * jnp.einsum("td,jhd->jth", grads, wd, preferred_element_type=F32)
-    th = jnp.tanh(GELU_C * (a + GELU_A * a * a * a))
-    half = 0.5 * (1.0 + th)
-    act = a * half
-    slope = half + (0.5 * GELU_C) * a * (1.0 - th * th) * (1.0 + (3.0 * GELU_A) * a * a)
-    da = (u * b * slope).astype(BF16)
-    db = (u * act).astype(BF16)
-    gh = (own * act * b).astype(BF16)
-    grad_gate = jnp.einsum("td,jth->jdh", rows, da, preferred_element_type=F32)
-    grad_up = jnp.einsum("td,jth->jdh", rows, db, preferred_element_type=F32)
-    grad_down = jnp.einsum("jth,td->jhd", gh, grads, preferred_element_type=F32)
-
-    def over_dp(value):
-        return lax.psum_scatter(value.astype(BF16), "dp", scatter_dimension=1, tiled=True).astype(F32)
-
-    grad_qkv = jnp.einsum("mtd,mte->de", xa, dqkv, preferred_element_type=F32).astype(BF16)
-    grad_out = jnp.einsum("mtd,mte->de", ob, dattn, preferred_element_type=F32).astype(BF16)
-    grad_qkv = lax.psum_scatter(grad_qkv, owners, scatter_dimension=0, tiled=True).astype(F32)
-    grad_out = lax.psum_scatter(grad_out, owners, scatter_dimension=0, tiled=True).astype(F32)
-    grad_small = lax.psum_scatter(gsmall.T, owners, scatter_dimension=0, tiled=True)
+    span_z = max(1, min(nz, 1024 // (ny * tokens)))
+    rows = span_z * ny * tokens
+    padded = -(-shard // 16) * 16
+    attn_width = qkv_width + width
+    part = width // nz
+    small_shape = (SMALL_ROWS, width)
+    gate_g, up_g, down_g, attn_g, small_g = pl.pallas_call(
+        functools.partial(tail_kernel, ny, nz, sections, span_z),
+        out_shape=(
+            shape(nz, part, half),
+            shape(nz, part, half),
+            shape(half, width),
+            shape(padded, attn_width, dtype=F32),
+            shape(*small_shape, dtype=F32),
+        ),
+        in_specs=[VMEM] * 3 + [ANY] * 8,
+        out_specs=tuple([ANY] * 2 + [VMEM] * 3),
+        scratch_shapes=[
+            pltpu.VMEM((3, 2 * half, width), BF16),
+            pltpu.VMEM((span_z, ny, tokens, width), BF16),
+            pltpu.VMEM((span_z, ny, tokens, width), BF16),
+            pltpu.VMEM((rows, 2 * half), BF16),
+            pltpu.VMEM((rows, 2 * half), BF16),
+            pltpu.VMEM((rows, 2 * half), BF16),
+            pltpu.VMEM((width, 2 * half), F32),
+            pltpu.VMEM((width, 2 * half), F32),
+            pltpu.VMEM((2 * half, width), F32),
+            pltpu.VMEM((2, nz, part, half), BF16),
+            pltpu.VMEM((2, nz, part, half), BF16),
+            pltpu.VMEM((half, width), BF16),
+            pltpu.VMEM((half, width), BF16),
+            pltpu.VMEM((ny, 2, micro, tokens, block), BF16),
+            pltpu.VMEM((ny, 2, micro, tokens, block), BF16),
+            pltpu.VMEM((2, micro, tokens, qkv_width), BF16),
+            pltpu.VMEM((2, micro, tokens, width), BF16),
+            pltpu.VMEM((nz, padded, attn_width), BF16),
+            pltpu.VMEM((max(1, ny - 1), nz, padded, attn_width), BF16),
+            pltpu.VMEM((max(1, ny - 1), nz, padded, attn_width), BF16),
+            pltpu.VMEM((max(1, nz - 1), padded, attn_width), BF16),
+            pltpu.VMEM((2,) + small_shape, F32),
+            pltpu.VMEM((ny,) + small_shape, F32),
+            pltpu.VMEM((nz,) + small_shape, F32),
+            DMA((2,)), DMA((2,)),
+            DMA((2 * ny * micro + 2,)), DMA((2 * ny * micro + 2,)), DMA((2 * ny * micro + 2,)),
+            DMA((ny + nz,)), DMA((ny + nz,)),
+            DMA((3, nz)), DMA((3, nz)),
+            DMA((2, nz)), DMA((2, nz)),
+            DMA((ny, nz)), DMA((ny, nz)),
+            DMA((1, nz)), DMA((1, nz)),
+        ],
+        compiler_params=pltpu.CompilerParams(
+            collective_id=2, has_side_effects=True, vmem_limit_bytes=62 * 2**20
+        ),
+        name="weight_gradients",
+    )(routes_all, small, gsmall, zf, zb, slices, partner, xab, obb, dqkv, dattn)
+
+    def unturned(value):
+        value = value.reshape(nz, part, 2, slice_h)
+        return jnp.transpose(value, (2, 1, 0, 3)).reshape(1, 2, part, hidden).astype(F32)
+
+    mine = lax.dynamic_slice_in_dim(small_g, (place_e * nz + place_d) * shard, shard, 1)
     return (
         out[None, :, None],
         gin[None, :, None],
-        grad_small[:, ROUTER_ROWS][None],
-        grad_qkv[None],
-        grad_out[None],
-        grad_small[:, ROUTER_ROWS + 1][None],
-        grad_small[:, 0:total_experts][None],
-        over_dp(grad_gate)[None],
-        over_dp(grad_up)[None],
-        over_dp(grad_down)[None],
+        mine[ROUTER_ROWS][None],
+        attn_g[None, 0:shard, 0:qkv_width],
+        attn_g[None, 0:shard, qkv_width:],
+        mine[ROUTER_ROWS + 1][None],
+        mine[0:total_experts].T[None],
+        unturned(gate_g),
+        unturned(up_g),
+        down_g.reshape(1, 2, slice_h, width).astype(F32),
     )
 
 
 def solution(mesh):
     owners = ("expert", "dp")
     return jax.shard_map(
-        functools.partial(per_device, mesh.shape["expert"], mesh.shape["section"]),
+        functools.partial(per_device, mesh.shape["expert"], mesh.shape["dp"], mesh.shape["section"]),
         mesh=mesh,
         in_specs=(
             P(None, owners, None, None),

time: 862 us -> 637 us (0.74)
  waiting for transfers between devices: 437 us -> 45.1 us
  Pallas kernels: 223 us -> 475 us
  matrix products: 61.8 us -> 0 us
  local copies, waits for them, and re-layouts: 66.2 us -> 29.9 us
  blocking collectives: 41.5 us -> 65 us
    pallas_call x2 -> x3, Pallas kernels: 223 us -> 475 us  [the longest x1 203 us: per_device(): pl.pallas_call(functools.partial(tail_kernel, ny, nz, sections, span_z),...]
    reduce_scatter x3 -> x0, waiting for transfers between devices: 194 us -> none  [the longest x1 86.7 us: per_device(): lax.psum_scatter(grad_qkv, owners, scatter_dimension=0, tiled=True)]
    unnamed x11 -> x2, waiting for transfers between devices: 167 us -> 1.38 us
    dot_general x8 -> x0, matrix products: 61.8 us -> none  [the longest x1 12.4 us: per_device(): grad_gate = jnp.einsum('td,jth->jdh', rows, da, preferred_element_type=F32)]
    unnamed x43 -> x33, local copies, waits for them, and re-layouts: 62.8 us -> 11.8 us
    all_gather x1, blocking collectives: 5.85 us -> 29.4 us  [per_device(): lax.all_gather(jnp.transpose(routes[0, :, 0], (0, 2, 1)), owners, axis=0)]
    all_gather x1, waiting for transfers between devices: 62.7 us -> 43.7 us  [per_device(): wqkv = lax.all_gather(w_qkv[0], owners, axis=0, tiled=True)]
    all_gather x1, waiting for transfers between devices: 13.8 us -> 0.01 us  [per_device(): wout = lax.all_gather(w_out[0], owners, axis=0, tiled=True)]
  transfers between devices with their start and end apart: 8 -> 2, of which waited for: 7 -> 1; matrix products, arithmetic and copies ran while one was open for 15% -> 2% of each run, Pallas kernels for 0% -> 0%
where the time goes in v2:
time: 637 us; the launch traced here: 633 us
  Pallas kernels  475 us (75%)
  blocking collectives  65 us (10%)
  waiting for transfers between devices  45.1 us (7%)
  local copies, waits for them, and re-layouts  29.9 us (5%)
  between operations  14.4 us (2%)
    pallas_call x1, Pallas kernels, per_device(): pl.pallas_call(functools.partial(tail_kernel, ny, nz, sections, span_z),...  203 us
    pallas_call x1, Pallas kernels, per_device(): pl.pallas_call(functools.partial(backward_kernel, ny, nz, sections), out_...  190 us
    pallas_call x1, Pallas kernels, per_device(): pl.pallas_call(functools.partial(forward_kernel, ny, nz, sections), out_s...  81.5 us
    all_gather x1, waiting for transfers between devices, per_device(): wqkv = lax.all_gather(w_qkv[0], owners, axis=0, tiled=True)  43.7 us
    all_gather x1, blocking collectives, per_device(): small = lax.all_gather(small, owners, axis=0, tiled=True).T  35.6 us
    all_gather x1, blocking collectives, per_device(): lax.all_gather(jnp.transpose(routes[0, :, 0], (0, 2, 1)), owners, axis=0)  29.4 us
  transfers between devices with their start and end apart: 2, of which 1 were waited for; matrix products, arithmetic and copies ran while one was open for 2% of the time, Pallas kernels for 0%

profile of v2, /device:TPU:0, one launch (start us, length us, event | category | flops | bytes accessed | tf_op | source)
XLA Modules:
  0.0 633.1 jit_solution(3519252268186323192)
XLA Ops:
  7.2 0.7 all-gather.9.cloned.1.call-update
  8.0 0.7 all-gather.7.cloned.1.call-update
  8.7 4.0 constant_dynamic-slice_fusion.1
  12.7 1.5 copy.59
  14.2 1.5 copy.60
  15.6 0.1 pad.11.clone
  15.7 0.1 fusion.4
  15.8 35.6 %all-gather.3 = bf16[16,96,32]{1,2,0:T(8,128)(2,1)S(1)} all-gather(bf16[1,96,32]{1,2,0:T(8,128)(2,1)S(1)} %fusion.4), channel_id=1, replica_groups=mesh['section'=2,'expert'=4,'dp'=4] {'expert','dp'}, dimensions={0}, use_global_device_ids=true | all-gather | bytes 104448 | tf_op jit(solution)/shard_map/all_gather | solution.py:1098
  51.5 0.1 copy.45
  51.5 0.8 reshape.89
  52.3 0.8 copy.48.segc_ref
  53.1 29.4 %all-gather = s32[32,4,128]{2,1,0:T(4,128)S(1)} all-gather(s32[2,4,128]{2,1,0:T(4,128)S(1)} %bitcast.89), channel_id=2, replica_groups=mesh['section'=2,'expert'=4,'dp'=4] {'expert','dp'}, dimensions={0}, use_global_device_ids=true | all-gather | bytes 69632 | tf_op jit(solution)/shard_map/all_gather | solution.py:1101
  82.5 0.6 dynamic-slice_bitcast_fusion.route_ref
  83.1 1.3 constant_dynamic-slice_fusion
  84.5 2.0 pad_maximum_fusion.slices_h
  86.5 43.7 %all-gather.7.cloned.1.call-done = bf16[1,1536,2048]{2,1,0:T(8,128)(2,1)} async-done(((bf16[1,96,2048]{2,1,0:T(8,128)(2,1)}), bf16[1,1536,2048]{2,1,0:T(8,128)(2,1)}) %all-gather.7.cloned.1.call-update) | async-done | bytes 6291472 | tf_op jit(solution)/shard_map/all_gather | solution.py:1099
  130.2 81.5 %layers_forward.1 = (bf16[2,128,1536]{2,1,0:T(8,128)(2,1)}, bf16[2,128,1536]{2,1,0:T(8,128)(2,1)}, f32[2,128,1536]{2,1,0:T(8,128)}, bf16[2,128,2048]{2,1,0:T(8,1...) custom-call(bf16[2,128,1536]{2,1,0:T(8,128)(2,1)} %bitcast.85, ...), custom_call_target="tpu_custom_call" | custom-call | tf_op jit(solution)/shard_map/layers_forward/pallas_call | solution.py:1144
  211.7 190.5 %layers_backward.1 = (bf16[2,128,1536]{2,1,0:T(8,128)(2,1)}, bf16[2,2,2,128,1536]{4,3,2,1,0:T(8,128)(2,1)}, bf16[2,4,128,384]{3,2,1,0:T(8,128)(2,1)}, bf16[2,128...) custom-call(bf16[2,128,1536]{2,1,0:T(8,128)(2,1)} %bitcast.78, ...), custom_call_target="tpu_custom_call" | custom-call | tf_op jit(solution)/shard_map/layers_backward/pallas_call | solution.py:1180
  402.2 202.9 %weight_gradients.1 = (bf16[4,384,384]{2,1,0:T(8,128)(2,1)}, bf16[4,384,384]{2,1,0:T(8,128)(2,1)}, bf16[384,1536]{1,0:T(8,128)(2,1)}, f32[96,3584]{1,0:T(8,128)}, f32[32,1536]{1,0:T(8,128)}) custom-call(s32[16,2,4,128]{3,2,1,0:T(4,128)} %bitcast.87, bf16[32,1536]{1,0:T(8,128)(2,1)} %bitcast.81, f32[32,1536]{1,0:T(8,128)} %get-tuple-element.37.gsmall_ref, ...), custom_call_target="tpu_custom_call" | custom-call | tf_op jit(solution)/shard_map/weight_gradients/pallas_call | solution.py:1223
  605.1 2.2 slice_bitcast_fusion
  607.3 1.9 slice_bitcast_fusion.1
  609.2 0.6 copy.50
  609.8 1.6 copy.51
  611.4 3.1 copy.56
  614.6 0.6 copy.52
  615.2 1.6 copy.53
  616.8 3.1 copy.57
  619.9 1.7 convert.7
  621.6 1.4 dynamic-slice_bitcast_fusion.1
  623.0 1.4 fusion.5
  624.3 0.9 copy.63
  625.2 0.9 copy.64
  (30 shorter events, 0.1 us)
Async XLA Ops:
  7.2 79.4 %all-gather.9.cloned.1.call-start = ((), (), s32[]{:S(2)}) async-start(), calls=%async_computation.1 | async-start | bytes 5013504 | tf_op jit(solution)/shard_map/all_gather | solution.py:1100
  7.9 122.3 %all-gather.7.cloned.1.call-start = ((), (), s32[]{:S(2)}) async-start(), calls=%async_computation | async-start | bytes 6684672 | tf_op jit(solution)/shard_map/all_gather | solution.py:1099
  12.7 3.1 copy-start.10
  12.7 3.1 copy-start.11
  12.7 3.0 copy-start.12
  14.2 38.1 %copy-start.8 = (s32[2,1,128]{2,1,0:T(1,128)S(1)}, s32[2,1,128]{2,1,0:T(1,128)}, u32[]{:S(2)}) copy-start(s32[2,1,128]{2,1,0:T(1,128)} %segr_ref.3) | copy-start | bytes 3076
  14.2 39.0 %copy-start.9 = (s32[1,2,1,128,4]{3,4,2,1,0:T(4,128)S(1)}, s32[1,2,1,128,4]{3,4,2,1,0:T(4,128)}, u32[]{:S(2)}) copy-start(s32[1,2,1,128,4]{3,4,2,1,0:T(4,128)} %param.17) | copy-start | bytes 12292
  14.2 70.3 %copy-start = (bf16[1,2,1536,192]{2,3,1,0:T(8,128)(2,1)S(1)}, bf16[1,2,1536,192]{2,3,1,0:T(8,128)(2,1)}, u32[]{:S(2)}) copy-start(bf16[1,2,1536,192]{2,3,1,0:T(8,128)(2,1)} %copy.59) | copy-start | bytes 3538948
  15.6 68.9 %copy-start.1 = (bf16[1,2,1536,192]{2,3,1,0:T(8,128)(2,1)S(1)}, bf16[1,2,1536,192]{2,3,1,0:T(8,128)(2,1)}, u32[]{:S(2)}) copy-start(bf16[1,2,1536,192]{2,3,1,0:T(8,128)(2,1)} %copy.60) | copy-start | bytes 3538948
  82.5 4.0 copy-start.7
  605.1 4.1 copy-start.4
  611.4 3.1 copy-start.3
  616.8 3.1 copy-start.2
  619.9 4.4 copy-start.5
  619.9 5.3 copy-start.6
Sparse Core Ops, SparseCore 0:
  10.3 57.0 all-gather.8
  69.7 60.5 all-gather.6

commit v3 on v2

--- a/solution.py
+++ b/solution.py
@@ -18,7 +18,9 @@
 SCALE = HEAD ** (-0.5)
 ROUTER_ROWS = 16
 SMALL_ROWS = 32
-CHUNKS = 2
+FORWARD_CHUNKS = 2
+BACKWARD_CHUNKS = 1
+HOP_CHUNKS = 2
 MESH = pl.DeviceIdType.MESH
 F32 = jnp.float32
 BF16 = jnp.bfloat16
@@ -116,67 +118,130 @@
     )
 
 
+class Line:
+    def __init__(self, place, slot, send, recv):
+        self.place, self.slot, self.send, self.recv = place, slot, send, recv
+
+    def origin(self, way, h):
+        return self.place.d - h if way == 0 else self.place.d + h
+
+    def comes(self, way, h):
+        return self.place.d >= h if way == 0 else self.place.d + h < self.place.nz
+
+    def leaves(self, way, h):
+        d, nz = self.place.d, self.place.nz
+        return (d + 1 < nz) & (d >= h - 1) if way == 0 else (d >= 1) & (d + h - 1 < nz)
+
+    def out(self, way, h, src=None):
+        g = self.place
+        at = self.slot(self.origin(way, h - 1))
+        next_door = (g.s, g.e, g.d + 1 if way == 0 else g.d - 1)
+        return remote(at if src is None else src, at, self.send.at[way, h], self.recv.at[way, h], next_door)
+
+    def came(self, way, h):
+        g = self.place
+        at = self.slot(self.origin(way, h))
+        return remote(at, at, self.send.at[way, h], self.recv.at[way, h], g.core)
+
+    def start(self, src):
+        for way in range(2):
+            @pl.when(self.leaves(way, 1))
+            def _():
+                self.out(way, 1, src).start()
+
+    def step(self, h, then=None):
+        for way in range(2):
+            @pl.when(self.comes(way, h))
+            def _():
+                self.came(way, h).wait_recv()
+                if h + 1 < self.place.nz:
+                    @pl.when(self.leaves(way, h + 1))
+                    def _():
+                        self.out(way, h + 1).start()
+                if then is not None:
+                    then(way, h)
+
+    def finish(self):
+        for way in range(2):
+            for h in range(1, self.place.nz):
+                @pl.when(self.leaves(way, h))
+                def _():
+                    self.out(way, h).wait_send()
+
+
 class Gather:
-    def __init__(self, place, buf, send, recv, local):
-        self.place, self.buf, self.send, self.recv, self.local = place, buf, send, recv, local
-
-    def one(self, i, k, r, src):
+    def __init__(self, place, buf, send, recv, ysend, yrecv, local):
+        self.place, self.buf, self.local = place, buf, local
+        self.send, self.recv, self.ysend, self.yrecv = send, recv, ysend, yrecv
+
+    def line(self, i, r):
+        return Line(self.place, lambda zz: self.buf.at[i, zz, r], self.send.at[i, r], self.recv.at[i, r])
+
+    def near(self, i, r, src):
+        return pltpu.make_async_copy(src, self.buf.at[i, self.place.d, r], self.local.at[i, r])
+
+    def across(self, i, way, h, r):
+        at = self.line(i, 0).origin(way, h)
         return remote(
-            src, self.buf.at[i, k, r], self.send.at[i, k, r], self.recv.at[i, k, r], self.place.z_behind(k)
+            self.buf.at[i, at, 0], self.buf.at[i, at, r],
+            self.ysend.at[i, way, h, r], self.yrecv.at[i, way, h, r], self.place.behind(r),
         )
 
-    def away(self, i, r, src):
-        return [self.one(i, k, r, src) for k in range(1, self.place.nz)]
-
-    def near(self, i, r, src):
-        return pltpu.make_async_copy(src, self.buf.at[i, 0, r], self.local.at[i, r])
-
-    def push(self, i, r, src, keep=True):
+    def start(self, i, r, src, keep=True):
         if keep:
             self.near(i, r, src).start()
-        for copy in self.away(i, r, src):
-            copy.start()
-
-    def across(self, i, k, r):
+        self.line(i, r).start(src)
+
+    def pass_one(self, i, way, h):
+        for r in range(1, self.place.ny):
+            self.across(i, way, h, r).start()
+
+    def step(self, i, h, slots):
+        for r in slots:
+            self.line(i, r).step(h)
+
+    def passes(self, i, early):
+        line, d = self.line(i, 0), self.place.d
+        for h in range(1, self.place.nz):
+            for way in range(2):
+                soon = (way == 0) | (d == 0) if h == 1 else False
+                here = soon if early else jnp.logical_not(soon)
+
+                @pl.when(line.comes(way, h) & here)
+                def _():
+                    self.pass_one(i, way, h)
+
+    def pass_early(self, i):
+        self.passes(i, True)
+
+    def pass_rest(self, i):
+        self.passes(i, False)
+
+    def finish(self, i, slots, kept):
         g = self.place
-        return remote(
-            self.buf.at[i, k, 0], self.buf.at[i, k, r], self.send.at[i, k, r], self.recv.at[i, k, r], g.behind(r)
-        )
-
-    def pass_on(self, i):
-        for k in range(1, self.place.nz):
-            self.one(i, k, 0, self.buf.at[i, 0, 0]).wait_recv()
-            for r in range(1, self.place.ny):
-                self.across(i, k, r).start()
-
-    def drain(self, i, keep=True):
-        for r in range(self.place.ny):
-            src = self.buf.at[i, 0, r]
-            if keep or r == 0:
-                self.near(i, r, src).wait()
-            for copy in self.away(i, r, src):
-                copy.wait()
-
-    def drain_passed(self, i):
-        g = self.place
+        for r in kept:
+            self.near(i, r, self.buf.at[i, g.d, r]).wait()
+        for r in slots:
+            self.line(i, r).finish()
+        line = self.line(i, 0)
         for r in range(g.ny):
-            self.near(i, r, self.buf.at[i, 0, r]).wait()
-        for copy in self.away(i, 0, self.buf.at[i, 0, 0]):
-            copy.wait_send()
-        for k in range(1, g.nz):
-            for r in range(1, g.ny):
-                self.across(i, k, r).wait()
+            if r not in slots:
+                for h in range(1, g.nz):
+                    for way in range(2):
+                        @pl.when(line.comes(way, h))
+                        def _():
+                            self.across(i, way, h, r).wait()
 
 
 class Exchange:
-    def __init__(self, place, rows_ref, retl, retc, rety, sendl, sendc, sendy, sems):
-        self.place = place
+    def __init__(self, place, chunks, rows_ref, retl, retc, rety, sendl, sendc, sendy, sems):
+        self.place, self.chunks = place, chunks
         self.rows_ref = rows_ref
         self.retl, self.retc, self.rety = retl, retc, rety
         self.sendl, self.sendc, self.sendy = sendl, sendc, sendy
         self.sems = sems
         self.tokens = rows_ref.shape[2]
-        self.span = self.tokens // CHUNKS
+        self.span = self.tokens // chunks
 
     def rows(self, q):
         return pl.ds(q * self.span, self.span)
@@ -240,14 +305,14 @@
         )
 
     def send_own(self):
-        for q in range(CHUNKS):
+        for q in range(self.chunks):
             for r in range(1, self.place.ny):
                 self.y_own(r, q).start()
         self.core_own().start()
 
-    def run(self, local_block, remote_block, complete):
+    def run(self, local_block, remote_block, complete, meanwhile=None):
         ny = self.place.ny
-        items = [(r, q) for q in range(CHUNKS) for r in range(1, ny)]
+        items = [(r, q) for q in range(self.chunks) for r in range(1, ny)]
         self.core_own().wait_recv()
         local_block()
         self.back_local().start()
@@ -255,11 +320,13 @@
         def arrive(r, q):
             self.y_own(r, q).wait_recv()
             self.forward(r, q).start()
-            if q == CHUNKS - 1:
+            if q == self.chunks - 1:
                 complete(r)
 
         if items:
             arrive(*items[0])
+        if meanwhile is not None:
+            meanwhile()
         for i, (r, q) in enumerate(items):
             self.forward(r, q).wait_recv()
             own = remote_block(r, q)
@@ -280,7 +347,7 @@
         ny = self.place.ny
         self.core_own().wait_send()
         self.back_local().wait_send()
-        for q in range(CHUNKS):
+        for q in range(self.chunks):
             for r in range(1, ny):
                 self.y_own(r, q).wait_send()
                 self.forward(r, q).wait_send()
@@ -293,8 +360,8 @@
         self.cs, self.cr, self.ys, self.yr, self.bs, self.br, self.zs, self.zr = [ref.at[m] for ref in refs]
 
 
-def sem_shapes(micro, ny):
-    return [pltpu.SemaphoreType.DMA((micro, ny, CHUNKS)) for _ in range(8)]
+def sem_shapes(micro, ny, chunks):
+    return [pltpu.SemaphoreType.DMA((micro, ny, chunks)) for _ in range(8)]
 
 
 def chosen_gates(logits_t, route):
@@ -317,17 +384,145 @@
     return jnp.concatenate([lanes] * (width // 128), 1)
 
 
+def gather_kernel(
+    ny, nz,
+    small_ref, route_h, wqkv_h, wout_h, wg_h, wu_h, wd_h,
+    small_t, route_o, wqkv_o, wout_o, slices_o, partner_o,
+    small_s, wg, wu, turned,
+    lsem, own_sem, cs, cr, ys, yr, zs, zr, sls, pls, plr,
+):
+    g = Place(ny, nz)
+    hidden, width = turned.shape[2], turned.shape[3]
+    slice_h = hidden // nz
+    loads = [pltpu.make_async_copy(src, dst, lsem.at[i]) for i, (src, dst) in enumerate(((wg_h, wg), (wu_h, wu)))]
+    for copy in loads:
+        copy.start()
+    g.greet(with_x=False)
+    arrays = ((small_ref, small_s), (route_h, route_o), (wqkv_h, wqkv_o), (wout_h, wout_o))
+    count = len(arrays)
+
+    def near(n):
+        src, dst = arrays[n]
+        return pltpu.make_async_copy(src, dst.at[g.e, g.d], own_sem.at[n])
+
+    lines = [Line(g, lambda zz, dst=dst: dst.at[g.e, zz], zs.at[n], zr.at[n]) for n, (_, dst) in enumerate(arrays)]
+
+    def along_y(n, way, h, r):
+        src, dst = arrays[n]
+        at = dst.at[g.e, lines[n].origin(way, h)]
+        return remote(src if h == 0 else at, at, ys.at[n, way, h, r], yr.at[n, way, h, r], g.behind(r))
+
+    def to_core(n, way, h, r):
+        src, dst = arrays[n]
+        at = dst.at[g.pack(r, False), lines[n].origin(way, h)]
+        own = h == 0 and r == 0
+        return remote(src if own else at, at, cs.at[n, way, h, r], cr.at[n, way, h, r], g.core)
+
+    for n in range(count):
+        for r in range(1, ny):
+            along_y(n, 0, 0, r).start()
+        lines[n].start(arrays[n][0])
+        near(n).start()
+        to_core(n, 0, 0, 0).start()
+
+    def got_z(n, h):
+        def then(way, h):
+            for r in range(1, ny):
+                along_y(n, way, h, r).start()
+            to_core(n, way, h, 0).start()
+
+        lines[n].step(h, then)
+
+    def got_y(n, h):
+        for way in range(1 if h == 0 else 2):
+            def pass_on():
+                for r in range(1, ny):
+                    along_y(n, way, h, r).wait_recv()
+                    to_core(n, way, h, r).start()
+
+            if h == 0:
+                pass_on()
+            else:
+                pl.when(lines[n].comes(way, h))(pass_on)
+
+    parts = []
+    here = pl.ds(pl.multiple_of(g.d * slice_h, slice_h), slice_h)
+    for i in range(3):
+        for j in range(2):
+            src = wd_h.at[j, here] if i == 2 else turned.at[i, j, here]
+            to = slice(j * slice_h, (j + 1) * slice_h)
+            parts.append(pltpu.make_async_copy(src, slices_o.at[i, to], sls.at[i, j]))
+            parts.append(remote(src, partner_o.at[i, to], pls.at[i, j], plr.at[i, j], g.core))
+
+    def turn(i, j, n):
+        src = (wg, wu)[i]
+        if j == 0 and n == 0:
+            loads[i].wait()
+        cols = slice(n * 256, (n + 1) * 256)
+        turned[i, j, cols, :] = jnp.transpose(src[j, :, cols])
+
+    turns = [(i, j, n) for i in range(2) for j in range(2) for n in range(hidden // 256)]
+
+    z_items = [(n, h) for h in range(1, nz) for n in range(count)]
+    y_items = [(n, 0) for n in range(count)] + z_items
+    done = 0
+    for i, item in enumerate(z_items):
+        got_z(*item)
+        if i % 2 == 1 or i >= count:
+            got_y(*y_items[done])
+            done += 1
+        for piece in turns[:2]:
+            turn(*piece)
+        turns = turns[2:]
+        if not turns and parts:
+            for copy in parts:
+                copy.start()
+            started, parts = parts, []
+    for item in y_items[done:]:
+        got_y(*item)
+
+    def each(act):
+        for n in range(count):
+            for h in range(nz):
+                for way in range(1 if h == 0 else 2):
+                    if h == 0:
+                        act(n, way, h)
+                    else:
+                        pl.when(lines[n].comes(way, h))(lambda: act(n, way, h))
+
+    def arrived(n, way, h):
+        for r in range(ny):
+            to_core(n, way, h, r).wait_recv()
+
+    def sent(n, way, h):
+        for r in range(ny):
+            to_core(n, way, h, r).wait_send()
+            if r:
+                along_y(n, way, h, r).wait_send()
+
+    each(arrived)
+    for n in range(count):
+        near(n).wait()
+    gathered = small_s[...].reshape(width, small_s.shape[3])
+    small_t[...] = jnp.transpose(gathered)[0:SMALL_ROWS].astype(BF16)
+    each(sent)
+    for line in lines:
+        line.finish()
+    for copy in started:
+        copy.wait()
+
+
 def forward_kernel(
     ny, nz, sections,
     x_ref, segc_ref, segr_ref, route_ref, small_ref, cos_ref, sin_ref,
-    cot_h, slices_h, wqkv_h, wout_h, wg_h, wu_h, wd_h,
-    out_ref, hin_ref, h1_ref, qkv_ref, obb_ref, xm_ref, gates_ref, zf_h, partner_h,
+    cot_h, wqkv_h, wout_h, wg_h, wu_h, wd_h,
+    out_ref, hin_ref, h1_ref, qkv_ref, obb_ref, xm_ref, gates_ref, zf_h,
     wqkv, wout, wg, wu, wd, ob_s, hid, accl, accr, retl, retc, rety, sendl, sendc, sendy,
-    wsem, zs, zr, zl, ps, pr, gs, gr, xs, xr, *sem_refs,
+    wsem, zs, zr, zys, zyr, zl, gs, gr, xs, xr, *sem_refs,
 ):
     micro, tokens, width = x_ref.shape
     hidden = wg.shape[2]
-    span = tokens // CHUNKS
+    span = tokens // FORWARD_CHUNKS
     loads = [
         pltpu.make_async_copy(src, dst, wsem.at[i])
         for i, (src, dst) in enumerate([(wqkv_h, wqkv), (wout_h, wout), (wg_h, wg), (wu_h, wu), (wd_h, wd)])
@@ -339,26 +534,25 @@
     gain_a = small_ref[ROUTER_ROWS : ROUTER_ROWS + 1, :].astype(F32)
     gain_m = small_ref[ROUTER_ROWS + 1 : ROUTER_ROWS + 2, :].astype(F32)
     cos, sin = cos_ref[...], sin_ref[...]
-    gather = Gather(g, zf_h, zs, zr, zl)
+    gather = Gather(g, zf_h, zs, zr, zys, zyr, zl)
+    every = range(ny)
     first, last = g.s == 0, g.s == sections - 1
 
-    partner_copy = remote(slices_h, partner_h, ps, pr, g.core)
-    partner_copy.start()
-
     def cot_copy(r):
-        return remote(cot_h.at[0], zf_h.at[0, 0, r], gs.at[r], gr.at[r], g.behind(r))
+        return remote(cot_h.at[0], zf_h.at[0, g.d, r], gs.at[r], gr.at[r], g.behind(r))
 
     @pl.when(last)
     def _():
         for r in range(1, ny):
             cot_copy(r).start()
-        gather.push(0, 0, cot_h.at[0])
+        gather.start(0, 0, cot_h.at[0])
         for r in range(1, ny):
             cot_copy(r).wait_recv()
-            gather.push(0, r, zf_h.at[0, 0, r], keep=False)
+            gather.start(0, r, zf_h.at[0, g.d, r], keep=False)
+        gather.step(0, 1, every)
 
     def hop(m, q):
-        here = pl.ds(q * span, span)
+        here = pl.ds(q * (tokens // HOP_CHUNKS), tokens // HOP_CHUNKS)
         return remote(out_ref.at[m, here], hin_ref.at[m, here], xs.at[m, q], xr.at[m, q], g.x)
 
     def experts(rows, lanes, keep):
@@ -386,7 +580,7 @@
 
         @pl.when(g.s > 0)
         def _():
-            for q in range(CHUNKS):
+            for q in range(HOP_CHUNKS):
                 hop(m, q).wait_recv()
 
         h = hin_ref[m].astype(F32)
@@ -432,15 +626,27 @@
         h1 = h1_ref[m]
         xm_ref[m, 0, 0] = (h1 * lax.rsqrt(jnp.mean(h1 * h1, -1, keepdims=True) + EPS) * gain_m).astype(BF16)
 
-        ex = Exchange(g, xm_ref.at[m], retl, retc, rety, sendl, sendc, sendy, Sems(sem_refs, m))
+        ex = Exchange(g, FORWARD_CHUNKS, xm_ref.at[m], retl, retc, rety, sendl, sendc, sendy, Sems(sem_refs, m))
         ex.send_own()
 
         def complete(r):
             @pl.when(first & (m == 0))
             def _():
-                gather.push(0, r, xm_ref.at[0, r, 0])
+                gather.start(0, r, xm_ref.at[0, r, 0])
+
+        def move(h):
+            if h + 1 < nz:
+                @pl.when(last & (m == 0))
+                def _():
+                    gather.step(0, h + 1, every)
+
+            if h < nz:
+                @pl.when(first & (m == 1))
+                def _():
+                    gather.step(0, h, every)
 
         complete(0)
+        move(1)
 
         @pl.when(m == 0)
         def _():
@@ -450,7 +656,7 @@
         def gates_for(r, other, here):
             rows = xm_ref[m, r, other, here, :]
             logits_t = dot_nt(small_ref[0:ROUTER_ROWS, :], rows)
-            gates_t = chosen_gates(logits_t, route_ref[g.pack(r, other), m][:, here])
+            gates_t = chosen_gates(logits_t, route_ref[g.pack(r, other) * nz + g.d, m][:, here])
             return gates_t
 
         def lanes_of(blocks):
@@ -493,7 +699,7 @@
             return lambda: accr[...]
 
         ex.run(local_block, remote_block, complete)
-        for q in range(CHUNKS):
+        for q in range(HOP_CHUNKS):
             here = slice(q * span, (q + 1) * span)
             ex.arrived(q)
             total = h1_ref[m, here, :] + accl[here, :] + retl[here, :].astype(F32)
@@ -506,26 +712,30 @@
                 hop(m, q).start()
 
         ex.finish()
+        move(2)
         return carry
 
     lax.fori_loop(0, micro, body, 0)
-    partner_copy.wait()
 
     @pl.when(g.s < sections - 1)
     def _():
         for m in range(micro):
-            for q in range(CHUNKS):
+            for q in range(HOP_CHUNKS):
                 hop(m, q).wait_send()
 
     @pl.when(first)
     def _():
-        gather.drain(0)
+        for h in range(3, nz):
+            gather.step(0, h, every)
+        gather.finish(0, every, every)
 
     @pl.when(last)
     def _():
         for r in range(1, ny):
             cot_copy(r).wait_send()
-        gather.drain(0, keep=False)
+        for h in range(4, nz):
+            gather.step(0, h, every)
+        gather.finish(0, every, [0])
 
 
 def backward_kernel(
@@ -536,11 +746,11 @@
     gin_ref, grows_ref, xab_ref, dqkv_ref, dattn_ref, gsmall_ref, zb_h,
     wqkv, wout, wg, wu, wd, xm_s, hid, act_s, slope_s, da_s, db_s, accl, accr, dh1_s, n_s,
     retl, retc, rety, sendl, sendc, sendy,
-    wsem, xmsem, zs, zr, zl, xs, xr, *sem_refs,
+    wsem, xmsem, zs, zr, zys, zyr, zl, xs, xr, *sem_refs,
 ):
     micro, tokens, width = cot_ref.shape
     hidden = wg.shape[2]
-    span = tokens // CHUNKS
+    span = tokens // BACKWARD_CHUNKS
     loads = [
         pltpu.make_async_copy(src, dst, wsem.at[i])
         for i, (src, dst) in enumerate([(wg_h, wg), (wu_h, wu), (wd_h, wd), (wout_h, wout), (wqkv_h, wqkv)])
@@ -553,40 +763,39 @@
     gain_m = small_ref[ROUTER_ROWS + 1 : ROUTER_ROWS + 2, :].astype(F32)
     cos, sin = cos_ref[...], sin_ref[...]
     gsmall_ref[...] = jnp.zeros_like(gsmall_ref)
-    gather = Gather(g, zb_h, zs, zr, zl)
+    gather = Gather(g, zb_h, zs, zr, zys, zyr, zl)
+    every = range(ny)
     first, last = g.s == 0, g.s == sections - 1
 
     @pl.when(first)
     def _():
         for m in range(1, micro):
-            for r in range(ny):
-                gather.push(micro + m, r, xm_h.at[m, r, 0])
-
-    @pl.when(last)
-    def _():
-        for m in range(micro):
-            gather.push(m, 0, xm_h.at[m, 0, 0])
-            for r in range(1, ny):
-                gather.near(m, r, xm_h.at[m, r, 0]).start()
+            for r in every:
+                gather.start(micro + m, r, xm_h.at[m, r, 0])
+            for h in range(1, nz):
+                gather.step(micro + m, h, every)
 
     def hop(m, q):
-        here = pl.ds(q * span, span)
+        here = pl.ds(q * (tokens // HOP_CHUNKS), tokens // HOP_CHUNKS)
         return remote(gin_ref.at[m, here], grows_ref.at[m, 0, 0, here], xs.at[m, q], xr.at[m, q], g.x)
 
     def body(m, carry):
         load_xm = pltpu.make_async_copy(xm_h.at[m], xm_s, xmsem)
         load_xm.start()
 
-        @pl.when(g.s == sections - 1)
+        @pl.when(last)
         def _():
             grows_ref[m, 0, 0] = cot_ref[m]
+            gather.start(m, 0, xm_h.at[m, 0, 0])
+            for r in range(1, ny):
+                gather.near(m, r, xm_h.at[m, r, 0]).start()
 
         @pl.when(g.s < sections - 1)
         def _():
-            for q in range(CHUNKS):
+            for q in range(HOP_CHUNKS):
                 hop(m, q).wait_recv()
 
-        ex = Exchange(g, grows_ref.at[m], retl, retc, rety, sendl, sendc, sendy, Sems(sem_refs, m))
+        ex = Exchange(g, BACKWARD_CHUNKS, grows_ref.at[m], retl, retc, rety, sendl, sendc, sendy, Sems(sem_refs, m))
         ex.send_own()
 
         def complete(r):
@@ -595,13 +804,13 @@
             @pl.when(first)
             def _():
                 if r == 0:
-                    gather.push(m, 0, src)
+                    gather.start(m, 0, src)
                 else:
                     gather.near(m, r, src).start()
 
-            @pl.when(last & (m > 0))
-            def _():
-                gather.push(micro + m, r, src)
+        def move(hops):
+            for h in hops:
+                gather.step(m, h, [0])
 
         complete(0)
 
@@ -686,8 +895,16 @@
             experts(grows_ref[m, r, :, here, :].reshape(2 * span, width), r, here, keep)
             return lambda: accr[...]
 
-        ex.run(local_block, remote_block, complete)
-        for q in range(CHUNKS):
+        def meanwhile():
+            move(range(1, 2))
+
+            @pl.when(first)
+            def _():
+                gather.pass_early(m)
+
+        ex.run(local_block, remote_block, complete, meanwhile)
+        move(range(2, min(3, nz)))
+        for q in range(BACKWARD_CHUNKS):
             ex.arrived(q)
         total = accl[...] + retl[...].astype(F32)
         for r in range(1, ny):
@@ -721,7 +938,11 @@
             for load in loads[3:]:
                 load.wait()
 
-        gather.pass_on(m)
+        @pl.when(first)
+        def _():
+            move(range(3, nz))
+            gather.pass_rest(m)
+
         bias = mask_bias(segc_ref[m], segr_ref[m])
         bias6 = jnp.concatenate([bias] * GROUP, 0)
         qkv = qkv_ref.at[m]
@@ -774,8 +995,9 @@
 
         @pl.when(g.s > 0)
         def _():
-            for q in range(CHUNKS):
+            for q in range(HOP_CHUNKS):
                 hop(m, q).start()
+            move(range(3, nz))
 
         ex.finish()
         return carry
@@ -785,13 +1007,24 @@
     @pl.when(g.s > 0)
     def _():
         for m in range(micro):
-            for q in range(CHUNKS):
+            for q in range(HOP_CHUNKS):
                 hop(m, q).wait_send()
 
+    @pl.when(last)
+    def _():
+        for m in range(micro):
+            gather.pass_early(m)
+            gather.pass_rest(m)
+        for m in range(1, micro):
+            for r in every:
+                gather.start(micro + m, r, grows_ref.at[m, r, 0])
+            for h in range(1, nz):
+                gather.step(micro + m, h, every)
+
     for m in range(micro):
-        gather.drain_passed(m)
+        gather.finish(m, [0], every)
     for m in range(1, micro):
-        gather.drain(micro + m)
+        gather.finish(micro + m, every, every)
 
 
 def tail_kernel(
@@ -888,20 +1121,31 @@
                 for zi in range(nz):
                     dst[zi, 0:shard, at + n * 512 : at + (n + 1) * 512] = got[zi * shard : (zi + 1) * shard]
 
+    def flipped(mask):
+        place = g.d
+        for b in range(nz.bit_length()):
+            if mask >> b & 1:
+                place = place + (1 << b) - (2 << b) * lax.rem(lax.div(g.d, 1 << b), 2)
+        return place
+
     def y_copy(r, k):
-        zi = g.z_of(k)
+        zi = flipped(k)
         return remote(ysend.at[r - 1, zi], yland.at[ny - r - 1, zi], ys.at[r, k], yr.at[ny - r, k], g.ahead(r))
 
     def y_arrival(r, k):
-        zi = g.z_of(k)
+        zi = flipped(k)
         return remote(ysend.at[r - 1, zi], yland.at[r - 1, zi], ys.at[r, k], yr.at[r, k], g.ahead(r))
 
     order = list(range(1, nz)) + [0]
+    masks = list(range(nz - 1, -1, -1))
+
+    def y_start(k):
+        for r in range(1, ny):
+            y_copy(r, k).start()
+
     for r in range(1, ny):
         attn_rows(lax.rem(g.y + r, ny), ysend.at[r - 1])
-    for k in order:
-        for r in range(1, ny):
-            y_copy(r, k).start()
+    y_start(masks[0])
     sm_core.wait_recv()
     sm_s[0] = gsmall_ref[...] + sm_s[1]
     sm_core.wait_send()
@@ -909,22 +1153,43 @@
         sm_y(r).start()
     attn_rows(g.y, own_s)
 
-    def z_copy(k):
-        return remote(own_s.at[g.z_of(k)], zland.at[nz - k - 1], zs.at[0, k], zr.at[0, nz - k], g.z_ahead(k))
-
-    def z_arrival(k):
-        return remote(own_s.at[g.d], zland.at[k - 1], zs.at[0, k], zr.at[0, k], g.z_ahead(k))
-
-    def attn_sum(k):
+    bits = nz.bit_length() - 1
+
+    def low(mask):
+        return (mask & -mask).bit_length() - 1 if mask else bits
+
+    landings = [(mask, b) for mask in range(nz) for b in range(low(mask))]
+
+    def z_copy(mask):
+        b = low(mask)
+        at = landings.index((mask - (1 << b), b))
+        device = (g.s, g.e, flipped(1 << b))
+        return remote(own_s.at[flipped(mask)], zland.at[at], zs.at[0, mask], zr.at[0, at], device)
+
+    def z_arrival(mask, b):
+        at = landings.index((mask, b))
+        device = (g.s, g.e, flipped(1 << b))
+        return remote(own_s.at[flipped(mask)], zland.at[at], zs.at[0, mask], zr.at[0, at], device)
+
+    def advance(mask):
         for r in range(1, ny):
-            y_arrival(r, k).wait_recv()
-        zi = g.z_of(k)
-        total = own_s[zi].astype(F32)
-        for r in range(1, ny):
-            total = total + yland[r - 1, zi].astype(F32)
-        own_s[zi] = total.astype(BF16)
-        if k:
-            z_copy(k).start()
+            y_arrival(r, mask).wait_recv()
+        zi = flipped(mask)
+        for b in range(low(mask)):
+            z_arrival(mask, b).wait_recv()
+        for n in range((qkv_width + width) // 512):
+            cols = slice(n * 512, (n + 1) * 512)
+            total = own_s[zi, :, cols].astype(F32)
+            for r in range(1, ny):
+                total = total + yland[r - 1, zi, :, cols].astype(F32)
+            for b in range(low(mask)):
+                total = total + zland[landings.index((mask, b)), :, cols].astype(F32)
+            if mask:
+                own_s[zi, :, cols] = total.astype(BF16)
+            else:
+                attn_ref[:, cols] = total
+        if mask:
+            z_copy(mask).start()
 
     for copy in mine:
         copy.wait()
@@ -938,6 +1203,10 @@
     chosen = 2 * owner + jnp.where(local < slice_h, 0, 1)
     spread = jnp.where(expert == chosen, 1.0, 0.0).astype(BF16)
 
+    blocks = span * ny
+    total_blocks = micro * groups * blocks
+    polls = (total_blocks * 7 // 16, total_blocks * 10 // 16)
+
     def group(i, carry):
         m = lax.div(i, groups)
         wait_load()
@@ -945,7 +1214,7 @@
         def block(b, carry):
             k = lax.rem(i, groups) * span + lax.div(b, ny)
             r = lax.rem(b, ny)
-            place = (lax.rem(g.y + r, ny) * 2 + g.c) * nz + g.z_of(k)
+            place = (lax.rem(g.y + r, ny) * 2 + g.c) * nz + k
             x = x_s[lax.div(b, ny), r]
             gr = g_s[lax.div(b, ny), r]
             gates_t = chosen_gates(dot_nt(small_ref[0:ROUTER_ROWS, :], x), route_ref[place, m])
@@ -966,9 +1235,18 @@
                 da_s[here, cols] = (u * slope * bb).astype(BF16)
                 db_s[here, cols] = (u * act).astype(BF16)
                 gh_s[here, cols] = ((act * bb).astype(BF16).astype(F32) * gate).astype(BF16)
+            for n, poll in enumerate(polls):
+                @pl.when(i * blocks + b == poll - 1)
+                def _():
+                    y_start(masks[n + 1])
+
+                @pl.when(i * blocks + b == poll)
+                def _():
+                    advance(masks[n])
+
             return carry
 
-        lax.fori_loop(0, span * ny, block, 0)
+        lax.fori_loop(0, blocks, block, 0)
 
         def columns(n, carry):
             cols = pl.ds(pl.multiple_of(n * 256, 256), 256)
@@ -987,6 +1265,10 @@
         return carry
 
     lax.fori_loop(0, micro * groups, group, 0)
+    for mask in masks[3:]:
+        y_start(mask)
+    for mask in masks[2:-1]:
+        advance(mask)
 
     def core_copy(n, k):
         return remote(csend.at[n, k], cland.at[n, k], cs.at[n, k], cr.at[n, k], g.core)
@@ -1014,7 +1296,6 @@
     dsend[...] = acc_d[half:both, :].astype(BF16)
     down_copy.start()
     for k in order[:-1]:
-        attn_sum(k)
         for n in range(2):
             core_copy(n, k).wait_recv()
             total = accs[n][width_rows(k), 0:half] + cland[n, k].astype(F32)
@@ -1025,8 +1306,9 @@
         cland[n, 0] = (accs[n][width_rows(0), 0:half] + cland[n, 0].astype(F32)).astype(BF16)
         turn_near(n).start()
     down_copy.wait_recv()
-    down_ref[...] = (acc_d[0:half, :] + dland[...].astype(F32)).astype(BF16)
-    attn_sum(0)
+    dland[...] = (acc_d[0:half, :] + dland[...].astype(F32)).astype(BF16)
+    down_near = pltpu.make_async_copy(dland, down_ref, ts.at[0, nz])
+    down_near.start()
 
     for r in range(1, ny):
         sm_y_arrival(r).wait_recv()
@@ -1041,12 +1323,7 @@
         total = total + smz[k]
     small_out[...] = total
 
-    for k in range(1, nz):
-        z_arrival(k).wait_recv()
-    total = own_s[g.d].astype(F32)
-    for k in range(1, nz):
-        total = total + zland[k - 1].astype(F32)
-    attn_ref[...] = total
+    advance(0)
     for k in range(1, nz):
         for n in range(2):
             turn_arrival(n, k).wait_recv()
@@ -1068,6 +1345,29 @@
     down_copy.wait_send()
     for n in range(2):
         turn_near(n).wait()
+    down_near.wait()
+
+
+def finish_kernel(nz, experts, gate_in, up_in, down_in, attn_in, small_in, gate, up, down, qkv, out, router, again, mgain):
+    slice_h = gate_in.shape[2] // 2
+    for src, dst in ((gate_in, gate), (up_in, up)):
+        for j in range(2):
+            cols = slice(j * slice_h, (j + 1) * slice_h)
+            dst[0, j] = jnp.concatenate([src[z, :, cols].astype(F32) for z in range(nz)], 1)
+    down[0, 0] = down_in[...].astype(F32)
+    shard, split = qkv.shape[1], qkv.shape[2]
+    qkv[0] = attn_in[0:shard, 0:split]
+    out[0] = attn_in[0:shard, split:]
+    rows, width = small_in.shape
+    base = (lax.axis_index("expert") * nz + lax.axis_index("dp")) * shard
+    at = lax.broadcasted_iota(jnp.int32, (width, 128), 0)
+    lane = lax.broadcasted_iota(jnp.int32, (width, 128), 1)
+    pick = jnp.where(at == base + lane, 1.0, 0.0).astype(F32)
+    got = jnp.dot(small_in[...], pick, precision=lax.Precision.HIGHEST, preferred_element_type=F32)
+    again[...] = got[ROUTER_ROWS : ROUTER_ROWS + 1, 0:shard]
+    mgain[...] = got[ROUTER_ROWS + 1 : ROUTER_ROWS + 2, 0:shard]
+    turned = jnp.transpose(jnp.concatenate([got, jnp.zeros((128 - rows, 128), F32)], 0))
+    router[0] = turned[0:shard, 0:experts]
 
 
 VMEM = pl.BlockSpec(memory_space=pltpu.VMEM)
@@ -1088,48 +1388,64 @@
     place_e, place_d = lax.axis_index("expert"), lax.axis_index("dp")
     small = jnp.concatenate(
         [
-            jnp.pad(w_router[0], ((0, 0), (0, ROUTER_ROWS - total_experts))),
+            w_router[0],
+            jnp.zeros((shard, ROUTER_ROWS - total_experts), BF16),
             attn_gain[0][:, None],
             moe_gain[0][:, None],
-            jnp.zeros((shard, SMALL_ROWS - ROUTER_ROWS - 2), BF16),
+            jnp.zeros((shard, 128 - ROUTER_ROWS - 2), BF16),
         ],
         1,
-    )
-    small = lax.all_gather(small, owners, axis=0, tiled=True).T
-    wqkv = lax.all_gather(w_qkv[0], owners, axis=0, tiled=True)
-    wout = lax.all_gather(w_out[0], owners, axis=0, tiled=True)
-    routes_all = lax.all_gather(jnp.transpose(routes[0, :, 0], (0, 2, 1)), owners, axis=0)
-    route = lax.dynamic_index_in_dim(
-        routes_all.reshape((ne, nz) + routes_all.shape[1:]), place_d, 1, keepdims=False
-    )
+    ).astype(F32)
+    own_routes = jnp.transpose(routes[0, :, 0], (0, 2, 1))
     cos, sin = rotary_tables(tokens)
     segs = segments[:, 0]
     segc, segr = segs[:, :, None], segs[:, None, :]
     x = layer_input[:, 0]
     cot = cotangent[:, 0]
     wg, wu, wd = w_gate[0], w_up[0], w_down[0]
-    span = tokens // CHUNKS
-    qkv_width = wqkv.shape[1]
+    qkv_width = w_qkv.shape[2]
     slice_h = hidden // nz
     half = 2 * slice_h
-    at = place_d * slice_h
-    slices = jnp.stack(
-        [
-            jnp.swapaxes(lax.dynamic_slice_in_dim(wg, at, slice_h, 2), 1, 2).reshape(half, width),
-            jnp.swapaxes(lax.dynamic_slice_in_dim(wu, at, slice_h, 2), 1, 2).reshape(half, width),
-            lax.dynamic_slice_in_dim(wd, at, slice_h, 1).reshape(half, width),
-        ]
-    )
 
     def shape(*dims, dtype=BF16):
         return jax.ShapeDtypeStruct(dims, dtype)
 
+    grid_sems = [DMA((4, 2, nz, ny)) for _ in range(4)]
+    small, routes_all, wqkv, wout, slices, partner = pl.pallas_call(
+        functools.partial(gather_kernel, ny, nz),
+        out_shape=(
+            shape(SMALL_ROWS, width),
+            shape(ne, nz, *own_routes.shape, dtype=jnp.int32),
+            shape(ne, nz, shard, qkv_width),
+            shape(ne, nz, shard, width),
+            shape(3, half, width),
+            shape(3, half, width),
+        ),
+        in_specs=[VMEM] + [ANY] * 6,
+        out_specs=tuple([VMEM] + [ANY] * 5),
+        scratch_shapes=[
+            pltpu.VMEM((ne, nz, shard, 128), F32),
+            pltpu.VMEM(wg.shape, BF16),
+            pltpu.VMEM(wu.shape, BF16),
+            pltpu.VMEM((2, 2, hidden, width), BF16),
+            DMA((2,)), DMA((4,)),
+        ]
+        + grid_sems
+        + [DMA((4, 2, nz)), DMA((4, 2, nz)), DMA((3, 2)), DMA((3, 2)), DMA((3, 2))],
+        compiler_params=pltpu.CompilerParams(
+            collective_id=3, has_side_effects=True, vmem_limit_bytes=60 * 2**20
+        ),
+        name="gather_weights",
+    )(small, own_routes, w_qkv[0], w_out[0], wg, wu, wd)
+    wqkv = wqkv.reshape(width, qkv_width)
+    wout = wout.reshape(width, width)
+    routes_all = routes_all.reshape((ne * nz,) + own_routes.shape)
     weights = [pltpu.VMEM(w.shape, BF16) for w in (wqkv, wout, wg, wu, wd)]
-    hop_sems = [DMA((micro, CHUNKS)) for _ in range(2)]
+    hop_sems = [DMA((micro, HOP_CHUNKS)) for _ in range(2)]
     block = width // ne
 
     def gather_sems(count):
-        return [DMA((count, nz, ny)), DMA((count, nz, ny)), DMA((count, ny))]
+        return [DMA((count, ny, 2, nz))] * 2 + [DMA((count, 2, nz, ny))] * 2 + [DMA((count, ny))]
 
     def returns(wide):
         return [
@@ -1141,7 +1457,7 @@
             pltpu.VMEM((max(1, ny - 1), tokens, wide), BF16),
         ]
 
-    out, hin, h1, qkv, obb, xm, gates, zf, partner = pl.pallas_call(
+    out, hin, h1, qkv, obb, xm, gates, zf = pl.pallas_call(
         functools.partial(forward_kernel, ny, nz, sections),
         out_shape=(
             shape(micro, tokens, width),
@@ -1152,28 +1468,27 @@
             shape(micro, ny, 2, tokens, width),
             shape(micro, ny, 2, ROUTER_ROWS, tokens, dtype=F32),
             shape(1, nz, ny, tokens, width),
-            shape(3, half, width),
         ),
-        in_specs=[VMEM] * 7 + [ANY] * 7,
-        out_specs=tuple([VMEM] * 7 + [ANY] * 2),
+        in_specs=[VMEM] * 7 + [ANY] * 6,
+        out_specs=tuple([VMEM] * 7 + [ANY]),
         scratch_shapes=weights
         + [
             pltpu.VMEM((tokens, width), BF16),
             pltpu.VMEM((2, 2 * tokens, hidden), BF16),
             pltpu.VMEM((tokens, width), F32),
-            pltpu.VMEM((span, width), F32),
+            pltpu.VMEM((tokens // FORWARD_CHUNKS, width), F32),
         ]
         + returns(width)
         + [DMA((5,))]
         + gather_sems(1)
-        + [DMA, DMA, DMA((ny,)), DMA((ny,))]
+        + [DMA((ny,)), DMA((ny,))]
         + hop_sems
-        + sem_shapes(micro, ny),
+        + sem_shapes(micro, ny, FORWARD_CHUNKS),
         compiler_params=pltpu.CompilerParams(
             collective_id=0, has_side_effects=True, vmem_limit_bytes=60 * 2**20
         ),
         name="layers_forward",
-    )(x, segc, segr, route, small, cos, sin, cot, slices, wqkv, wout, wg, wu, wd)
+    )(x, segc, segr, routes_all, small, cos, sin, cot, wqkv, wout, wg, wu, wd)
 
     wide = width + 128
     every = (2, ny, 2, tokens, hidden)
@@ -1199,7 +1514,7 @@
             pltpu.VMEM((2, 2 * tokens, hidden), BF16),
             pltpu.VMEM((2, 2 * tokens, hidden), BF16),
             pltpu.VMEM((tokens, wide), F32),
-            pltpu.VMEM((span, wide), F32),
+            pltpu.VMEM((tokens // BACKWARD_CHUNKS, wide), F32),
             pltpu.VMEM((tokens, width), F32),
             pltpu.VMEM((tokens, width), F32),
         ]
@@ -1207,7 +1522,7 @@
         + [DMA((5,)), DMA]
         + gather_sems(2 * micro)
         + hop_sems
-        + sem_shapes(micro, ny),
+        + sem_shapes(micro, ny, BACKWARD_CHUNKS),
         compiler_params=pltpu.CompilerParams(
             collective_id=1, has_side_effects=True, vmem_limit_bytes=62 * 2**20
         ),
@@ -1230,7 +1545,7 @@
             shape(*small_shape, dtype=F32),
         ),
         in_specs=[VMEM] * 3 + [ANY] * 8,
-        out_specs=tuple([ANY] * 2 + [VMEM] * 3),
+        out_specs=tuple([ANY] * 3 + [VMEM] * 2),
         scratch_shapes=[
             pltpu.VMEM((3, 2 * half, width), BF16),
             pltpu.VMEM((span_z, ny, tokens, width), BF16),
@@ -1260,7 +1575,7 @@
             DMA((2 * ny * micro + 2,)), DMA((2 * ny * micro + 2,)), DMA((2 * ny * micro + 2,)),
             DMA((ny + nz,)), DMA((ny + nz,)),
             DMA((3, nz)), DMA((3, nz)),
-            DMA((2, nz)), DMA((2, nz)),
+            DMA((2, nz + 1)), DMA((2, nz)),
             DMA((ny, nz)), DMA((ny, nz)),
             DMA((1, nz)), DMA((1, nz)),
         ],
@@ -1270,22 +1585,52 @@
         name="weight_gradients",
     )(routes_all, small, gsmall, zf, zb, slices, partner, xab, obb, dqkv, dattn)
 
-    def unturned(value):
-        value = value.reshape(nz, part, 2, slice_h)
-        return jnp.transpose(value, (2, 1, 0, 3)).reshape(1, 2, part, hidden).astype(F32)
-
-    mine = lax.dynamic_slice_in_dim(small_g, (place_e * nz + place_d) * shard, shard, 1)
+    steps = 2
+    finals = pl.pallas_call(
+        functools.partial(finish_kernel, nz, total_experts),
+        grid=(steps,),
+        out_shape=(
+            shape(1, 2, part, hidden, dtype=F32),
+            shape(1, 2, part, hidden, dtype=F32),
+            shape(1, 2, slice_h, width, dtype=F32),
+            shape(1, shard, qkv_width, dtype=F32),
+            shape(1, shard, width, dtype=F32),
+            shape(1, shard, total_experts, dtype=F32),
+            shape(1, shard, dtype=F32),
+            shape(1, shard, dtype=F32),
+        ),
+        in_specs=[
+            pl.BlockSpec((nz, part // steps, half), lambda i: (0, i, 0)),
+            pl.BlockSpec((nz, part // steps, half), lambda i: (0, i, 0)),
+            pl.BlockSpec((slice_h, width), lambda i: (i, 0)),
+            pl.BlockSpec((padded, attn_width), lambda i: (0, 0)),
+            pl.BlockSpec(small_shape, lambda i: (0, 0)),
+        ],
+        out_specs=(
+            pl.BlockSpec((1, 2, part // steps, hidden), lambda i: (0, 0, i, 0)),
+            pl.BlockSpec((1, 2, part // steps, hidden), lambda i: (0, 0, i, 0)),
+            pl.BlockSpec((1, 1, slice_h, width), lambda i: (0, i, 0, 0)),
+            pl.BlockSpec((1, shard, qkv_width), lambda i: (0, 0, 0)),
+            pl.BlockSpec((1, shard, width), lambda i: (0, 0, 0)),
+            pl.BlockSpec((1, shard, total_experts), lambda i: (0, 0, 0)),
+            pl.BlockSpec((1, shard), lambda i: (0, 0)),
+            pl.BlockSpec((1, shard), lambda i: (0, 0)),
+        ),
+        compiler_params=pltpu.CompilerParams(vmem_limit_bytes=60 * 2**20),
+        name="finish_gradients",
+    )(gate_g, up_g, down_g, attn_g, small_g)
+    grad_gate, grad_up, grad_down, grad_qkv, grad_out, grad_router, grad_again, grad_mgain = finals
     return (
         out[None, :, None],
         gin[None, :, None],
-        mine[ROUTER_ROWS][None],
-        attn_g[None, 0:shard, 0:qkv_width],
-        attn_g[None, 0:shard, qkv_width:],
-        mine[ROUTER_ROWS + 1][None],
-        mine[0:total_experts].T[None],
-        unturned(gate_g),
-        unturned(up_g),
-        down_g.reshape(1, 2, slice_h, width).astype(F32),
+        grad_again,
+        grad_qkv,
+        grad_out,
+        grad_mgain,
+        grad_router,
+        grad_gate,
+        grad_up,
+        grad_down,
     )
 
 

time: 637 us -> 490 us (0.77)
  blocking collectives: 65 us -> 0 us
  waiting for transfers between devices: 45.1 us -> 0 us
  local copies, waits for them, and re-layouts: 29.9 us -> 7.17 us
  between operations: 14.4 us -> 1.15 us
    pallas_call x0 -> x2, Pallas kernels: none -> 82.9 us  [the longest x1 76.7 us: per_device(): pl.pallas_call(functools.partial(gather_kernel, ny, nz), out_shape=(shape...]
    all_gather x2 -> x0, blocking collectives: 65 us -> none  [the longest x1 35.6 us: per_device(): small = lax.all_gather(small, owners, axis=0, tiled=True).T]
    pallas_call x1, Pallas kernels: 203 us -> 149 us  [per_device(): pl.pallas_call(functools.partial(tail_kernel, ny, nz, sections, span_z),...]
    all_gather x2 -> x0, waiting for transfers between devices: 43.7 us -> none  [the longest x1 43.7 us: per_device(): wqkv = lax.all_gather(w_qkv[0], owners, axis=0, tiled=True)]
    pallas_call x1, Pallas kernels: 190 us -> 168 us  [per_device(): pl.pallas_call(functools.partial(backward_kernel, ny, nz, sections), out_...]
    unnamed x33 -> x8, local copies, waits for them, and re-layouts: 11.8 us -> 4.02 us
  transfers between devices with their start and end apart: 2 -> 0, of which waited for: 1 -> 0; matrix products, arithmetic and copies ran while one was open for 2% -> 0% of each run, Pallas kernels for 0% -> 0%
where the time goes in v3:
time: 490 us; the launch traced here: 486 us
  Pallas kernels  477 us (97%)
  local copies, waits for them, and re-layouts  7.17 us (1%)
    pallas_call x1, Pallas kernels, per_device(): pl.pallas_call(functools.partial(backward_kernel, ny, nz, sections), out_...  168 us
    pallas_call x1, Pallas kernels, per_device(): pl.pallas_call(functools.partial(tail_kernel, ny, nz, sections, span_z),...  149 us
    pallas_call x1, Pallas kernels, per_device(): pl.pallas_call(functools.partial(forward_kernel, ny, nz, sections), out_s...  77.5 us
    pallas_call x1, Pallas kernels, per_device(): pl.pallas_call(functools.partial(gather_kernel, ny, nz), out_shape=(shape...  76.7 us

profile of v3, /device:TPU:0, one launch (start us, length us, event | category | flops | bytes accessed | tf_op | source)
XLA Modules:
  0.0 486.0 jit_solution(5816834900434728643)
XLA Ops:
  0.6 0.8 copy.31
  1.4 0.8 copy.32
  2.2 0.8 copy.30
  3.0 0.1 concatenate.3
  3.1 0.6 convert_element_type.3.small_ref
  3.7 1.5 copy.33.segc_ref
  5.2 76.7 %gather_weights.1 = (bf16[32,1536]{1,0:T(8,128)(2,1)}, s32[4,4,2,4,128]{4,3,2,1,0:T(4,128)}, bf16[4,4,96,2048]{3,2,1,0:T(8,128)(2,1)}, bf16[4,4,96,1536]{3,2,1,0...) custom-call(f32[96,128]{1,0:T(8,128)} %convert_element_type.3.small_ref, ...), custom_call_target="tpu_custom_call" | custom-call | tf_op jit(solution)/shard_map/gather_weights/pallas_call | solution.py:1414
  82.0 77.5 %layers_forward.1 = (bf16[2,128,1536]{2,1,0:T(8,128)(2,1)}, bf16[2,128,1536]{2,1,0:T(8,128)(2,1)}, f32[2,128,1536]{2,1,0:T(8,128)}, bf16[2,128,2048]{2,1,0:T(8,1...) custom-call(bf16[2,128,1536]{2,1,0:T(8,128)(2,1)} %bitcast.40, ...), custom_call_target="tpu_custom_call" | custom-call | tf_op jit(solution)/shard_map/layers_forward/pallas_call | solution.py:1460
  159.5 167.6 %layers_backward.1 = (bf16[2,128,1536]{2,1,0:T(8,128)(2,1)}, bf16[2,2,2,128,1536]{4,3,2,1,0:T(8,128)(2,1)}, bf16[2,4,128,384]{3,2,1,0:T(8,128)(2,1)}, bf16[2,128...) custom-call(bf16[2,128,1536]{2,1,0:T(8,128)(2,1)} %bitcast.37, ...), custom_call_target="tpu_custom_call" | custom-call | tf_op jit(solution)/shard_map/layers_backward/pallas_call | solution.py:1495
  327.0 149.1 %weight_gradients.1 = (bf16[4,384,384]{2,1,0:T(8,128)(2,1)}, bf16[4,384,384]{2,1,0:T(8,128)(2,1)}, bf16[384,1536]{1,0:T(8,128)(2,1)}, f32[96,3584]{1,0:T(8,128)}, f32[32,1536]{1,0:T(8,128)}) custom-call(s32[16,2,4,128]{3,2,1,0:T(4,128)} %bitcast.44, bf16[32,1536]{1,0:T(8,128)(2,1)} %get-tuple-element.44.small_ref, f32[32,1536]{1,0:T(8,128)} %get-tuple-element.54.gsmall_ref, ...), custom_call_target="tpu_custom_call" | custom-call | tf_op jit(solution)/shard_map/weight_gradients/pallas_call | solution.py:1538
  476.1 0.0 copy-start
  476.1 0.0 copy-start.1
  476.1 6.2 %finish_gradients.1 = (f32[1,2,384,768]{3,2,1,0:T(8,128)}, f32[1,2,384,768]{3,2,1,0:T(8,128)}, f32[1,2,192,1536]{3,2,1,0:T(8,128)}, f32[1,96,2048]{2,1,0:T(8,128...) custom-call(bf16[4,384,384]{2,1,0:T(8,128)(2,1)} %get-tuple-element.63.gate_in, ...), custom_call_target="tpu_custom_call" | custom-call | tf_op jit(solution)/shard_map/finish_gradients/pallas_call | solution.py:1589
  482.3 1.5 copy.37
  483.8 0.0 copy-done
  483.8 0.9 copy.40
  484.7 0.0 copy-done.1
  484.7 0.9 copy.41
  (2 shorter events, 0.0 us)
Async XLA Ops:
  476.1 7.7 %copy-start = (bf16[2,128,1536]{2,1,0:T(8,128)(2,1)S(1)}, bf16[2,128,1536]{2,1,0:T(8,128)(2,1)}, u32[]{:S(2)}) copy-start(bf16[2,128,1536]{2,1,0:T(8,128)(2,1)} %get-tuple-element.47) | copy-start | bytes 2359300
  476.1 8.5 %copy-start.1 = (bf16[2,128,1536]{2,1,0:T(8,128)(2,1)S(1)}, bf16[2,128,1536]{2,1,0:T(8,128)(2,1)}, u32[]{:S(2)}) copy-start(bf16[2,128,1536]{2,1,0:T(8,128)(2,1)} %get-tuple-element.53) | copy-start | bytes 2359300

commit v4 on v3

--- a/solution.py
+++ b/solution.py
@@ -149,21 +149,27 @@
             def _():
                 self.out(way, 1, src).start()
 
-    def step(self, h, then=None):
+    def go_on(self, h):
+        for way in range(2):
+            @pl.when(self.leaves(way, h))
+            def _():
+                self.out(way, h).start()
+
+    def step(self, h, then=None, forward=True):
         for way in range(2):
             @pl.when(self.comes(way, h))
             def _():
                 self.came(way, h).wait_recv()
-                if h + 1 < self.place.nz:
+                if forward and h + 1 < self.place.nz:
                     @pl.when(self.leaves(way, h + 1))
                     def _():
                         self.out(way, h + 1).start()
                 if then is not None:
                     then(way, h)
 
-    def finish(self):
+    def finish(self, hops=None):
         for way in range(2):
-            for h in range(1, self.place.nz):
+            for h in range(1, self.place.nz) if hops is None else hops:
                 @pl.when(self.leaves(way, h))
                 def _():
                     self.out(way, h).wait_send()
@@ -173,69 +179,71 @@
     def __init__(self, place, buf, send, recv, ysend, yrecv, local):
         self.place, self.buf, self.local = place, buf, local
         self.send, self.recv, self.ysend, self.yrecv = send, recv, ysend, yrecv
-
-    def line(self, i, r):
-        return Line(self.place, lambda zz: self.buf.at[i, zz, r], self.send.at[i, r], self.recv.at[i, r])
+        self.tokens = buf.shape[3]
+        self.cut = self.tokens // 2
+
+    def rows(self, r, whole):
+        return pl.ds(0, self.tokens if whole or r == 0 else self.cut)
+
+    def line(self, i, r, whole=True):
+        rows = self.rows(r, whole)
+        return Line(self.place, lambda zz: self.buf.at[i, zz, r, rows], self.send.at[i, r], self.recv.at[i, r])
 
     def near(self, i, r, src):
         return pltpu.make_async_copy(src, self.buf.at[i, self.place.d, r], self.local.at[i, r])
 
     def across(self, i, way, h, r):
         at = self.line(i, 0).origin(way, h)
+        rest = pl.ds(self.cut, self.tokens - self.cut)
         return remote(
-            self.buf.at[i, at, 0], self.buf.at[i, at, r],
+            self.buf.at[i, at, 0, rest], self.buf.at[i, at, r, rest],
             self.ysend.at[i, way, h, r], self.yrecv.at[i, way, h, r], self.place.behind(r),
         )
 
-    def start(self, i, r, src, keep=True):
+    def start(self, i, r, src, keep=True, whole=True):
         if keep:
             self.near(i, r, src).start()
-        self.line(i, r).start(src)
-
-    def pass_one(self, i, way, h):
-        for r in range(1, self.place.ny):
-            self.across(i, way, h, r).start()
-
-    def step(self, i, h, slots):
-        for r in slots:
-            self.line(i, r).step(h)
-
-    def passes(self, i, early):
-        line, d = self.line(i, 0), self.place.d
-        for h in range(1, self.place.nz):
+        self.line(i, r, whole).start(src.at[self.rows(r, whole)])
+
+    def step(self, i, h, whole=True, forward=True):
+        for r in range(self.place.ny):
+            self.line(i, r, whole).step(h, forward=forward)
+
+    def go_on(self, i, h, whole=True):
+        for r in range(self.place.ny):
+            self.line(i, r, whole).go_on(h)
+
+    def passes(self, i, hops):
+        line = self.line(i, 0)
+        for h in hops:
             for way in range(2):
-                soon = (way == 0) | (d == 0) if h == 1 else False
-                here = soon if early else jnp.logical_not(soon)
-
-                @pl.when(line.comes(way, h) & here)
+                @pl.when(line.comes(way, h))
                 def _():
-                    self.pass_one(i, way, h)
-
-    def pass_early(self, i):
-        self.passes(i, True)
-
-    def pass_rest(self, i):
-        self.passes(i, False)
-
-    def finish(self, i, slots, kept):
+                    for r in range(1, self.place.ny):
+                        self.across(i, way, h, r).start()
+
+    def finish(self, i, kept, whole=True, hops=None):
+        for r in kept:
+            self.near(i, r, self.buf.at[i, self.place.d, r]).wait()
+        for r in range(self.place.ny):
+            self.line(i, r, whole).finish(hops)
+        if not whole:
+            self.finish_passes(i, hops)
+
+    def finish_passes(self, i, hops=None):
         g = self.place
-        for r in kept:
-            self.near(i, r, self.buf.at[i, g.d, r]).wait()
-        for r in slots:
-            self.line(i, r).finish()
         line = self.line(i, 0)
-        for r in range(g.ny):
-            if r not in slots:
-                for h in range(1, g.nz):
-                    for way in range(2):
-                        @pl.when(line.comes(way, h))
-                        def _():
-                            self.across(i, way, h, r).wait()
+        for h in range(1, g.nz) if hops is None else hops:
+            for way in range(2):
+                @pl.when(line.comes(way, h))
+                def _():
+                    for r in range(1, g.ny):
+                        self.across(i, way, h, r).wait()
 
 
 class Exchange:
-    def __init__(self, place, chunks, rows_ref, retl, retc, rety, sendl, sendc, sendy, sems):
-        self.place, self.chunks = place, chunks
+    def __init__(self, place, chunks, rows_ref, retl, retc, rety, sendl, sendc, sendy, sems, parts=1):
+        self.place, self.chunks, self.parts = place, chunks, parts
         self.rows_ref = rows_ref
         self.retl, self.retc, self.rety = retl, retc, rety
         self.sendl, self.sendc, self.sendy = sendl, sendc, sendy
@@ -252,15 +260,20 @@
             self.rows_ref.at[0, 0], self.rows_ref.at[0, 1], self.sems.cs.at[0, 0], self.sems.cr.at[0, 0], g.core
         )
 
-    def y_own(self, r, q):
+    def y_part(self, r, i):
         g = self.place
+        size = self.span // self.parts
+        rows = pl.ds(i * size, size)
         return remote(
-            self.rows_ref.at[0, 0, self.rows(q)],
-            self.rows_ref.at[r, 0, self.rows(q)],
-            self.sems.ys.at[r, q],
-            self.sems.yr.at[r, q],
+            self.rows_ref.at[0, 0, rows],
+            self.rows_ref.at[r, 0, rows],
+            self.sems.ys.at[r, i],
+            self.sems.yr.at[r, i],
             g.behind(r),
         )
+
+    def y_parts(self, r, q):
+        return [self.y_part(r, q * self.parts + p) for p in range(self.parts)]
 
     def forward(self, r, q):
         g = self.place
@@ -305,28 +318,39 @@
         )
 
     def send_own(self):
-        for q in range(self.chunks):
-            for r in range(1, self.place.ny):
-                self.y_own(r, q).start()
+        for i in range(self.chunks * self.parts):
+            self.send_part(i)
         self.core_own().start()
 
-    def run(self, local_block, remote_block, complete, meanwhile=None):
+    def send_part(self, i):
+        for r in range(1, self.place.ny):
+            self.y_part(r, i).start()
+
+    def run(self, local_block, remote_block, complete, early=None):
         ny = self.place.ny
         items = [(r, q) for q in range(self.chunks) for r in range(1, ny)]
+        def arrive(r, q):
+            for part in self.y_parts(r, q):
+                part.wait_recv()
+            self.forward(r, q).start()
+            if q == self.chunks - 1:
+                complete(r)
+
+        if items and early is not None:
+            @pl.when(early)
+            def _():
+                arrive(*items[0])
+
         self.core_own().wait_recv()
         local_block()
         self.back_local().start()
-
-        def arrive(r, q):
-            self.y_own(r, q).wait_recv()
-            self.forward(r, q).start()
-            if q == self.chunks - 1:
-                complete(r)
-
-        if items:
+        if items and early is None:
             arrive(*items[0])
-        if meanwhile is not None:
-            meanwhile()
+        if items and early is not None:
+            @pl.when(jnp.logical_not(early))
+            def _():
+                arrive(*items[0])
+
         for i, (r, q) in enumerate(items):
             self.forward(r, q).wait_recv()
             own = remote_block(r, q)
@@ -349,7 +373,8 @@
         self.back_local().wait_send()
         for q in range(self.chunks):
             for r in range(1, ny):
-                self.y_own(r, q).wait_send()
+                for part in self.y_parts(r, q):
+                    part.wait_send()
                 self.forward(r, q).wait_send()
                 self.back_core(r, q).wait_send()
                 self.back_y(r, q).wait_send()
@@ -516,9 +541,9 @@
     ny, nz, sections,
     x_ref, segc_ref, segr_ref, route_ref, small_ref, cos_ref, sin_ref,
     cot_h, wqkv_h, wout_h, wg_h, wu_h, wd_h,
-    out_ref, hin_ref, h1_ref, qkv_ref, obb_ref, xm_ref, gates_ref, zf_h,
+    out_ref, hin_ref, h1_ref, qkv_ref, obb_ref, xm_ref, gates_ref, zf_h, obp_h,
     wqkv, wout, wg, wu, wd, ob_s, hid, accl, accr, retl, retc, rety, sendl, sendc, sendy,
-    wsem, zs, zr, zys, zyr, zl, gs, gr, xs, xr, *sem_refs,
+    wsem, zs, zr, zys, zyr, zl, gs, gr, xs, xr, ps, pr, *sem_refs,
 ):
     micro, tokens, width = x_ref.shape
     hidden = wg.shape[2]
@@ -549,7 +574,7 @@
         for r in range(1, ny):
             cot_copy(r).wait_recv()
             gather.start(0, r, zf_h.at[0, g.d, r], keep=False)
-        gather.step(0, 1, every)
+        gather.step(0, 1)
 
     def hop(m, q):
         here = pl.ds(q * (tokens // HOP_CHUNKS), tokens // HOP_CHUNKS)
@@ -572,6 +597,9 @@
                 term = widen(lanes[j], 512) * eo
                 total = term if total is None else total + term
             keep(cols, total)
+
+    def partner(m, yy):
+        return remote(obb_ref.at[m, yy * 2 + 1 - g.c], obp_h.at[m, yy], ps.at[m, yy], pr.at[m, yy], g.core)
 
     def body(m, carry):
         @pl.when(g.s == 0)
@@ -638,12 +666,12 @@
             if h + 1 < nz:
                 @pl.when(last & (m == 0))
                 def _():
-                    gather.step(0, h + 1, every)
+                    gather.step(0, h + 1)
 
             if h < nz:
                 @pl.when(first & (m == 1))
                 def _():
-                    gather.step(0, h, every)
+                    gather.step(0, h)
 
         complete(0)
         move(1)
@@ -712,10 +740,15 @@
                 hop(m, q).start()
 
         ex.finish()
+        for yy in range(ny):
+            partner(m, yy).start()
         move(2)
         return carry
 
     lax.fori_loop(0, micro, body, 0)
+    for m in range(micro):
+        for yy in range(ny):
+            partner(m, yy).wait()
 
     @pl.when(g.s < sections - 1)
     def _():
@@ -726,16 +759,16 @@
     @pl.when(first)
     def _():
         for h in range(3, nz):
-            gather.step(0, h, every)
-        gather.finish(0, every, every)
+            gather.step(0, h)
+        gather.finish(0, every)
 
     @pl.when(last)
     def _():
         for r in range(1, ny):
             cot_copy(r).wait_send()
         for h in range(4, nz):
-            gather.step(0, h, every)
-        gather.finish(0, every, [0])
+            gather.step(0, h)
+        gather.finish(0, [0])
 
 
 def backward_kernel(
@@ -743,10 +776,10 @@
     cot_ref, segc_ref, segr_ref, small_ref, cos_ref, sin_ref,
     hin_ref, h1_ref, qkv_ref, gates_ref,
     xm_h, wqkv_h, wout_h, wg_h, wu_h, wd_h,
-    gin_ref, grows_ref, xab_ref, dqkv_ref, dattn_ref, gsmall_ref, zb_h,
+    gin_ref, grows_ref, xab_ref, dqkv_ref, dattn_ref, gsmall_ref, zb_h, xap_h, dqp_h, dtp_h,
     wqkv, wout, wg, wu, wd, xm_s, hid, act_s, slope_s, da_s, db_s, accl, accr, dh1_s, n_s,
     retl, retc, rety, sendl, sendc, sendy,
-    wsem, xmsem, zs, zr, zys, zyr, zl, xs, xr, *sem_refs,
+    wsem, xmsem, zs, zr, zys, zyr, zl, xs, xr, ps, pr, *sem_refs,
 ):
     micro, tokens, width = cot_ref.shape
     hidden = wg.shape[2]
@@ -773,12 +806,21 @@
             for r in every:
                 gather.start(micro + m, r, xm_h.at[m, r, 0])
             for h in range(1, nz):
-                gather.step(micro + m, h, every)
+                gather.step(micro + m, h)
 
     def hop(m, q):
         here = pl.ds(q * (tokens // HOP_CHUNKS), tokens // HOP_CHUNKS)
         return remote(gin_ref.at[m, here], grows_ref.at[m, 0, 0, here], xs.at[m, q], xr.at[m, q], g.x)
 
+    def partner(m):
+        pairs = [(dattn_ref.at[m], dtp_h.at[m]), (dqkv_ref.at[m], dqp_h.at[m])]
+        pairs += [(xab_ref.at[m, yy * 2 + 1 - g.c], xap_h.at[m, yy]) for yy in range(ny)]
+        return [remote(src, dst, ps.at[m, n], pr.at[m, n], g.core) for n, (src, dst) in enumerate(pairs)]
+
+    def late(m):
+        for h in range(3, nz):
+            gather.step(m, h, whole=False)
+
     def body(m, carry):
         load_xm = pltpu.make_async_copy(xm_h.at[m], xm_s, xmsem)
         load_xm.start()
@@ -786,33 +828,16 @@
         @pl.when(last)
         def _():
             grows_ref[m, 0, 0] = cot_ref[m]
-            gather.start(m, 0, xm_h.at[m, 0, 0])
-            for r in range(1, ny):
-                gather.near(m, r, xm_h.at[m, r, 0]).start()
-
-        @pl.when(g.s < sections - 1)
-        def _():
-            for q in range(HOP_CHUNKS):
-                hop(m, q).wait_recv()
-
-        ex = Exchange(g, BACKWARD_CHUNKS, grows_ref.at[m], retl, retc, rety, sendl, sendc, sendy, Sems(sem_refs, m))
-        ex.send_own()
-
-        def complete(r):
-            src = grows_ref.at[m, r, 0]
-
-            @pl.when(first)
-            def _():
-                if r == 0:
-                    gather.start(m, 0, src)
-                else:
-                    gather.near(m, r, src).start()
-
-        def move(hops):
-            for h in hops:
-                gather.step(m, h, [0])
-
-        complete(0)
+            for r in every:
+                gather.start(m, r, xm_h.at[m, r, 0], whole=False)
+
+        ex = Exchange(
+            g, BACKWARD_CHUNKS, grows_ref.at[m], retl, retc, rety, sendl, sendc, sendy, Sems(sem_refs, m), HOP_CHUNKS
+        )
+
+        @pl.when(last)
+        def _():
+            ex.send_own()
 
         @pl.when(m == 0)
         def _():
@@ -839,7 +864,38 @@
                     slope_s[j, r, :, :, cols] = (slope * b).astype(BF16).reshape(shape)
             return 0
 
-        lax.fori_loop(0, ny, again, 0)
+        @pl.when(first)
+        def _():
+            lax.fori_loop(0, ny, again, 0)
+
+            @pl.when(m > 0)
+            def _():
+                late(m - 1)
+
+            for q in range(HOP_CHUNKS):
+                hop(m, q).wait_recv()
+                ex.send_part(q)
+            ex.core_own().start()
+
+        def complete(r):
+            src = grows_ref.at[m, r, 0]
+
+            @pl.when(first)
+            def _():
+                gather.start(m, r, src, whole=False)
+
+        open_end = first & (m == micro - 1)
+
+        def move(hops):
+            for h in hops:
+                gather.step(m, h, whole=False)
+
+        complete(0)
+
+        @pl.when(last)
+        def _():
+            lax.fori_loop(0, ny, again, 0)
+
 
         def experts(rows, r, here, keep):
             count = 2 * (here.stop - here.start)
@@ -895,15 +951,8 @@
             experts(grows_ref[m, r, :, here, :].reshape(2 * span, width), r, here, keep)
             return lambda: accr[...]
 
-        def meanwhile():
-            move(range(1, 2))
-
-            @pl.when(first)
-            def _():
-                gather.pass_early(m)
-
-        ex.run(local_block, remote_block, complete, meanwhile)
-        move(range(2, min(3, nz)))
+        ex.run(local_block, remote_block, complete, last)
+        move(range(1, 2))
         for q in range(BACKWARD_CHUNKS):
             ex.arrived(q)
         total = accl[...] + retl[...].astype(F32)
@@ -938,11 +987,24 @@
             for load in loads[3:]:
                 load.wait()
 
+        @pl.when(jnp.logical_not(open_end))
+        def _():
+            move(range(2, min(3, nz)))
+
         @pl.when(first)
         def _():
-            move(range(3, nz))
-            gather.pass_rest(m)
-
+            gather.passes(m, range(1, 2))
+
+        @pl.when(first & (m > 0))
+        def _():
+            gather.passes(m - 1, range(3, nz))
+
+        @pl.when(first & (m < micro - 1))
+        def _():
+            gather.passes(m, range(2, min(3, nz)))
+
+        for copy in partner(m)[:1]:
+            copy.start()
         bias = mask_bias(segc_ref[m], segr_ref[m])
         bias6 = jnp.concatenate([bias] * GROUP, 0)
         qkv = qkv_ref.at[m]
@@ -997,7 +1059,18 @@
         def _():
             for q in range(HOP_CHUNKS):
                 hop(m, q).start()
+
+        for copy in partner(m)[1:]:
+            copy.start()
+
+        @pl.when(last)
+        def _():
             move(range(3, nz))
+
+        @pl.when(open_end)
+        def _():
+            for h in range(2, min(3, nz)):
+                gather.step(m, h, whole=False, forward=False)
 
         ex.finish()
         return carry
@@ -1010,31 +1083,53 @@
             for q in range(HOP_CHUNKS):
                 hop(m, q).wait_send()
 
+    few = range(1, min(3, nz))
+
     @pl.when(last)
     def _():
         for m in range(micro):
-            gather.pass_early(m)
-            gather.pass_rest(m)
+            gather.passes(m, range(1, nz))
         for m in range(1, micro):
             for r in every:
                 gather.start(micro + m, r, grows_ref.at[m, r, 0])
-            for h in range(1, nz):
-                gather.step(micro + m, h, every)
+            for h in few:
+                gather.step(micro + m, h, forward=m < micro - 1 or h < few[-1])
+            if m < micro - 1:
+                for h in range(3, nz):
+                    gather.step(micro + m, h)
+
+    for m in range(micro - 1):
+        gather.finish(m, every, whole=False)
+    for m in range(1, micro - 1):
+        gather.finish(micro + m, every)
+
+    @pl.when(first)
+    def _():
+        for r in every:
+            gather.near(micro - 1, r, grows_ref.at[micro - 1, r, 0]).wait()
+        for r in every:
+            gather.line(micro - 1, r, False).finish(few)
+        gather.finish_passes(micro - 1, range(1, 2))
+        gather.finish(2 * micro - 1, every)
+
+    @pl.when(last)
+    def _():
+        gather.finish(micro - 1, every, whole=False)
+        gather.finish(2 * micro - 1, every, hops=few)
 
     for m in range(micro):
-        gather.finish(m, [0], every)
-    for m in range(1, micro):
-        gather.finish(micro + m, every, every)
+        for copy in partner(m):
+            copy.wait()
 
 
 def tail_kernel(
     ny, nz, sections, span,
     route_ref, small_ref, gsmall_ref,
-    zf_h, zb_h, slices_h, partner_h, xab_h, obb_h, dqkv_h, dattn_h,
-    gate_ref, up_ref, down_ref, attn_ref, small_out,
+    zf_h, zb_in, slices_h, partner_h, xab_h, obb_h, dqkv_h, dattn_h, xap_h, obp_h, dqp_h, dtp_h,
+    gate_ref, up_ref, down_ref, attn_ref, small_out, zb_h,
     w4, x_s, g_s, da_s, db_s, gh_s, acc_g, acc_u, acc_d, csend, cland, dsend, dland,
     xa_s, ob_s, dq_s, dt_s, own_s, ysend, yland, zland, sm_s, smy, smz,
-    wsem, xsem, asem, as_, ar, ss, sr, cs, cr, ts, tr, ys, yr, zs, zr,
+    wsem, xsem, asem, ss, sr, cs, cr, ts, tr, ys, yr, zs, zr, hs, hr, hys, hyr, hl,
 ):
     micro, tokens, width = dqkv_h.shape[0], zf_h.shape[3], zf_h.shape[4]
     half = slices_h.shape[1]
@@ -1071,43 +1166,50 @@
         pltpu.make_async_copy(zf_h.at[0, pl.ds(0, span)], x_s, xsem.at[0]).wait()
         pltpu.make_async_copy(zf_h.at[0, pl.ds(0, span)], g_s, xsem.at[1]).wait()
 
+    acts = []
+    for m in range(micro):
+        for yy in range(ny):
+            own = yy * 2 + g.c
+            acts.append((xab_h.at[m, own], xa_s.at[yy, 0, m]))
+            acts.append((xap_h.at[m, yy], xa_s.at[yy, 1, m]))
+            acts.append((obb_h.at[m, own], ob_s.at[yy, 0, m]))
+            acts.append((obp_h.at[m, yy], ob_s.at[yy, 1, m]))
+    acts += [(dqkv_h, dq_s.at[0]), (dqp_h, dq_s.at[1]), (dattn_h, dt_s.at[0]), (dtp_h, dt_s.at[1])]
+    acts = [pltpu.make_async_copy(src, dst, asem.at[i]) for i, (src, dst) in enumerate(acts)]
+    for copy in acts:
+        copy.start()
+    g.greet(with_x=False)
+    gather = Gather(g, zb_h, hs, hr, hys, hyr, hl)
+    late_hops = range(3, nz)
+    newest = micro - 1
+
+    @pl.when(first)
+    def _():
+        gather.passes(newest, range(2, min(3, nz)))
+        for h in late_hops[:1]:
+            gather.go_on(newest, h, whole=False)
+
+    @pl.when(jnp.logical_not(first))
+    def _():
+        for h in late_hops[:1]:
+            gather.go_on(micro + newest, h)
+    sm_core = remote(gsmall_ref, sm_s.at[1], ss.at[0], sr.at[0], g.core)
+    sm_core.start()
+
+    def sm_y(r):
+        return remote(sm_s.at[0], smy.at[ny - r], ss.at[r], sr.at[ny - r], g.ahead(r))
+
+    def sm_y_arrival(r):
+        return remote(sm_s.at[0], smy.at[r], ss.at[r], sr.at[r], g.ahead(r))
+
+    def sm_z(k):
+        return remote(sm_s.at[1], smz.at[k], ss.at[ny + k], sr.at[ny + k], g.z_behind(k))
+
+    for copy in acts:
+        copy.wait()
     for copy in mine:
         copy.start()
     start_load(0)
-    g.greet(with_x=False)
-
-    away, here = [], []
-    for m in range(micro):
-        for yy in range(ny):
-            other = yy * 2 + 1 - g.c
-            own = yy * 2 + g.c
-            for n, (src, dst) in enumerate(((xab_h, xa_s), (obb_h, ob_s))):
-                i = (m * ny + yy) * 2 + n
-                away.append(remote(src.at[m, other], dst.at[yy, 1, m], as_.at[i], ar.at[i], g.core))
-                here.append(pltpu.make_async_copy(src.at[m, own], dst.at[yy, 0, m], asem.at[i]))
-    base = 2 * ny * micro
-    for n, (src, dst) in enumerate(((dqkv_h, dq_s), (dattn_h, dt_s))):
-        i = base + n
-        away.append(remote(src, dst.at[1], as_.at[i], ar.at[i], g.core))
-        here.append(pltpu.make_async_copy(src, dst.at[0], asem.at[i]))
-    for copy in away + here:
-        copy.start()
-    sm_core = remote(gsmall_ref, sm_s.at[1], ss.at[0], sr.at[0], g.core)
-    sm_core.start()
-
-    def sm_y(r):
-        return remote(sm_s.at[0], smy.at[ny - r], ss.at[r], sr.at[ny - r], g.ahead(r))
-
-    def sm_y_arrival(r):
-        return remote(sm_s.at[0], smy.at[r], ss.at[r], sr.at[r], g.ahead(r))
-
-    def sm_z(k):
-        return remote(sm_s.at[1], smz.at[k], ss.at[ny + k], sr.at[ny + k], g.z_behind(k))
-
-    for copy in away:
-        copy.wait_recv()
-    for copy in here:
-        copy.wait()
 
     count = 2 * micro * tokens
 
@@ -1203,29 +1305,51 @@
     chosen = 2 * owner + jnp.where(local < slice_h, 0, 1)
     spread = jnp.where(expert == chosen, 1.0, 0.0).astype(BF16)
 
-    blocks = span * ny
-    total_blocks = micro * groups * blocks
-    polls = (total_blocks * 7 // 16, total_blocks * 10 // 16)
+    last_group = micro * groups - 1
+    half_way = (micro * groups) // 2 - 1
+
+    def core_copy(n, k):
+        return remote(csend.at[n, k], cland.at[n, k], cs.at[n, k], cr.at[n, k], g.core)
+
+    def width_rows(k):
+        return pl.ds(pl.multiple_of(g.z_of(k) * part, part), part)
+
+    accs = (acc_g, acc_u)
+
+    def give_half(n):
+        for k in order:
+            csend[n, k] = accs[n][width_rows(k), half:both].astype(BF16)
+            core_copy(n, k).start()
+
+    def small_z():
+        for r in range(1, ny):
+            sm_y_arrival(r).wait_recv()
+        total = sm_s[0]
+        for r in range(1, ny):
+            total = total + smy[r]
+        sm_s[1] = total
+        for k in range(1, nz):
+            sm_z(k).start()
 
     def group(i, carry):
         m = lax.div(i, groups)
         wait_load()
 
         def block(b, carry):
-            k = lax.rem(i, groups) * span + lax.div(b, ny)
-            r = lax.rem(b, ny)
-            place = (lax.rem(g.y + r, ny) * 2 + g.c) * nz + k
-            x = x_s[lax.div(b, ny), r]
-            gr = g_s[lax.div(b, ny), r]
-            gates_t = chosen_gates(dot_nt(small_ref[0:ROUTER_ROWS, :], x), route_ref[place, m])
+            k = lax.rem(i, groups) * span + b
+            x = x_s[b].reshape(ny * tokens, width)
+            gr = g_s[b].reshape(ny * tokens, width)
+            places = [(lax.rem(g.y + r, ny) * 2 + g.c) * nz + k for r in range(ny)]
+            route = jnp.concatenate([route_ref[place, m] for place in places], 1)
+            gates_t = chosen_gates(dot_nt(small_ref[0:ROUTER_ROWS, :], x), route)
             high = gates_t.astype(BF16)
-            low = (gates_t - high.astype(F32)).astype(BF16)
-            here = pl.ds(pl.multiple_of(b * tokens, tokens), tokens)
+            low_part = (gates_t - high.astype(F32)).astype(BF16)
+            here = pl.ds(pl.multiple_of(b * ny * tokens, ny * tokens), ny * tokens)
             for n in range(both // tile):
                 cols = slice(n * tile, (n + 1) * tile)
                 a = dot_nt(x, w4[0, cols])
                 bb = dot_nt(x, w4[1, cols])
-                gate = dot_tn(high, spread[:, cols]) + dot_tn(low, spread[:, cols])
+                gate = dot_tn(high, spread[:, cols]) + dot_tn(low_part, spread[:, cols])
                 u = dot_nt(gr, w4[2, cols]) * gate
                 square = a * a
                 th = jnp.tanh(GELU_C * (a + GELU_A * square * a))
@@ -1235,43 +1359,90 @@
                 da_s[here, cols] = (u * slope * bb).astype(BF16)
                 db_s[here, cols] = (u * act).astype(BF16)
                 gh_s[here, cols] = ((act * bb).astype(BF16).astype(F32) * gate).astype(BF16)
-            for n, poll in enumerate(polls):
-                @pl.when(i * blocks + b == poll - 1)
-                def _():
-                    y_start(masks[n + 1])
-
-                @pl.when(i * blocks + b == poll)
-                def _():
-                    advance(masks[n])
+
+            @pl.when((i == half_way) & (b == span // 2 - 1))
+            def _():
+                advance(masks[0])
+                y_start(masks[1])
+
+            @pl.when((i == last_group) & (b == span // 2 - 1))
+            def _():
+                advance(masks[2])
+                y_start(masks[3])
 
             return carry
 
-        lax.fori_loop(0, blocks, block, 0)
-
-        def columns(n, carry):
-            cols = pl.ds(pl.multiple_of(n * 256, 256), 256)
-            x = x_s[:, :, :, cols].reshape(rows, 256)
-            acc_g[cols, :] += dot_tn(x, da_s[...])
-            acc_u[cols, :] += dot_tn(x, db_s[...])
-            acc_d[:, cols] += dot_tn(gh_s[...], g_s[:, :, :, cols].reshape(rows, 256))
-            return carry
-
-        lax.fori_loop(0, width // 256, columns, 0)
-
-        @pl.when(i + 1 < micro * groups)
+        lax.fori_loop(0, span, block, 0)
+
+        @pl.when(first & (i == newest * groups - 1))
+        def _():
+            for h in late_hops:
+                gather.step(newest, h, whole=False)
+            gather.passes(newest, late_hops)
+
+        @pl.when(jnp.logical_not(first) & (i == newest * groups - 1))
+        def _():
+            for h in late_hops:
+                gather.step(micro + newest, h)
+
+        def gate_rows(cols):
+            acc_g[cols, :] += dot_tn(x_s[:, :, :, cols].reshape(rows, 256), da_s[...])
+
+        def up_rows(cols):
+            acc_u[cols, :] += dot_tn(x_s[:, :, :, cols].reshape(rows, 256), db_s[...])
+
+        def down_rows(cols):
+            acc_d[cols, :] += dot_tn(gh_s[:, cols], g_s[...].reshape(rows, width))
+
+        def over(act, extent, size):
+            def columns(n, carry):
+                act(pl.ds(pl.multiple_of(n * size, size), size))
+                return carry
+
+            lax.fori_loop(0, extent // size, columns, 0)
+
+        over(gate_rows, width, 256)
+
+        @pl.when(i == last_group)
+        def _():
+            give_half(0)
+
+        over(up_rows, width, 256)
+
+        @pl.when(i == half_way)
+        def _():
+            advance(masks[1])
+            y_start(masks[2])
+
+        @pl.when(i == last_group)
+        def _():
+            give_half(1)
+
+        over(down_rows, both, tile)
+
+        @pl.when(first & (i == newest * groups - 1))
+        def _():
+            for r in range(ny):
+                gather.line(newest, r, False).finish(late_hops)
+            gather.finish_passes(newest, range(2, nz))
+
+        @pl.when(jnp.logical_not(first) & (i == newest * groups - 1))
+        def _():
+            gather.finish(micro + newest, [], hops=late_hops)
+
+        @pl.when(i < last_group)
         def _():
             start_load(i + 1)
 
+        @pl.when(i == half_way)
+        def _():
+            small_z()
+
         return carry
 
     lax.fori_loop(0, micro * groups, group, 0)
-    for mask in masks[3:]:
+    for mask in masks[4:]:
         y_start(mask)
-    for mask in masks[2:-1]:
-        advance(mask)
-
-    def core_copy(n, k):
-        return remote(csend.at[n, k], cland.at[n, k], cs.at[n, k], cr.at[n, k], g.core)
 
     def turn_copy(n, k):
         dst = (gate_ref, up_ref)[n]
@@ -1284,23 +1455,17 @@
         dst = (gate_ref, up_ref)[n]
         return remote(cland.at[n, k], dst.at[g.z_of(nz - k)], ts.at[n, k], tr.at[n, k], g.z_behind(k))
 
-    def width_rows(k):
-        return pl.ds(pl.multiple_of(g.z_of(k) * part, part), part)
-
     down_copy = remote(dsend, dland, cs.at[2, 0], cr.at[2, 0], g.core)
-    accs = (acc_g, acc_u)
-    for n in range(2):
-        for k in order:
-            csend[n, k] = accs[n][width_rows(k), half:both].astype(BF16)
-            core_copy(n, k).start()
     dsend[...] = acc_d[half:both, :].astype(BF16)
     down_copy.start()
-    for k in order[:-1]:
-        for n in range(2):
+    for n in range(2):
+        for k in order[:-1]:
             core_copy(n, k).wait_recv()
             total = accs[n][width_rows(k), 0:half] + cland[n, k].astype(F32)
             cland[n, k] = total.astype(BF16)
             turn_copy(n, k).start()
+    for mask in masks[3:-1]:
+        advance(mask)
     for n in range(2):
         core_copy(n, 0).wait_recv()
         cland[n, 0] = (accs[n][width_rows(0), 0:half] + cland[n, 0].astype(F32)).astype(BF16)
@@ -1310,14 +1475,7 @@
     down_near = pltpu.make_async_copy(dland, down_ref, ts.at[0, nz])
     down_near.start()
 
-    for r in range(1, ny):
-        sm_y_arrival(r).wait_recv()
-    total = sm_s[0]
-    for r in range(1, ny):
-        total = total + smy[r]
-    sm_s[1] = total
-    for k in range(1, nz):
-        sm_z(k).start()
+    total = sm_s[1]
     for k in range(1, nz):
         sm_z(k).wait_recv()
         total = total + smz[k]
@@ -1328,8 +1486,6 @@
         for n in range(2):
             turn_arrival(n, k).wait_recv()
 
-    for copy in away:
-        copy.wait_send()
     for r in range(1, ny):
         sm_y(r).wait_send()
         for k in range(nz):
@@ -1457,7 +1613,7 @@
             pltpu.VMEM((max(1, ny - 1), tokens, wide), BF16),
         ]
 
-    out, hin, h1, qkv, obb, xm, gates, zf = pl.pallas_call(
+    out, hin, h1, qkv, obb, xm, gates, zf, obp = pl.pallas_call(
         functools.partial(forward_kernel, ny, nz, sections),
         out_shape=(
             shape(micro, tokens, width),
@@ -1468,9 +1624,10 @@
             shape(micro, ny, 2, tokens, width),
             shape(micro, ny, 2, ROUTER_ROWS, tokens, dtype=F32),
             shape(1, nz, ny, tokens, width),
+            shape(micro, ny, tokens, block),
         ),
         in_specs=[VMEM] * 7 + [ANY] * 6,
-        out_specs=tuple([VMEM] * 7 + [ANY]),
+        out_specs=tuple([VMEM] * 7 + [ANY] * 2),
         scratch_shapes=weights
         + [
             pltpu.VMEM((tokens, width), BF16),
@@ -1483,6 +1640,7 @@
         + gather_sems(1)
         + [DMA((ny,)), DMA((ny,))]
         + hop_sems
+        + [DMA((micro, ny))] * 2
         + sem_shapes(micro, ny, FORWARD_CHUNKS),
         compiler_params=pltpu.CompilerParams(
             collective_id=0, has_side_effects=True, vmem_limit_bytes=60 * 2**20
@@ -1492,7 +1650,7 @@
 
     wide = width + 128
     every = (2, ny, 2, tokens, hidden)
-    gin, grows, xab, dqkv, dattn, gsmall, zb = pl.pallas_call(
+    gin, grows, xab, dqkv, dattn, gsmall, zb, xap, dqp, dtp = pl.pallas_call(
         functools.partial(backward_kernel, ny, nz, sections),
         out_shape=(
             shape(micro, tokens, width),
@@ -1502,9 +1660,12 @@
             shape(micro, tokens, width),
             shape(SMALL_ROWS, width, dtype=F32),
             shape(2 * micro, nz, ny, tokens, width),
+            shape(micro, ny, tokens, block),
+            shape(micro, tokens, qkv_width),
+            shape(micro, tokens, width),
         ),
         in_specs=[VMEM] * 10 + [ANY] * 6,
-        out_specs=tuple([VMEM] * 6 + [ANY]),
+        out_specs=tuple([VMEM] * 6 + [ANY] * 4),
         scratch_shapes=weights
         + [
             pltpu.VMEM((ny, 2, tokens, width), BF16),
@@ -1522,7 +1683,8 @@
         + [DMA((5,)), DMA]
         + gather_sems(2 * micro)
         + hop_sems
-        + sem_shapes(micro, ny, BACKWARD_CHUNKS),
+        + [DMA((micro, ny + 2))] * 2
+        + sem_shapes(micro, ny, BACKWARD_CHUNKS * HOP_CHUNKS),
         compiler_params=pltpu.CompilerParams(
             collective_id=1, has_side_effects=True, vmem_limit_bytes=62 * 2**20
         ),
@@ -1535,7 +1697,7 @@
     attn_width = qkv_width + width
     part = width // nz
     small_shape = (SMALL_ROWS, width)
-    gate_g, up_g, down_g, attn_g, small_g = pl.pallas_call(
+    gate_g, up_g, down_g, attn_g, small_g, _ = pl.pallas_call(
         functools.partial(tail_kernel, ny, nz, sections, span_z),
         out_shape=(
             shape(nz, part, half),
@@ -1543,9 +1705,11 @@
             shape(half, width),
             shape(padded, attn_width, dtype=F32),
             shape(*small_shape, dtype=F32),
+            shape(*zb.shape),
         ),
-        in_specs=[VMEM] * 3 + [ANY] * 8,
-        out_specs=tuple([ANY] * 3 + [VMEM] * 2),
+        in_specs=[VMEM] * 3 + [ANY] * 12,
+        out_specs=tuple([ANY] * 3 + [VMEM] * 2 + [ANY]),
+        input_output_aliases={4: 5},
         scratch_shapes=[
             pltpu.VMEM((3, 2 * half, width), BF16),
             pltpu.VMEM((span_z, ny, tokens, width), BF16),
@@ -1572,18 +1736,19 @@
             pltpu.VMEM((ny,) + small_shape, F32),
             pltpu.VMEM((nz,) + small_shape, F32),
             DMA((2,)), DMA((2,)),
-            DMA((2 * ny * micro + 2,)), DMA((2 * ny * micro + 2,)), DMA((2 * ny * micro + 2,)),
+            DMA((4 * ny * micro + 4,)),
             DMA((ny + nz,)), DMA((ny + nz,)),
             DMA((3, nz)), DMA((3, nz)),
             DMA((2, nz + 1)), DMA((2, nz)),
             DMA((ny, nz)), DMA((ny, nz)),
             DMA((1, nz)), DMA((1, nz)),
-        ],
+        ]
+        + gather_sems(2 * micro),
         compiler_params=pltpu.CompilerParams(
             collective_id=2, has_side_effects=True, vmem_limit_bytes=62 * 2**20
         ),
         name="weight_gradients",
-    )(routes_all, small, gsmall, zf, zb, slices, partner, xab, obb, dqkv, dattn)
+    )(routes_all, small, gsmall, zf, zb, slices, partner, xab, obb, dqkv, dattn, xap, obp, dqp, dtp)
 
     steps = 2
     finals = pl.pallas_call(

time: 490 us -> 471 us (0.961)
  Pallas kernels: 477 us -> 456 us
    pallas_call x1, Pallas kernels: 149 us -> 137 us  [per_device(): pl.pallas_call(functools.partial(tail_kernel, ny, nz, sections, span_z),...]
    pallas_call x1, Pallas kernels: 168 us -> 159 us  [per_device(): pl.pallas_call(functools.partial(backward_kernel, ny, nz, sections), out_...]
where the time goes in v4:
time: 471 us; the launch traced here: 464 us
  Pallas kernels  456 us (97%)
  local copies, waits for them, and re-layouts  7.17 us (2%)
    pallas_call x1, Pallas kernels, per_device(): pl.pallas_call(functools.partial(backward_kernel, ny, nz, sections), out_...  159 us
    pallas_call x1, Pallas kernels, per_device(): pl.pallas_call(functools.partial(tail_kernel, ny, nz, sections, span_z),...  137 us
    pallas_call x1, Pallas kernels, per_device(): pl.pallas_call(functools.partial(forward_kernel, ny, nz, sections), out_s...  77.6 us
    pallas_call x1, Pallas kernels, per_device(): pl.pallas_call(functools.partial(gather_kernel, ny, nz), out_shape=(shape...  76.7 us

profile of v4, /device:TPU:0, one launch (start us, length us, event | category | flops | bytes accessed | tf_op | source)
XLA Modules:
  0.0 464.4 jit_solution(8962987728582100489)
XLA Ops:
  0.6 0.8 copy.32
  1.4 0.8 copy.33
  2.2 0.8 copy.31
  3.0 0.1 concatenate.3
  3.1 0.6 convert_element_type.3.small_ref
  3.7 1.5 copy.34.segc_ref
  5.2 76.7 %gather_weights.1 = (bf16[32,1536]{1,0:T(8,128)(2,1)}, s32[4,4,2,4,128]{4,3,2,1,0:T(4,128)}, bf16[4,4,96,2048]{3,2,1,0:T(8,128)(2,1)}, bf16[4,4,96,1536]{3,2,1,0...) custom-call(f32[96,128]{1,0:T(8,128)} %convert_element_type.3.small_ref, ...), custom_call_target="tpu_custom_call" | custom-call | tf_op jit(solution)/shard_map/gather_weights/pallas_call | solution.py:1570
  82.0 77.6 %layers_forward.1 = (bf16[2,128,1536]{2,1,0:T(8,128)(2,1)}, bf16[2,128,1536]{2,1,0:T(8,128)(2,1)}, f32[2,128,1536]{2,1,0:T(8,128)}, bf16[2,128,2048]{2,1,0:T(8,1...) custom-call(bf16[2,128,1536]{2,1,0:T(8,128)(2,1)} %bitcast.40, ...), custom_call_target="tpu_custom_call" | custom-call | tf_op jit(solution)/shard_map/layers_forward/pallas_call | solution.py:1616
  159.6 158.6 %layers_backward.1 = (bf16[2,128,1536]{2,1,0:T(8,128)(2,1)}, bf16[2,2,2,128,1536]{4,3,2,1,0:T(8,128)(2,1)}, bf16[2,4,128,384]{3,2,1,0:T(8,128)(2,1)}, bf16[2,128...) custom-call(bf16[2,128,1536]{2,1,0:T(8,128)(2,1)} %bitcast.37, ...), custom_call_target="tpu_custom_call" | custom-call | tf_op jit(solution)/shard_map/layers_backward/pallas_call | solution.py:1653
  318.2 136.6 %weight_gradients.1 = (bf16[4,384,384]{2,1,0:T(8,128)(2,1)}, bf16[4,384,384]{2,1,0:T(8,128)(2,1)}, bf16[384,1536]{1,0:T(8,128)(2,1)}, f32[96,3584]{1,0:T(8,128)}...) custom-call(s32[16,2,4,128]{3,2,1,0:T(4,128)} %bitcast.44, ...), custom_call_target="tpu_custom_call", output_to_operand_aliasing={{5}: (4, {})} | custom-call | tf_op jit(solution)/shard_map/weight_gradients/pallas_call | solution.py:1700
  454.8 0.0 copy-start
  454.8 0.0 copy-start.1
  454.8 6.2 %finish_gradients.1 = (f32[1,2,384,768]{3,2,1,0:T(8,128)}, f32[1,2,384,768]{3,2,1,0:T(8,128)}, f32[1,2,192,1536]{3,2,1,0:T(8,128)}, f32[1,96,2048]{2,1,0:T(8,128...) custom-call(bf16[4,384,384]{2,1,0:T(8,128)(2,1)} %get-tuple-element.71.gate_in, ...), custom_call_target="tpu_custom_call" | custom-call | tf_op jit(solution)/shard_map/finish_gradients/pallas_call | solution.py:1754
  461.0 1.5 copy.38
  462.5 0.0 copy-done
  462.5 0.9 copy.42
  463.4 0.0 copy-done.1
  463.4 0.9 copy.43
  (2 shorter events, 0.0 us)
Async XLA Ops:
  454.8 7.7 %copy-start = (bf16[2,128,1536]{2,1,0:T(8,128)(2,1)S(1)}, bf16[2,128,1536]{2,1,0:T(8,128)(2,1)}, u32[]{:S(2)}) copy-start(bf16[2,128,1536]{2,1,0:T(8,128)(2,1)} %get-tuple-element.51) | copy-start | bytes 2359300
  454.8 8.5 %copy-start.1 = (bf16[2,128,1536]{2,1,0:T(8,128)(2,1)S(1)}, bf16[2,128,1536]{2,1,0:T(8,128)(2,1)}, u32[]{:S(2)}) copy-start(bf16[2,128,1536]{2,1,0:T(8,128)(2,1)} %get-tuple-element.57) | copy-start | bytes 2359300

commit v5 on v4

--- a/solution.py
+++ b/solution.py
@@ -411,10 +411,10 @@
 
 def gather_kernel(
     ny, nz,
-    small_ref, route_h, wqkv_h, wout_h, wg_h, wu_h, wd_h,
-    small_t, route_o, wqkv_o, wout_o, slices_o, partner_o,
+    small_ref, route_h, wqkv_h, wout_h, wg_h, wu_h,
+    small_t, route_o, wqkv_o, wout_o, slices_o,
     small_s, wg, wu, turned,
-    lsem, own_sem, cs, cr, ys, yr, zs, zr, sls, pls, plr,
+    lsem, own_sem, cs, cr, ys, yr, zs, zr, sls,
 ):
     g = Place(ny, nz)
     hidden, width = turned.shape[2], turned.shape[3]
@@ -471,13 +471,13 @@
                 pl.when(lines[n].comes(way, h))(pass_on)
 
     parts = []
-    here = pl.ds(pl.multiple_of(g.d * slice_h, slice_h), slice_h)
-    for i in range(3):
-        for j in range(2):
-            src = wd_h.at[j, here] if i == 2 else turned.at[i, j, here]
-            to = slice(j * slice_h, (j + 1) * slice_h)
-            parts.append(pltpu.make_async_copy(src, slices_o.at[i, to], sls.at[i, j]))
-            parts.append(remote(src, partner_o.at[i, to], pls.at[i, j], plr.at[i, j], g.core))
+    for i in range(2):
+        for t in range(nz // 2):
+            here = pl.ds(pl.multiple_of(g.z_of(2 * t) * slice_h, slice_h), slice_h)
+            for j in range(2):
+                n = 2 * t + j
+                to = slice(n * slice_h, (n + 1) * slice_h)
+                parts.append(pltpu.make_async_copy(turned.at[i, j, here], slices_o.at[i, to], sls.at[i, n]))
 
     def turn(i, j, n):
         src = (wg, wu)[i]
@@ -540,10 +540,10 @@
 def forward_kernel(
     ny, nz, sections,
     x_ref, segc_ref, segr_ref, route_ref, small_ref, cos_ref, sin_ref,
-    cot_h, wqkv_h, wout_h, wg_h, wu_h, wd_h,
-    out_ref, hin_ref, h1_ref, qkv_ref, obb_ref, xm_ref, gates_ref, zf_h, obp_h,
+    cot_h, slices_h, wqkv_h, wout_h, wg_h, wu_h, wd_h,
+    out_ref, hin_ref, h1_ref, qkv_ref, obb_ref, xm_ref, gates_ref, zf_h, obp_h, share_h,
     wqkv, wout, wg, wu, wd, ob_s, hid, accl, accr, retl, retc, rety, sendl, sendc, sendy,
-    wsem, zs, zr, zys, zyr, zl, gs, gr, xs, xr, ps, pr, *sem_refs,
+    wsem, zs, zr, zys, zyr, zl, gs, gr, xs, xr, ps, pr, hs, hr, *sem_refs,
 ):
     micro, tokens, width = x_ref.shape
     hidden = wg.shape[2]
@@ -563,6 +563,15 @@
     every = range(ny)
     first, last = g.s == 0, g.s == sections - 1
 
+    slice_h = hidden // nz
+    shares = [remote(slices_h.at[i], share_h.at[i], hs.at[i], hr.at[i], g.core) for i in range(2)]
+    for t in range(nz // 2):
+        here = pl.ds(pl.multiple_of(g.z_of(2 * t) * slice_h, slice_h), slice_h)
+        for j in range(2):
+            n = 2 * t + j
+            to = slice(n * slice_h, (n + 1) * slice_h)
+            shares.append(remote(wd_h.at[j, here], share_h.at[2, to], hs.at[2 + n], hr.at[2 + n], g.core))
+
     def cot_copy(r):
         return remote(cot_h.at[0], zf_h.at[0, g.d, r], gs.at[r], gr.at[r], g.behind(r))
 
@@ -574,6 +583,8 @@
         for r in range(1, ny):
             cot_copy(r).wait_recv()
             gather.start(0, r, zf_h.at[0, g.d, r], keep=False)
+        for copy in shares:
+            copy.start()
         gather.step(0, 1)
 
     def hop(m, q):
@@ -746,6 +757,12 @@
         return carry
 
     lax.fori_loop(0, micro, body, 0)
+
+    @pl.when(jnp.logical_not(last))
+    def _():
+        for copy in shares:
+            copy.start()
+
     for m in range(micro):
         for yy in range(ny):
             partner(m, yy).wait()
@@ -761,6 +778,9 @@
         for h in range(3, nz):
             gather.step(0, h)
         gather.finish(0, every)
+
+    for copy in shares:
+        copy.wait()
 
     @pl.when(last)
     def _():
@@ -1125,16 +1145,19 @@
 def tail_kernel(
     ny, nz, sections, span,
     route_ref, small_ref, gsmall_ref,
-    zf_h, zb_in, slices_h, partner_h, xab_h, obb_h, dqkv_h, dattn_h, xap_h, obp_h, dqp_h, dtp_h,
+    zf_h, zb_in, slices_h, partner_h, wd_h, xab_h, obb_h, dqkv_h, dattn_h, xap_h, obp_h, dqp_h, dtp_h,
     gate_ref, up_ref, down_ref, attn_ref, small_out, zb_h,
     w4, x_s, g_s, da_s, db_s, gh_s, acc_g, acc_u, acc_d, csend, cland, dsend, dland,
     xa_s, ob_s, dq_s, dt_s, own_s, ysend, yland, zland, sm_s, smy, smz,
     wsem, xsem, asem, ss, sr, cs, cr, ts, tr, ys, yr, zs, zr, hs, hr, hys, hyr, hl,
 ):
     micro, tokens, width = dqkv_h.shape[0], zf_h.shape[3], zf_h.shape[4]
-    half = slices_h.shape[1]
+    hidden = slices_h.shape[1]
+    turns = nz // 2
+    half = hidden // turns
     slice_h = half // 2
     both = 2 * half
+    wide = 2 * hidden
     tile = 256 if both % 256 == 0 else 128
     qkv_width = dqkv_h.shape[2]
     shard = width // (2 * ny * nz)
@@ -1143,8 +1166,17 @@
     groups = nz // span
     g = Place(ny, nz)
     first = g.s == 0
-    mine = [pltpu.make_async_copy(src, w4.at[:, i * half : (i + 1) * half], wsem.at[i])
-            for i, src in enumerate((slices_h, partner_h))]
+    pieces = []
+    for t in range(turns):
+        own, other = 2 * t, 2 * t + 1
+        rows_t = slice(t * half, (t + 1) * half)
+        pieces.append((slices_h.at[:, rows_t], w4.at[0:2, own * half : (own + 1) * half]))
+        pieces.append((partner_h.at[:, rows_t], w4.at[:, other * half : (other + 1) * half]))
+        here = pl.ds(pl.multiple_of(g.z_of(2 * t) * slice_h, slice_h), slice_h)
+        for j in range(2):
+            at = own * half + j * slice_h
+            pieces.append((wd_h.at[j, here], w4.at[2, at : at + slice_h]))
+    mine = [pltpu.make_async_copy(src, dst, wsem.at[n]) for n, (src, dst) in enumerate(pieces)]
 
     def load(i):
         m, k = lax.div(i, groups), pl.ds(lax.rem(i, groups) * span, span)
@@ -1286,10 +1318,7 @@
                 total = total + yland[r - 1, zi, :, cols].astype(F32)
             for b in range(low(mask)):
                 total = total + zland[landings.index((mask, b)), :, cols].astype(F32)
-            if mask:
-                own_s[zi, :, cols] = total.astype(BF16)
-            else:
-                attn_ref[:, cols] = total
+            own_s[zi, :, cols] = total.astype(BF16)
         if mask:
             z_copy(mask).start()
 
@@ -1298,28 +1327,57 @@
     acc_g[...] = jnp.zeros_like(acc_g)
     acc_u[...] = jnp.zeros_like(acc_u)
     acc_d[...] = jnp.zeros_like(acc_d)
-    column = lax.broadcasted_iota(jnp.int32, (ROUTER_ROWS, both), 1)
-    expert = lax.broadcasted_iota(jnp.int32, (ROUTER_ROWS, both), 0)
+    column = lax.rem(lax.broadcasted_iota(jnp.int32, (ROUTER_ROWS, wide), 1), both)
+    expert = lax.broadcasted_iota(jnp.int32, (ROUTER_ROWS, wide), 0)
     owner = jnp.where(column < half, g.e, 2 * g.y + 1 - g.c)
     local = jnp.where(column < half, column, column - half)
     chosen = 2 * owner + jnp.where(local < slice_h, 0, 1)
     spread = jnp.where(expert == chosen, 1.0, 0.0).astype(BF16)
 
     last_group = micro * groups - 1
-    half_way = (micro * groups) // 2 - 1
-
-    def core_copy(n, k):
-        return remote(csend.at[n, k], cland.at[n, k], cs.at[n, k], cr.at[n, k], g.core)
-
-    def width_rows(k):
-        return pl.ds(pl.multiple_of(g.z_of(k) * part, part), part)
-
     accs = (acc_g, acc_u)
+    parity = lax.rem(g.d, 2)
+
+    def rows_of(x):
+        at = parity if x == 0 else 1 - parity
+        return pl.ds(pl.multiple_of(at * part, part), part)
+
+    def cols_of(t, o):
+        return slice((2 * t + o) * half, (2 * t + o + 1) * half)
+
+    def core_copy(n, x, t):
+        return remote(csend.at[n, x, t], cland.at[n, x, t], cs.at[n, x * turns + t], cr.at[n, x * turns + t], g.core)
 
     def give_half(n):
-        for k in order:
-            csend[n, k] = accs[n][width_rows(k), half:both].astype(BF16)
-            core_copy(n, k).start()
+        for x in (1, 0):
+            for t in range(turns):
+                csend[n, x, t] = accs[n][rows_of(x), cols_of(t, 1)].astype(BF16)
+                core_copy(n, x, t).start()
+
+    def turn_copy(n, t):
+        dst = (gate_ref, up_ref)[n]
+        device = (g.s, g.e, flipped(1))
+        return remote(cland.at[n, 1, t], dst.at[g.z_of(2 * t)], ts.at[n, t], tr.at[n, t], device)
+
+    def turn_arrival(n, t):
+        dst = (gate_ref, up_ref)[n]
+        device = (g.s, g.e, flipped(1))
+        return remote(cland.at[n, 1, t], dst.at[lax.rem(flipped(1) + 2 * t, nz)], ts.at[n, t], tr.at[n, t], device)
+
+    def turn_near(n, t):
+        dst = (gate_ref, up_ref)[n]
+        return pltpu.make_async_copy(cland.at[n, 0, t], dst.at[g.z_of(2 * t)], ts.at[n, turns + t])
+
+    def take_half(n):
+        for x in (1, 0):
+            for t in range(turns):
+                core_copy(n, x, t).wait_recv()
+                total = accs[n][rows_of(x), cols_of(t, 0)] + cland[n, x, t].astype(F32)
+                cland[n, x, t] = total.astype(BF16)
+                if x:
+                    turn_copy(n, t).start()
+                else:
+                    turn_near(n, t).start()
 
     def small_z():
         for r in range(1, ny):
@@ -1345,7 +1403,7 @@
             high = gates_t.astype(BF16)
             low_part = (gates_t - high.astype(F32)).astype(BF16)
             here = pl.ds(pl.multiple_of(b * ny * tokens, ny * tokens), ny * tokens)
-            for n in range(both // tile):
+            for n in range(wide // tile):
                 cols = slice(n * tile, (n + 1) * tile)
                 a = dot_nt(x, w4[0, cols])
                 bb = dot_nt(x, w4[1, cols])
@@ -1358,18 +1416,8 @@
                 slope = hf + (0.5 * GELU_C) * a * (1.0 - th * th) * (1.0 + (3.0 * GELU_A) * square)
                 da_s[here, cols] = (u * slope * bb).astype(BF16)
                 db_s[here, cols] = (u * act).astype(BF16)
-                gh_s[here, cols] = ((act * bb).astype(BF16).astype(F32) * gate).astype(BF16)
-
-            @pl.when((i == half_way) & (b == span // 2 - 1))
-            def _():
-                advance(masks[0])
-                y_start(masks[1])
-
-            @pl.when((i == last_group) & (b == span // 2 - 1))
-            def _():
-                advance(masks[2])
-                y_start(masks[3])
-
+                if (n + 1) * tile <= both:
+                    gh_s[here, cols] = ((act * bb).astype(BF16).astype(F32) * gate).astype(BF16)
             return carry
 
         lax.fori_loop(0, span, block, 0)
@@ -1385,40 +1433,43 @@
             for h in late_hops:
                 gather.step(micro + newest, h)
 
-        def gate_rows(cols):
-            acc_g[cols, :] += dot_tn(x_s[:, :, :, cols].reshape(rows, 256), da_s[...])
-
-        def up_rows(cols):
-            acc_u[cols, :] += dot_tn(x_s[:, :, :, cols].reshape(rows, 256), db_s[...])
-
-        def down_rows(cols):
-            acc_d[cols, :] += dot_tn(gh_s[:, cols], g_s[...].reshape(rows, width))
-
-        def over(act, extent, size):
+        size = 256 if (2 * part) % 256 == 0 else 128
+        base = lax.div(g.d, 2) * (2 * part)
+
+        def x_columns(n):
+            cols = pl.ds(pl.multiple_of(base + n * size, size), size)
+            return x_s[:, :, :, cols].reshape(rows, size)
+
+        def sum_rows(acc, right):
             def columns(n, carry):
-                act(pl.ds(pl.multiple_of(n * size, size), size))
+                at = pl.ds(pl.multiple_of(n * size, size), size)
+                acc[at, :] += dot_tn(x_columns(n), right[...])
                 return carry
 
-            lax.fori_loop(0, extent // size, columns, 0)
-
-        over(gate_rows, width, 256)
+            lax.fori_loop(0, 2 * part // size, columns, 0)
+
+        def down():
+            def columns(n, carry):
+                cols = pl.ds(pl.multiple_of(n * tile, tile), tile)
+                acc_d[cols, :] += dot_tn(gh_s[:, cols], g_s[...].reshape(rows, width))
+                return carry
+
+            lax.fori_loop(0, both // tile, columns, 0)
+
+        sum_rows(acc_g, da_s)
 
         @pl.when(i == last_group)
         def _():
             give_half(0)
 
-        over(up_rows, width, 256)
-
-        @pl.when(i == half_way)
-        def _():
-            advance(masks[1])
-            y_start(masks[2])
+        sum_rows(acc_u, db_s)
 
         @pl.when(i == last_group)
         def _():
             give_half(1)
-
-        over(down_rows, both, tile)
+            take_half(0)
+
+        down()
 
         @pl.when(first & (i == newest * groups - 1))
         def _():
@@ -1434,42 +1485,27 @@
         def _():
             start_load(i + 1)
 
-        @pl.when(i == half_way)
-        def _():
-            small_z()
+        for n in range(min(3, last_group)):
+            @pl.when(i == n)
+            def _():
+                advance(masks[n])
+                y_start(masks[n + 1])
+                if n == 1:
+                    small_z()
 
         return carry
 
     lax.fori_loop(0, micro * groups, group, 0)
-    for mask in masks[4:]:
+    polled = min(3, last_group)
+    for mask in masks[polled + 1 :]:
         y_start(mask)
-
-    def turn_copy(n, k):
-        dst = (gate_ref, up_ref)[n]
-        return remote(cland.at[n, k], dst.at[g.d], ts.at[n, k], tr.at[n, k], g.z_ahead(k))
-
-    def turn_near(n):
-        return pltpu.make_async_copy(cland.at[n, 0], (gate_ref, up_ref)[n].at[g.d], ts.at[n, 0])
-
-    def turn_arrival(n, k):
-        dst = (gate_ref, up_ref)[n]
-        return remote(cland.at[n, k], dst.at[g.z_of(nz - k)], ts.at[n, k], tr.at[n, k], g.z_behind(k))
 
     down_copy = remote(dsend, dland, cs.at[2, 0], cr.at[2, 0], g.core)
     dsend[...] = acc_d[half:both, :].astype(BF16)
     down_copy.start()
-    for n in range(2):
-        for k in order[:-1]:
-            core_copy(n, k).wait_recv()
-            total = accs[n][width_rows(k), 0:half] + cland[n, k].astype(F32)
-            cland[n, k] = total.astype(BF16)
-            turn_copy(n, k).start()
-    for mask in masks[3:-1]:
+    take_half(1)
+    for mask in masks[polled:-1]:
         advance(mask)
-    for n in range(2):
-        core_copy(n, 0).wait_recv()
-        cland[n, 0] = (accs[n][width_rows(0), 0:half] + cland[n, 0].astype(F32)).astype(BF16)
-        turn_near(n).start()
     down_copy.wait_recv()
     dland[...] = (acc_d[0:half, :] + dland[...].astype(F32)).astype(BF16)
     down_near = pltpu.make_async_copy(dland, down_ref, ts.at[0, nz])
@@ -1482,9 +1518,11 @@
     small_out[...] = total
 
     advance(0)
-    for k in range(1, nz):
+    attn_near = pltpu.make_async_copy(own_s.at[g.d], attn_ref, ts.at[1, nz])
+    attn_near.start()
+    for t in range(turns):
         for n in range(2):
-            turn_arrival(n, k).wait_recv()
+            turn_arrival(n, t).wait_recv()
 
     for r in range(1, ny):
         sm_y(r).wait_send()
@@ -1493,15 +1531,15 @@
     for k in range(1, nz):
         sm_z(k).wait_send()
         z_copy(k).wait_send()
-        for n in range(2):
-            turn_copy(n, k).wait_send()
     for n in range(2):
-        for k in range(nz):
-            core_copy(n, k).wait_send()
+        for t in range(turns):
+            turn_copy(n, t).wait_send()
+            turn_near(n, t).wait()
+            for x in range(2):
+                core_copy(n, x, t).wait_send()
     down_copy.wait_send()
-    for n in range(2):
-        turn_near(n).wait()
     down_near.wait()
+    attn_near.wait()
 
 
 def finish_kernel(nz, experts, gate_in, up_in, down_in, attn_in, small_in, gate, up, down, qkv, out, router, again, mgain):
@@ -1512,8 +1550,8 @@
             dst[0, j] = jnp.concatenate([src[z, :, cols].astype(F32) for z in range(nz)], 1)
     down[0, 0] = down_in[...].astype(F32)
     shard, split = qkv.shape[1], qkv.shape[2]
-    qkv[0] = attn_in[0:shard, 0:split]
-    out[0] = attn_in[0:shard, split:]
+    qkv[0] = attn_in[0:shard, 0:split].astype(F32)
+    out[0] = attn_in[0:shard, split:].astype(F32)
     rows, width = small_in.shape
     base = (lax.axis_index("expert") * nz + lax.axis_index("dp")) * shard
     at = lax.broadcasted_iota(jnp.int32, (width, 128), 0)
@@ -1567,18 +1605,17 @@
         return jax.ShapeDtypeStruct(dims, dtype)
 
     grid_sems = [DMA((4, 2, nz, ny)) for _ in range(4)]
-    small, routes_all, wqkv, wout, slices, partner = pl.pallas_call(
+    small, routes_all, wqkv, wout, slices = pl.pallas_call(
         functools.partial(gather_kernel, ny, nz),
         out_shape=(
             shape(SMALL_ROWS, width),
             shape(ne, nz, *own_routes.shape, dtype=jnp.int32),
             shape(ne, nz, shard, qkv_width),
             shape(ne, nz, shard, width),
-            shape(3, half, width),
-            shape(3, half, width),
+            shape(2, hidden, width),
         ),
-        in_specs=[VMEM] + [ANY] * 6,
-        out_specs=tuple([VMEM] + [ANY] * 5),
+        in_specs=[VMEM] + [ANY] * 5,
+        out_specs=tuple([VMEM] + [ANY] * 4),
         scratch_shapes=[
             pltpu.VMEM((ne, nz, shard, 128), F32),
             pltpu.VMEM(wg.shape, BF16),
@@ -1587,12 +1624,12 @@
             DMA((2,)), DMA((4,)),
         ]
         + grid_sems
-        + [DMA((4, 2, nz)), DMA((4, 2, nz)), DMA((3, 2)), DMA((3, 2)), DMA((3, 2))],
+        + [DMA((4, 2, nz)), DMA((4, 2, nz)), DMA((2, nz))],
         compiler_params=pltpu.CompilerParams(
             collective_id=3, has_side_effects=True, vmem_limit_bytes=60 * 2**20
         ),
         name="gather_weights",
-    )(small, own_routes, w_qkv[0], w_out[0], wg, wu, wd)
+    )(small, own_routes, w_qkv[0], w_out[0], wg, wu)
     wqkv = wqkv.reshape(width, qkv_width)
     wout = wout.reshape(width, width)
     routes_all = routes_all.reshape((ne * nz,) + own_routes.shape)
@@ -1613,7 +1650,7 @@
             pltpu.VMEM((max(1, ny - 1), tokens, wide), BF16),
         ]
 
-    out, hin, h1, qkv, obb, xm, gates, zf, obp = pl.pallas_call(
+    out, hin, h1, qkv, obb, xm, gates, zf, obp, partner = pl.pallas_call(
         functools.partial(forward_kernel, ny, nz, sections),
         out_shape=(
             shape(micro, tokens, width),
@@ -1625,9 +1662,10 @@
             shape(micro, ny, 2, ROUTER_ROWS, tokens, dtype=F32),
             shape(1, nz, ny, tokens, width),
             shape(micro, ny, tokens, block),
+            shape(3, hidden, width),
         ),
-        in_specs=[VMEM] * 7 + [ANY] * 6,
-        out_specs=tuple([VMEM] * 7 + [ANY] * 2),
+        in_specs=[VMEM] * 7 + [ANY] * 7,
+        out_specs=tuple([VMEM] * 7 + [ANY] * 3),
         scratch_shapes=weights
         + [
             pltpu.VMEM((tokens, width), BF16),
@@ -1641,12 +1679,13 @@
         + [DMA((ny,)), DMA((ny,))]
         + hop_sems
         + [DMA((micro, ny))] * 2
+        + [DMA((nz + 2,))] * 2
         + sem_shapes(micro, ny, FORWARD_CHUNKS),
         compiler_params=pltpu.CompilerParams(
             collective_id=0, has_side_effects=True, vmem_limit_bytes=60 * 2**20
         ),
         name="layers_forward",
-    )(x, segc, segr, routes_all, small, cos, sin, cot, wqkv, wout, wg, wu, wd)
+    )(x, segc, segr, routes_all, small, cos, sin, cot, slices, wqkv, wout, wg, wu, wd)
 
     wide = width + 128
     every = (2, ny, 2, tokens, hidden)
@@ -1691,7 +1730,7 @@
         name="layers_backward",
     )(cot, segc, segr, small, cos, sin, hin, h1, qkv, gates, xm, wqkv, wout, wg, wu, wd)
 
-    span_z = max(1, min(nz, 1024 // (ny * tokens)))
+    span_z = max(1, min(nz, 512 // (ny * tokens)))
     rows = span_z * ny * tokens
     padded = -(-shard // 16) * 16
     attn_width = qkv_width + width
@@ -1703,25 +1742,25 @@
             shape(nz, part, half),
             shape(nz, part, half),
             shape(half, width),
-            shape(padded, attn_width, dtype=F32),
+            shape(padded, attn_width),
             shape(*small_shape, dtype=F32),
             shape(*zb.shape),
         ),
-        in_specs=[VMEM] * 3 + [ANY] * 12,
-        out_specs=tuple([ANY] * 3 + [VMEM] * 2 + [ANY]),
+        in_specs=[VMEM] * 3 + [ANY] * 13,
+        out_specs=tuple([ANY] * 4 + [VMEM] + [ANY]),
         input_output_aliases={4: 5},
         scratch_shapes=[
-            pltpu.VMEM((3, 2 * half, width), BF16),
+            pltpu.VMEM((3, 2 * hidden, width), BF16),
             pltpu.VMEM((span_z, ny, tokens, width), BF16),
             pltpu.VMEM((span_z, ny, tokens, width), BF16),
+            pltpu.VMEM((rows, 2 * hidden), BF16),
+            pltpu.VMEM((rows, 2 * hidden), BF16),
             pltpu.VMEM((rows, 2 * half), BF16),
-            pltpu.VMEM((rows, 2 * half), BF16),
-            pltpu.VMEM((rows, 2 * half), BF16),
-            pltpu.VMEM((width, 2 * half), F32),
-            pltpu.VMEM((width, 2 * half), F32),
+            pltpu.VMEM((2 * part, 2 * hidden), F32),
+            pltpu.VMEM((2 * part, 2 * hidden), F32),
             pltpu.VMEM((2 * half, width), F32),
-            pltpu.VMEM((2, nz, part, half), BF16),
-            pltpu.VMEM((2, nz, part, half), BF16),
+            pltpu.VMEM((2, 2, nz // 2, part, half), BF16),
+            pltpu.VMEM((2, 2, nz // 2, part, half), BF16),
             pltpu.VMEM((half, width), BF16),
             pltpu.VMEM((half, width), BF16),
             pltpu.VMEM((ny, 2, micro, tokens, block), BF16),
@@ -1735,7 +1774,7 @@
             pltpu.VMEM((2,) + small_shape, F32),
             pltpu.VMEM((ny,) + small_shape, F32),
             pltpu.VMEM((nz,) + small_shape, F32),
-            DMA((2,)), DMA((2,)),
+            DMA((2 * nz,)), DMA((2,)),
             DMA((4 * ny * micro + 4,)),
             DMA((ny + nz,)), DMA((ny + nz,)),
             DMA((3, nz)), DMA((3, nz)),
@@ -1748,7 +1787,7 @@
             collective_id=2, has_side_effects=True, vmem_limit_bytes=62 * 2**20
         ),
         name="weight_gradients",
-    )(routes_all, small, gsmall, zf, zb, slices, partner, xab, obb, dqkv, dattn, xap, obp, dqp, dtp)
+    )(routes_all, small, gsmall, zf, zb, slices, partner, wd, xab, obb, dqkv, dattn, xap, obp, dqp, dtp)
 
     steps = 2
     finals = pl.pallas_call(

time: 471 us -> 450 us (0.955)
  Pallas kernels: 456 us -> 437 us
    pallas_call x1, Pallas kernels: 137 us -> 118 us  [per_device(): pl.pallas_call(functools.partial(tail_kernel, ny, nz, sections, span_z),...]
where the time goes in v5:
time: 450 us; the launch traced here: 446 us
  Pallas kernels  437 us (97%)
  local copies, waits for them, and re-layouts  7.17 us (2%)
    pallas_call x1, Pallas kernels, per_device(): pl.pallas_call(functools.partial(backward_kernel, ny, nz, sections), out_...  159 us
    pallas_call x1, Pallas kernels, per_device(): pl.pallas_call(functools.partial(tail_kernel, ny, nz, sections, span_z),...  118 us
    pallas_call x1, Pallas kernels, per_device(): pl.pallas_call(functools.partial(forward_kernel, ny, nz, sections), out_s...  77.7 us
    pallas_call x1, Pallas kernels, per_device(): pl.pallas_call(functools.partial(gather_kernel, ny, nz), out_shape=(shape...  76.6 us

profile of v5, /device:TPU:0, one launch (start us, length us, event | category | flops | bytes accessed | tf_op | source)
XLA Modules:
  0.0 445.6 jit_solution(1909596656083174463)
XLA Ops:
  0.6 0.8 copy.32
  1.4 0.8 copy.33
  2.2 0.8 copy.31
  3.0 0.1 concatenate.3
  3.1 0.6 convert_element_type.3.small_ref
  3.7 1.5 copy.34.segc_ref
  5.2 76.6 %gather_weights.1 = (bf16[32,1536]{1,0:T(8,128)(2,1)}, s32[4,4,2,4,128]{4,3,2,1,0:T(4,128)}, bf16[4,4,96,2048]{3,2,1,0:T(8,128)(2,1)}, bf16[4,4,96,1536]{3,2,1,0:T(8,128)(2,1)}, bf16[2,768,1536]{2,1,0:T(8,128)(2,1)}) custom-call(f32[96,128]{1,0:T(8,128)} %convert_element_type.3.small_ref, s32[2,4,128]{2,1,0:T(4,128)} %bitcast.47, bf16[96,2048]{1,0:T(8,128)(2,1)} %bitcast.41, ...), custom_call_target="tpu_custom_call" | custom-call | tf_op jit(solution)/shard_map/gather_weights/pallas_call | solution.py:1608
  81.8 77.7 %layers_forward.1 = (bf16[2,128,1536]{2,1,0:T(8,128)(2,1)}, bf16[2,128,1536]{2,1,0:T(8,128)(2,1)}, f32[2,128,1536]{2,1,0:T(8,128)}, bf16[2,128,2048]{2,1,0:T(8,1...) custom-call(bf16[2,128,1536]{2,1,0:T(8,128)(2,1)} %bitcast.40, ...), custom_call_target="tpu_custom_call" | custom-call | tf_op jit(solution)/shard_map/layers_forward/pallas_call | solution.py:1653
  159.5 158.5 %layers_backward.1 = (bf16[2,128,1536]{2,1,0:T(8,128)(2,1)}, bf16[2,2,2,128,1536]{4,3,2,1,0:T(8,128)(2,1)}, bf16[2,4,128,384]{3,2,1,0:T(8,128)(2,1)}, bf16[2,128...) custom-call(bf16[2,128,1536]{2,1,0:T(8,128)(2,1)} %bitcast.37, ...), custom_call_target="tpu_custom_call" | custom-call | tf_op jit(solution)/shard_map/layers_backward/pallas_call | solution.py:1692
  318.1 118.2 %weight_gradients.1 = (bf16[4,384,384]{2,1,0:T(8,128)(2,1)}, bf16[4,384,384]{2,1,0:T(8,128)(2,1)}, bf16[384,1536]{1,0:T(8,128)(2,1)}, bf16[96,3584]{1,0:T(8,128)...) custom-call(s32[16,2,4,128]{3,2,1,0:T(4,128)} %bitcast.44, ...), custom_call_target="tpu_custom_call", output_to_operand_aliasing={{5}: (4, {})} | custom-call | tf_op jit(solution)/shard_map/weight_gradients/pallas_call | solution.py:1739
  436.2 0.0 copy-start
  436.2 0.0 copy-start.1
  436.2 6.0 %finish_gradients.1 = (f32[1,2,384,768]{3,2,1,0:T(8,128)}, f32[1,2,384,768]{3,2,1,0:T(8,128)}, f32[1,2,192,1536]{3,2,1,0:T(8,128)}, f32[1,96,2048]{2,1,0:T(8,128...) custom-call(bf16[4,384,384]{2,1,0:T(8,128)(2,1)} %get-tuple-element.71.gate_in, ...), custom_call_target="tpu_custom_call" | custom-call | tf_op jit(solution)/shard_map/finish_gradients/pallas_call | solution.py:1793
  442.2 1.5 copy.38
  443.7 0.0 copy-done
  443.7 0.9 copy.42
  444.6 0.0 copy-done.1
  444.6 0.9 copy.43
  (2 shorter events, 0.0 us)
Async XLA Ops:
  436.2 7.5 %copy-start = (bf16[2,128,1536]{2,1,0:T(8,128)(2,1)S(1)}, bf16[2,128,1536]{2,1,0:T(8,128)(2,1)}, u32[]{:S(2)}) copy-start(bf16[2,128,1536]{2,1,0:T(8,128)(2,1)} %get-tuple-element.52) | copy-start | bytes 2359300
  436.2 8.4 %copy-start.1 = (bf16[2,128,1536]{2,1,0:T(8,128)(2,1)S(1)}, bf16[2,128,1536]{2,1,0:T(8,128)(2,1)}, u32[]{:S(2)}) copy-start(bf16[2,128,1536]{2,1,0:T(8,128)(2,1)} %get-tuple-element.58) | copy-start | bytes 2359300

commit v6 on v5

--- a/solution.py
+++ b/solution.py
@@ -423,27 +423,42 @@
     for copy in loads:
         copy.start()
     g.greet(with_x=False)
-    arrays = ((small_ref, small_s), (route_h, route_o), (wqkv_h, wqkv_o), (wout_h, wout_o))
+    split = width * 2 // 3
+    arrays = (
+        (small_ref, lambda e, zz: small_s.at[e, zz]),
+        (route_h, lambda e, zz: route_o.at[e, zz]),
+        (wqkv_h, lambda e, zz: wqkv_o.at[e, zz]),
+        (wout_h.at[:, 0:split], lambda e, zz: wout_o.at[e, zz, :, 0:split]),
+        (wout_h.at[:, split:width], lambda e, zz: wout_o.at[e, zz, :, split:width]),
+    )
     count = len(arrays)
+    turned_way = count - 1
+    plain = range(turned_way)
 
     def near(n):
-        src, dst = arrays[n]
-        return pltpu.make_async_copy(src, dst.at[g.e, g.d], own_sem.at[n])
-
-    lines = [Line(g, lambda zz, dst=dst: dst.at[g.e, zz], zs.at[n], zr.at[n]) for n, (_, dst) in enumerate(arrays)]
+        src, slot = arrays[n]
+        return pltpu.make_async_copy(src, slot(g.e, g.d), own_sem.at[n])
+
+    lines = [
+        Line(g, lambda zz, slot=slot: slot(g.e, zz), zs.at[n, 0], zr.at[n, 0]) for n, (_, slot) in enumerate(arrays)
+    ]
+    turned_lines = [
+        Line(g, lambda zz, r=r: arrays[turned_way][1](g.pack(r, False), zz), zs.at[turned_way, r], zr.at[turned_way, r])
+        for r in range(ny)
+    ]
 
     def along_y(n, way, h, r):
-        src, dst = arrays[n]
-        at = dst.at[g.e, lines[n].origin(way, h)]
+        src, slot = arrays[n]
+        at = slot(g.e, lines[n].origin(way, h))
         return remote(src if h == 0 else at, at, ys.at[n, way, h, r], yr.at[n, way, h, r], g.behind(r))
 
     def to_core(n, way, h, r):
-        src, dst = arrays[n]
-        at = dst.at[g.pack(r, False), lines[n].origin(way, h)]
+        src, slot = arrays[n]
+        at = slot(g.pack(r, False), lines[n].origin(way, h))
         own = h == 0 and r == 0
         return remote(src if own else at, at, cs.at[n, way, h, r], cr.at[n, way, h, r], g.core)
 
-    for n in range(count):
+    for n in [turned_way] + list(plain):
         for r in range(1, ny):
             along_y(n, 0, 0, r).start()
         lines[n].start(arrays[n][0])
@@ -451,6 +466,11 @@
         to_core(n, 0, 0, 0).start()
 
     def got_z(n, h):
+        if n == turned_way:
+            for r, line in enumerate(turned_lines):
+                line.step(h, lambda way, h, r=r: to_core(n, way, h, r).start())
+            return
+
         def then(way, h):
             for r in range(1, ny):
                 along_y(n, way, h, r).start()
@@ -464,6 +484,8 @@
                 for r in range(1, ny):
                     along_y(n, way, h, r).wait_recv()
                     to_core(n, way, h, r).start()
+                    if n == turned_way:
+                        turned_lines[r].start(arrays[n][1](g.pack(r, False), g.d))
 
             if h == 0:
                 pass_on()
@@ -489,11 +511,13 @@
     turns = [(i, j, n) for i in range(2) for j in range(2) for n in range(hidden // 256)]
 
     z_items = [(n, h) for h in range(1, nz) for n in range(count)]
-    y_items = [(n, 0) for n in range(count)] + z_items
+    y_items = [(n, h) for h in range(nz) for n in plain]
     done = 0
     for i, item in enumerate(z_items):
+        if item == (2, 1):
+            got_y(turned_way, 0)
         got_z(*item)
-        if i % 2 == 1 or i >= count:
+        if (i % 2 == 1 or i >= count) and item[0] != turned_way:
             got_y(*y_items[done])
             done += 1
         for piece in turns[:2]:
@@ -522,7 +546,7 @@
     def sent(n, way, h):
         for r in range(ny):
             to_core(n, way, h, r).wait_send()
-            if r:
+            if r and (h == 0 or n != turned_way):
                 along_y(n, way, h, r).wait_send()
 
     each(arrived)
@@ -531,7 +555,7 @@
     gathered = small_s[...].reshape(width, small_s.shape[3])
     small_t[...] = jnp.transpose(gathered)[0:SMALL_ROWS].astype(BF16)
     each(sent)
-    for line in lines:
+    for line in lines[:turned_way] + turned_lines:
         line.finish()
     for copy in started:
         copy.wait()
@@ -1229,13 +1253,13 @@
     sm_core.start()
 
     def sm_y(r):
-        return remote(sm_s.at[0], smy.at[ny - r], ss.at[r], sr.at[ny - r], g.ahead(r))
+        return remote(sm_s.at[0], smy.at[ny - r - 1], ss.at[r], sr.at[ny - r], g.ahead(r))
 
     def sm_y_arrival(r):
-        return remote(sm_s.at[0], smy.at[r], ss.at[r], sr.at[r], g.ahead(r))
+        return remote(sm_s.at[0], smy.at[r - 1], ss.at[r], sr.at[r], g.ahead(r))
 
     def sm_z(k):
-        return remote(sm_s.at[1], smz.at[k], ss.at[ny + k], sr.at[ny + k], g.z_behind(k))
+        return remote(sm_s.at[1], smz.at[k - 1], ss.at[ny + k], sr.at[ny + k], g.z_behind(k))
 
     for copy in acts:
         copy.wait()
@@ -1333,6 +1357,7 @@
     local = jnp.where(column < half, column, column - half)
     chosen = 2 * owner + jnp.where(local < slice_h, 0, 1)
     spread = jnp.where(expert == chosen, 1.0, 0.0).astype(BF16)
+    spread = jnp.concatenate([spread, spread], 0)
 
     last_group = micro * groups - 1
     accs = (acc_g, acc_u)
@@ -1384,7 +1409,7 @@
             sm_y_arrival(r).wait_recv()
         total = sm_s[0]
         for r in range(1, ny):
-            total = total + smy[r]
+            total = total + smy[r - 1]
         sm_s[1] = total
         for k in range(1, nz):
             sm_z(k).start()
@@ -1401,13 +1426,13 @@
             route = jnp.concatenate([route_ref[place, m] for place in places], 1)
             gates_t = chosen_gates(dot_nt(small_ref[0:ROUTER_ROWS, :], x), route)
             high = gates_t.astype(BF16)
-            low_part = (gates_t - high.astype(F32)).astype(BF16)
+            gates_b = jnp.concatenate([high, (gates_t - high.astype(F32)).astype(BF16)], 0)
             here = pl.ds(pl.multiple_of(b * ny * tokens, ny * tokens), ny * tokens)
             for n in range(wide // tile):
                 cols = slice(n * tile, (n + 1) * tile)
                 a = dot_nt(x, w4[0, cols])
                 bb = dot_nt(x, w4[1, cols])
-                gate = dot_tn(high, spread[:, cols]) + dot_tn(low_part, spread[:, cols])
+                gate = dot_tn(gates_b, spread[:, cols])
                 u = dot_nt(gr, w4[2, cols]) * gate
                 square = a * a
                 th = jnp.tanh(GELU_C * (a + GELU_A * square * a))
@@ -1514,7 +1539,7 @@
     total = sm_s[1]
     for k in range(1, nz):
         sm_z(k).wait_recv()
-        total = total + smz[k]
+        total = total + smz[k - 1]
     small_out[...] = total
 
     advance(0)
@@ -1604,7 +1629,7 @@
     def shape(*dims, dtype=BF16):
         return jax.ShapeDtypeStruct(dims, dtype)
 
-    grid_sems = [DMA((4, 2, nz, ny)) for _ in range(4)]
+    grid_sems = [DMA((5, 2, nz, ny)) for _ in range(4)]
     small, routes_all, wqkv, wout, slices = pl.pallas_call(
         functools.partial(gather_kernel, ny, nz),
         out_shape=(
@@ -1621,10 +1646,10 @@
             pltpu.VMEM(wg.shape, BF16),
             pltpu.VMEM(wu.shape, BF16),
             pltpu.VMEM((2, 2, hidden, width), BF16),
-            DMA((2,)), DMA((4,)),
+            DMA((2,)), DMA((5,)),
         ]
         + grid_sems
-        + [DMA((4, 2, nz)), DMA((4, 2, nz)), DMA((2, nz))],
+        + [DMA((5, ny, 2, nz)), DMA((5, ny, 2, nz)), DMA((2, nz))],
         compiler_params=pltpu.CompilerParams(
             collective_id=3, has_side_effects=True, vmem_limit_bytes=60 * 2**20
         ),
@@ -1772,8 +1797,8 @@
             pltpu.VMEM((max(1, ny - 1), nz, padded, attn_width), BF16),
             pltpu.VMEM((max(1, nz - 1), padded, attn_width), BF16),
             pltpu.VMEM((2,) + small_shape, F32),
-            pltpu.VMEM((ny,) + small_shape, F32),
-            pltpu.VMEM((nz,) + small_shape, F32),
+            pltpu.VMEM((max(1, ny - 1),) + small_shape, F32),
+            pltpu.VMEM((max(1, nz - 1),) + small_shape, F32),
             DMA((2 * nz,)), DMA((2,)),
             DMA((4 * ny * micro + 4,)),
             DMA((ny + nz,)), DMA((ny + nz,)),
@@ -1784,7 +1809,7 @@
         ]
         + gather_sems(2 * micro),
         compiler_params=pltpu.CompilerParams(
-            collective_id=2, has_side_effects=True, vmem_limit_bytes=62 * 2**20
+            collective_id=2, has_side_effects=True, vmem_limit_bytes=63 * 2**20
         ),
         name="weight_gradients",
     )(routes_all, small, gsmall, zf, zb, slices, partner, wd, xab, obb, dqkv, dattn, xap, obp, dqp, dtp)

time: 450 us -> 446 us (level)
  no operation moved by 1% of the time
where the time goes in v6:
time: 446 us; the launch traced here: 441 us
  Pallas kernels  433 us (97%)
  local copies, waits for them, and re-layouts  7.17 us (2%)
    pallas_call x1, Pallas kernels, per_device(): pl.pallas_call(functools.partial(backward_kernel, ny, nz, sections), out_...  160 us
    pallas_call x1, Pallas kernels, per_device(): pl.pallas_call(functools.partial(tail_kernel, ny, nz, sections, span_z),...  117 us
    pallas_call x1, Pallas kernels, per_device(): pl.pallas_call(functools.partial(forward_kernel, ny, nz, sections), out_s...  76 us
    pallas_call x1, Pallas kernels, per_device(): pl.pallas_call(functools.partial(gather_kernel, ny, nz), out_shape=(shape...  73.6 us

profile of v6, /device:TPU:0, one launch (start us, length us, event | category | flops | bytes accessed | tf_op | source)
XLA Modules:
  0.0 441.3 jit_solution(17937994069524873646)
XLA Ops:
  0.6 0.8 copy.32
  1.4 0.8 copy.33
  2.2 0.8 copy.31
  3.0 0.1 concatenate.3
  3.1 0.6 convert_element_type.3.small_ref
  3.7 1.5 copy.34.segc_ref
  5.2 73.6 %gather_weights.1 = (bf16[32,1536]{1,0:T(8,128)(2,1)}, s32[4,4,2,4,128]{4,3,2,1,0:T(4,128)}, bf16[4,4,96,2048]{3,2,1,0:T(8,128)(2,1)}, bf16[4,4,96,1536]{3,2,1,0:T(8,128)(2,1)}, bf16[2,768,1536]{2,1,0:T(8,128)(2,1)}) custom-call(f32[96,128]{1,0:T(8,128)} %convert_element_type.3.small_ref, s32[2,4,128]{2,1,0:T(4,128)} %bitcast.47, bf16[96,2048]{1,0:T(8,128)(2,1)} %bitcast.41, ...), custom_call_target="tpu_custom_call" | custom-call | tf_op jit(solution)/shard_map/gather_weights/pallas_call | solution.py:1633
  78.8 76.0 %layers_forward.1 = (bf16[2,128,1536]{2,1,0:T(8,128)(2,1)}, bf16[2,128,1536]{2,1,0:T(8,128)(2,1)}, f32[2,128,1536]{2,1,0:T(8,128)}, bf16[2,128,2048]{2,1,0:T(8,1...) custom-call(bf16[2,128,1536]{2,1,0:T(8,128)(2,1)} %bitcast.40, ...), custom_call_target="tpu_custom_call" | custom-call | tf_op jit(solution)/shard_map/layers_forward/pallas_call | solution.py:1678
  154.8 160.0 %layers_backward.1 = (bf16[2,128,1536]{2,1,0:T(8,128)(2,1)}, bf16[2,2,2,128,1536]{4,3,2,1,0:T(8,128)(2,1)}, bf16[2,4,128,384]{3,2,1,0:T(8,128)(2,1)}, bf16[2,128...) custom-call(bf16[2,128,1536]{2,1,0:T(8,128)(2,1)} %bitcast.37, ...), custom_call_target="tpu_custom_call" | custom-call | tf_op jit(solution)/shard_map/layers_backward/pallas_call | solution.py:1717
  314.8 117.1 %weight_gradients.1 = (bf16[4,384,384]{2,1,0:T(8,128)(2,1)}, bf16[4,384,384]{2,1,0:T(8,128)(2,1)}, bf16[384,1536]{1,0:T(8,128)(2,1)}, bf16[96,3584]{1,0:T(8,128)...) custom-call(s32[16,2,4,128]{3,2,1,0:T(4,128)} %bitcast.44, ...), custom_call_target="tpu_custom_call", output_to_operand_aliasing={{5}: (4, {})} | custom-call | tf_op jit(solution)/shard_map/weight_gradients/pallas_call | solution.py:1764
  431.9 0.0 copy-start
  431.9 0.0 copy-start.1
  431.9 6.0 %finish_gradients.1 = (f32[1,2,384,768]{3,2,1,0:T(8,128)}, f32[1,2,384,768]{3,2,1,0:T(8,128)}, f32[1,2,192,1536]{3,2,1,0:T(8,128)}, f32[1,96,2048]{2,1,0:T(8,128...) custom-call(bf16[4,384,384]{2,1,0:T(8,128)(2,1)} %get-tuple-element.71.gate_in, ...), custom_call_target="tpu_custom_call" | custom-call | tf_op jit(solution)/shard_map/finish_gradients/pallas_call | solution.py:1818
  437.9 1.5 copy.38
  439.4 0.0 copy-done
  439.4 0.9 copy.42
  440.3 0.0 copy-done.1
  440.3 0.9 copy.43
  (2 shorter events, 0.0 us)
Async XLA Ops:
  431.9 7.5 %copy-start = (bf16[2,128,1536]{2,1,0:T(8,128)(2,1)S(1)}, bf16[2,128,1536]{2,1,0:T(8,128)(2,1)}, u32[]{:S(2)}) copy-start(bf16[2,128,1536]{2,1,0:T(8,128)(2,1)} %get-tuple-element.52) | copy-start | bytes 2359300
  431.9 8.4 %copy-start.1 = (bf16[2,128,1536]{2,1,0:T(8,128)(2,1)S(1)}, bf16[2,128,1536]{2,1,0:T(8,128)(2,1)}, u32[]{:S(2)}) copy-start(bf16[2,128,1536]{2,1,0:T(8,128)(2,1)} %get-tuple-element.58) | copy-start | bytes 2359300

commit v7 on v6

--- a/solution.py
+++ b/solution.py
@@ -51,8 +51,10 @@
     )
 
 
-def mask_bias(col, row):
+def mask_bias(row):
     tokens = row.shape[1]
+    row = jnp.broadcast_to(row.astype(F32), (tokens, tokens))
+    col = jnp.transpose(row)
     ti = lax.broadcasted_iota(jnp.int32, (tokens, tokens), 0)
     ui = lax.broadcasted_iota(jnp.int32, (tokens, tokens), 1)
     return jnp.where((col == row) & (ui <= ti), 0.0, NEGATIVE).astype(F32)
@@ -563,7 +565,7 @@
 
 def forward_kernel(
     ny, nz, sections,
-    x_ref, segc_ref, segr_ref, route_ref, small_ref, cos_ref, sin_ref,
+    x_ref, segr_ref, route_ref, small_ref, cos_ref, sin_ref,
     cot_h, slices_h, wqkv_h, wout_h, wg_h, wu_h, wd_h,
     out_ref, hin_ref, h1_ref, qkv_ref, obb_ref, xm_ref, gates_ref, zf_h, obp_h, share_h,
     wqkv, wout, wg, wu, wd, ob_s, hid, accl, accr, retl, retc, rety, sendl, sendc, sendy,
@@ -662,7 +664,7 @@
                 if head < turned:
                     part = part * cos + pltpu.roll(part, HEAD // 2, 1) * sin
                 qkv_ref[m, :, head * HEAD : (head + 1) * HEAD] = part.astype(BF16)
-        bias = mask_bias(segc_ref[m], segr_ref[m])
+        bias = mask_bias(segr_ref[m])
         bias6 = jnp.concatenate([bias] * GROUP, 0)
         qkv = qkv_ref.at[m]
         for kv in range(KEY_VALUE_HEADS):
@@ -817,7 +819,7 @@
 
 def backward_kernel(
     ny, nz, sections,
-    cot_ref, segc_ref, segr_ref, small_ref, cos_ref, sin_ref,
+    cot_ref, segr_ref, small_ref, cos_ref, sin_ref,
     hin_ref, h1_ref, qkv_ref, gates_ref,
     xm_h, wqkv_h, wout_h, wg_h, wu_h, wd_h,
     gin_ref, grows_ref, xab_ref, dqkv_ref, dattn_ref, gsmall_ref, zb_h, xap_h, dqp_h, dtp_h,
@@ -1049,7 +1051,7 @@
 
         for copy in partner(m)[:1]:
             copy.start()
-        bias = mask_bias(segc_ref[m], segr_ref[m])
+        bias = mask_bias(segr_ref[m])
         bias6 = jnp.concatenate([bias] * GROUP, 0)
         qkv = qkv_ref.at[m]
         turned = QUERY_HEADS + KEY_VALUE_HEADS
@@ -1261,6 +1263,9 @@
     def sm_z(k):
         return remote(sm_s.at[1], smz.at[k - 1], ss.at[ny + k], sr.at[ny + k], g.z_behind(k))
 
+    acc_g[...] = jnp.zeros_like(acc_g)
+    acc_u[...] = jnp.zeros_like(acc_u)
+    acc_d[...] = jnp.zeros_like(acc_d)
     for copy in acts:
         copy.wait()
     for copy in mine:
@@ -1348,9 +1353,6 @@
 
     for copy in mine:
         copy.wait()
-    acc_g[...] = jnp.zeros_like(acc_g)
-    acc_u[...] = jnp.zeros_like(acc_u)
-    acc_d[...] = jnp.zeros_like(acc_d)
     column = lax.rem(lax.broadcasted_iota(jnp.int32, (ROUTER_ROWS, wide), 1), both)
     expert = lax.broadcasted_iota(jnp.int32, (ROUTER_ROWS, wide), 0)
     owner = jnp.where(column < half, g.e, 2 * g.y + 1 - g.c)
@@ -1618,7 +1620,7 @@
     own_routes = jnp.transpose(routes[0, :, 0], (0, 2, 1))
     cos, sin = rotary_tables(tokens)
     segs = segments[:, 0]
-    segc, segr = segs[:, :, None], segs[:, None, :]
+    segr = segs[:, None, :]
     x = layer_input[:, 0]
     cot = cotangent[:, 0]
     wg, wu, wd = w_gate[0], w_up[0], w_down[0]
@@ -1689,7 +1691,7 @@
             shape(micro, ny, tokens, block),
             shape(3, hidden, width),
         ),
-        in_specs=[VMEM] * 7 + [ANY] * 7,
+        in_specs=[VMEM] * 6 + [ANY] * 7,
         out_specs=tuple([VMEM] * 7 + [ANY] * 3),
         scratch_shapes=weights
         + [
@@ -1710,7 +1712,7 @@
             collective_id=0, has_side_effects=True, vmem_limit_bytes=60 * 2**20
         ),
         name="layers_forward",
-    )(x, segc, segr, routes_all, small, cos, sin, cot, slices, wqkv, wout, wg, wu, wd)
+    )(x, segr, routes_all, small, cos, sin, cot, slices, wqkv, wout, wg, wu, wd)
 
     wide = width + 128
     every = (2, ny, 2, tokens, hidden)
@@ -1728,7 +1730,7 @@
             shape(micro, tokens, qkv_width),
             shape(micro, tokens, width),
         ),
-        in_specs=[VMEM] * 10 + [ANY] * 6,
+        in_specs=[VMEM] * 9 + [ANY] * 6,
         out_specs=tuple([VMEM] * 6 + [ANY] * 4),
         scratch_shapes=weights
         + [
@@ -1753,7 +1755,7 @@
             collective_id=1, has_side_effects=True, vmem_limit_bytes=62 * 2**20
         ),
         name="layers_backward",
-    )(cot, segc, segr, small, cos, sin, hin, h1, qkv, gates, xm, wqkv, wout, wg, wu, wd)
+    )(cot, segr, small, cos, sin, hin, h1, qkv, gates, xm, wqkv, wout, wg, wu, wd)
 
     span_z = max(1, min(nz, 512 // (ny * tokens)))
     rows = span_z * ny * tokens
@@ -1814,7 +1816,7 @@
         name="weight_gradients",
     )(routes_all, small, gsmall, zf, zb, slices, partner, wd, xab, obb, dqkv, dattn, xap, obp, dqp, dtp)
 
-    steps = 2
+    steps = 4
     finals = pl.pallas_call(
         functools.partial(finish_kernel, nz, total_experts),
         grid=(steps,),
@@ -1831,14 +1833,14 @@
         in_specs=[
             pl.BlockSpec((nz, part // steps, half), lambda i: (0, i, 0)),
             pl.BlockSpec((nz, part // steps, half), lambda i: (0, i, 0)),
-            pl.BlockSpec((slice_h, width), lambda i: (i, 0)),
+            pl.BlockSpec((half // steps, width), lambda i: (i, 0)),
             pl.BlockSpec((padded, attn_width), lambda i: (0, 0)),
             pl.BlockSpec(small_shape, lambda i: (0, 0)),
         ],
         out_specs=(
             pl.BlockSpec((1, 2, part // steps, hidden), lambda i: (0, 0, i, 0)),
             pl.BlockSpec((1, 2, part // steps, hidden), lambda i: (0, 0, i, 0)),
-            pl.BlockSpec((1, 1, slice_h, width), lambda i: (0, i, 0, 0)),
+            pl.BlockSpec((1, 1, half // steps, width), lambda i: (0, i // 2, i % 2, 0)),
             pl.BlockSpec((1, shard, qkv_width), lambda i: (0, 0, 0)),
             pl.BlockSpec((1, shard, width), lambda i: (0, 0, 0)),
             pl.BlockSpec((1, shard, total_experts), lambda i: (0, 0, 0)),

time: 446 us -> 446 us (level)
  no operation moved by 1% of the time
where the time goes in v7:
time: 446 us; the launch traced here: 441 us
  Pallas kernels  434 us (97%)
  local copies, waits for them, and re-layouts  5.69 us (1%)
    pallas_call x1, Pallas kernels, per_device(): pl.pallas_call(functools.partial(backward_kernel, ny, nz, sections), out_...  160 us
    pallas_call x1, Pallas kernels, per_device(): pl.pallas_call(functools.partial(tail_kernel, ny, nz, sections, span_z),...  117 us
    pallas_call x1, Pallas kernels, per_device(): pl.pallas_call(functools.partial(forward_kernel, ny, nz, sections), out_s...  75.9 us
    pallas_call x1, Pallas kernels, per_device(): pl.pallas_call(functools.partial(gather_kernel, ny, nz), out_shape=(shape...  73.6 us

profile of v7, /device:TPU:0, one launch (start us, length us, event | category | flops | bytes accessed | tf_op | source)
XLA Modules:
  0.0 441.3 jit_solution(6912991052965936373)
XLA Ops:
  0.6 0.8 copy.26
  1.4 0.8 copy.27
  2.2 0.8 copy.25
  3.0 0.1 concatenate.3
  3.1 0.6 convert_element_type.3.small_ref
  3.7 73.6 %gather_weights.1 = (bf16[32,1536]{1,0:T(8,128)(2,1)}, s32[4,4,2,4,128]{4,3,2,1,0:T(4,128)}, bf16[4,4,96,2048]{3,2,1,0:T(8,128)(2,1)}, bf16[4,4,96,1536]{3,2,1,0:T(8,128)(2,1)}, bf16[2,768,1536]{2,1,0:T(8,128)(2,1)}) custom-call(f32[96,128]{1,0:T(8,128)} %convert_element_type.3.small_ref, s32[2,4,128]{2,1,0:T(4,128)} %bitcast.45, bf16[96,2048]{1,0:T(8,128)(2,1)} %bitcast.40, ...), custom_call_target="tpu_custom_call" | custom-call | tf_op jit(solution)/shard_map/gather_weights/pallas_call | solution.py:1635
  77.3 75.9 %layers_forward.1 = (bf16[2,128,1536]{2,1,0:T(8,128)(2,1)}, bf16[2,128,1536]{2,1,0:T(8,128)(2,1)}, f32[2,128,1536]{2,1,0:T(8,128)}, bf16[2,128,2048]{2,1,0:T(8,1...) custom-call(bf16[2,128,1536]{2,1,0:T(8,128)(2,1)} %bitcast.39, ...), custom_call_target="tpu_custom_call" | custom-call | tf_op jit(solution)/shard_map/layers_forward/pallas_call | solution.py:1680
  153.3 159.9 %layers_backward.1 = (bf16[2,128,1536]{2,1,0:T(8,128)(2,1)}, bf16[2,2,2,128,1536]{4,3,2,1,0:T(8,128)(2,1)}, bf16[2,4,128,384]{3,2,1,0:T(8,128)(2,1)}, bf16[2,128...) custom-call(bf16[2,128,1536]{2,1,0:T(8,128)(2,1)} %bitcast.36, ...), custom_call_target="tpu_custom_call" | custom-call | tf_op jit(solution)/shard_map/layers_backward/pallas_call | solution.py:1719
  313.2 117.2 %weight_gradients.1 = (bf16[4,384,384]{2,1,0:T(8,128)(2,1)}, bf16[4,384,384]{2,1,0:T(8,128)(2,1)}, bf16[384,1536]{1,0:T(8,128)(2,1)}, bf16[96,3584]{1,0:T(8,128)...) custom-call(s32[16,2,4,128]{3,2,1,0:T(4,128)} %bitcast.43, ...), custom_call_target="tpu_custom_call", output_to_operand_aliasing={{5}: (4, {})} | custom-call | tf_op jit(solution)/shard_map/weight_gradients/pallas_call | solution.py:1766
  430.4 0.0 copy-start
  430.4 0.0 copy-start.1
  430.4 7.4 %finish_gradients.1 = (f32[1,2,384,768]{3,2,1,0:T(8,128)}, f32[1,2,384,768]{3,2,1,0:T(8,128)}, f32[1,2,192,1536]{3,2,1,0:T(8,128)}, f32[1,96,2048]{2,1,0:T(8,128...) custom-call(bf16[4,384,384]{2,1,0:T(8,128)(2,1)} %get-tuple-element.71.gate_in, ...), custom_call_target="tpu_custom_call" | custom-call | tf_op jit(solution)/shard_map/finish_gradients/pallas_call | solution.py:1820
  437.8 1.5 copy.30
  439.3 0.0 copy-done
  439.3 0.9 copy.34
  440.2 0.0 copy-done.1
  440.2 0.9 copy.35
  (2 shorter events, 0.0 us)
Async XLA Ops:
  430.4 8.9 %copy-start = (bf16[2,128,1536]{2,1,0:T(8,128)(2,1)S(1)}, bf16[2,128,1536]{2,1,0:T(8,128)(2,1)}, u32[]{:S(2)}) copy-start(bf16[2,128,1536]{2,1,0:T(8,128)(2,1)} %get-tuple-element.52) | copy-start | bytes 2359300
  430.4 9.8 %copy-start.1 = (bf16[2,128,1536]{2,1,0:T(8,128)(2,1)S(1)}, bf16[2,128,1536]{2,1,0:T(8,128)(2,1)}, u32[]{:S(2)}) copy-start(bf16[2,128,1536]{2,1,0:T(8,128)(2,1)} %get-tuple-element.58) | copy-start | bytes 2359300
